TPU v7x, 256 devices: a whole 4x4x8 slice. The times are simulated.
256 devices in a mesh: px: 16 (over y, x_hi, core), py: 16 (over z, x_lo).
Axes of the slice: x: 4 (x_hi: 2, x_lo: 2; x = x_hi * 2 + x_lo), y: 4, z: 8, core: 2. Of those that a mesh axis runs over, the one named last changes fastest.
Arguments:
- state: float32 [5, 256, 256, 192], P(None, 'px', 'py'), may hold values from -6 to 6
- memory: float32 [5, 256, 256, 192], P(None, 'px', 'py'), may hold values from -3 to 3
- level_steps: int32 [192], replicated, may hold values from 1 to 3
- building_height: int32 [256, 256], P('px', 'py'), may hold values from 0 to 24
Outputs:
- updated: float32 [5, 256, 256, 192], P(None, 'px', 'py')
- pressure: float32 [256, 256, 192], P('px', 'py')
All inputs are finite; a program needn't handle non-finite values.
Results may differ from a plain program's by a relative error of at most 0.0003.
Values sent between devices are 32-bit elements; how exact they have to be, the bound alone decides.
No kernel may reach another device: no remote copies, remote signals or barrier semaphores. Data moves between devices by JAX's collectives and lax.ppermute only.
A program may use at most 64 MiB of HBM per device.

v0:
```python
import jax
import jax.numpy as jnp
from jax import lax
from jax.sharding import PartitionSpec as P

RK_KEEP = -5.0 / 9.0
RK_STEP = 15.0 / 16.0
TIME_STEP = 0.1
DIFFUSION = 0.05
BUOYANCY = 0.3
HIGHEST = lax.Precision.HIGHEST


def with_halo(block, sides, width):
    for axis, dim in sides:
        count = lax.axis_size(axis)
        forward = [(i, i + 1) for i in range(count - 1)]
        forward.append((count - 1, 0))
        backward = [(target, source) for source, target in forward]
        low = lax.ppermute(
            lax.slice_in_dim(block, block.shape[dim] - width, None, axis=dim), axis, forward
        )
        high = lax.ppermute(lax.slice_in_dim(block, 0, width, axis=dim), axis, backward)
        block = jnp.concatenate([low, block, high], axis=dim)
    return block


def passed_along(block, axis, distance):
    devices = range(lax.axis_size(axis))
    route = [((i - distance) % len(devices), i) for i in devices]
    return lax.ppermute(block, axis, route)


def level_geometry(level_steps):
    thickness = level_steps.astype(jnp.float32)
    spacing = jnp.concatenate([0.5 * (thickness[:-1] + thickness[1:]), thickness[-1:]])
    return (thickness, spacing)


def below_level(values):
    return jnp.concatenate([jnp.zeros_like(values[..., :1]), values[..., :-1]], axis=-1)


def above_level(values):
    return jnp.concatenate([values[..., 1:], values[..., -1:]], axis=-1)


def column_terms(values, z_velocity, thickness, spacing):
    upper_values = above_level(values)
    flux_up = z_velocity * (values + upper_values) * 0.5
    slope_up = (upper_values - values) / spacing
    return (
        (flux_up - below_level(flux_up)) / thickness,
        (slope_up - below_level(slope_up)) / thickness,
    )


def column_operator(thickness, spacing):
    upward = 1.0 / (thickness * spacing)
    downward = jnp.concatenate(
        [jnp.zeros_like(thickness[:1]), 1.0 / (thickness[1:] * spacing[:-1])]
    )
    above_diag = jnp.concatenate([upward[:-1], jnp.zeros_like(thickness[:1])])
    return (downward, -(upward + downward), above_diag)


def eigenvalues(frequency, total):
    return 2.0 - 2.0 * jnp.cos(2.0 * jnp.pi / total * frequency.astype(jnp.float32))


def with_rims(tile_block):
    return with_halo(tile_block, (("px", 1), ("py", 2)), 1)


def from_px(face_plane, offset):
    return passed_along(face_plane, "px", offset)


def from_py(face_plane, offset):
    return passed_along(face_plane, "py", offset)


def tendency(extended, velocity, thickness, spacing):
    values = extended[:, 1:-1, 1:-1]
    east_cells = extended[:, 2:, 1:-1]
    west_cells = extended[:, :-2, 1:-1]
    north_cells = extended[:, 1:-1, 2:]
    south_cells = extended[:, 1:-1, :-2]
    x_velocity = velocity[0, 1:-1, 1:-1]
    x_west = velocity[0, :-2, 1:-1]
    y_velocity = velocity[1, 1:-1, 1:-1]
    y_south = velocity[1, 1:-1, :-2]
    z_velocity = velocity[2, 1:-1, 1:-1]
    advect = (x_velocity * (values + east_cells) - x_west * (west_cells + values)) * 0.5
    advect = advect + (y_velocity * (values + north_cells) - y_south * (south_cells + values)) * 0.5
    vertical, spread = column_terms(values, z_velocity, thickness, spacing)
    diffuse = east_cells + west_cells + north_cells + south_cells - 4.0 * values + spread
    return DIFFUSION * diffuse - advect - vertical


def advance(current, stored, extended, velocity, forcing, fluid_mask, thickness, spacing):
    change = tendency(extended, velocity, thickness, spacing) + forcing
    carried = RK_KEEP * stored + TIME_STEP * fluid_mask * change
    return current + RK_STEP * carried


def phase_angles(row_index, col_index, total):
    phases = row_index[:, None] * col_index[None, :] % total
    return 2.0 * jnp.pi / total * phases.astype(jnp.float32)


def shifted_down(values, stride, fill_value):
    edge_cells = jnp.full(values.shape[:-1] + (stride,), fill_value, values.dtype)
    return jnp.concatenate([edge_cells, values[..., :-stride]], axis=-1)


def shifted_up(values, stride, fill_value):
    edge_cells = jnp.full(values.shape[:-1] + (stride,), fill_value, values.dtype)
    return jnp.concatenate([values[..., stride:], edge_cells], axis=-1)


def cyclic_solve(below_diag, diagonal, above_diag, right_side):
    levels_total = diagonal.shape[-1]
    stride = 1
    while stride < levels_total:
        lower_factor = -below_diag / shifted_down(diagonal, stride, 1.0)
        upper_factor = -above_diag / shifted_up(diagonal, stride, 1.0)
        new_diagonal = (
            diagonal
            + lower_factor * shifted_down(above_diag, stride, 0.0)
            + upper_factor * shifted_up(below_diag, stride, 0.0)
        )
        right_side = (
            right_side
            + lower_factor * shifted_down(right_side, stride, 0.0)
            + upper_factor * shifted_up(right_side, stride, 0.0)
        )
        below_diag = lower_factor * shifted_down(below_diag, stride, 0.0)
        above_diag = upper_factor * shifted_up(above_diag, stride, 0.0)
        diagonal = new_diagonal
        stride = stride * 2
    return right_side / diagonal


def solve_pressure(diverge, thickness, spacing):
    count_x = lax.axis_size("px")
    count_y = lax.axis_size("py")
    tile_x, tile_y, levels_total = diverge.shape
    wide_x = tile_x * count_x
    wide_y = tile_y * count_y
    share_y = tile_y // count_x
    share_x = wide_x // (count_x * count_y)
    block_x = wide_x // count_x
    position_x = jnp.arange(wide_x, dtype=jnp.int32)
    position_y = jnp.arange(wide_y, dtype=jnp.int32)
    row_group = position_y // (count_y * share_y)
    col_group = position_y // share_y % count_y
    order_y = col_group * tile_y + row_group * share_y + position_y % share_y
    high_group = position_x // (count_x * share_x)
    low_group = position_x // share_x % count_x
    order_k = low_group * block_x + high_group * share_x + position_x % share_x
    below_diag, middle, above_diag = column_operator(thickness, spacing)
    x_lines = lax.all_to_all(diverge, "px", split_axis=1, concat_axis=0, tiled=True)
    components = 2
    angles_x = phase_angles(position_x, position_x, wide_x)
    forward_x = jnp.stack([jnp.cos(angles_x), -jnp.sin(angles_x)], axis=1).reshape(
        2 * wide_x, wide_x
    )
    angles_y = phase_angles(position_y, position_y, wide_y)
    cos_y, sin_y = (jnp.cos(angles_y), jnp.sin(angles_y))
    forward_y = jnp.stack([jnp.stack([cos_y, sin_y], 1), jnp.stack([-sin_y, cos_y], 1)], 1).reshape(
        2 * wide_y, 2 * wide_y
    )
    angles_back = phase_angles(order_y, position_y, wide_y)
    cos_back, sin_back = (jnp.cos(angles_back), jnp.sin(angles_back))
    inverse_y = jnp.stack(
        [jnp.stack([cos_back, -sin_back], -1), jnp.stack([sin_back, cos_back], -1)], 1
    ).reshape(2 * wide_y, 2 * wide_y)
    angles_out = phase_angles(position_x, order_k, wide_x)
    inverse_x = jnp.stack([jnp.cos(angles_out), -jnp.sin(angles_out)], axis=1).reshape(
        wide_x, 2 * wide_x
    )
    inverse_x = inverse_x * (1.0 / (wide_x * wide_y))
    frequency_x, frequency_y = (position_x, position_y)
    spectrum_x = jnp.dot(
        forward_x, x_lines.reshape(wide_x, share_y * levels_total), precision=HIGHEST
    )
    spectrum_x = spectrum_x.reshape(wide_x, components, share_y, levels_total)
    y_lines = lax.all_to_all(
        lax.all_to_all(spectrum_x, "px", split_axis=0, concat_axis=2, tiled=True),
        "py",
        split_axis=0,
        concat_axis=2,
        tiled=True,
    )
    gathered = jnp.transpose(y_lines, (1, 2, 0, 3)).reshape(
        components * wide_y, share_x * levels_total
    )
    spectra = jnp.dot(forward_y, gathered, precision=HIGHEST).reshape(
        wide_y, components, share_x, levels_total
    )
    start_x = lax.axis_index("px") * block_x + lax.axis_index("py") * share_x
    local_x = lax.dynamic_slice_in_dim(frequency_x, start_x, share_x)
    eigen_shift = eigenvalues(frequency_y, wide_y)[:, None] + eigenvalues(local_x, wide_x)[None, :]
    diagonal = middle[None, None, None, :] - eigen_shift[:, None, :, None]
    solved = cyclic_solve(
        jnp.broadcast_to(below_diag, diagonal.shape),
        diagonal,
        jnp.broadcast_to(above_diag, diagonal.shape),
        spectra,
    )
    back_lines = jnp.dot(
        inverse_y, solved.reshape(wide_y * components, share_x * levels_total), precision=HIGHEST
    )
    back_lines = back_lines.reshape(wide_y, components, share_x, levels_total)
    x_spectra = lax.all_to_all(
        lax.all_to_all(back_lines, "px", split_axis=0, concat_axis=2, tiled=True),
        "py",
        split_axis=0,
        concat_axis=2,
        tiled=True,
    )
    gathered_back = jnp.transpose(x_spectra, (1, 2, 0, 3)).reshape(
        components * wide_x, share_y * levels_total
    )
    pressure_lines = jnp.dot(inverse_x, gathered_back, precision=HIGHEST).reshape(
        wide_x, share_y, levels_total
    )
    return lax.all_to_all(pressure_lines, "px", split_axis=0, concat_axis=1, tiled=True)


def project(provisional, fluid_mask, thickness, spacing):
    x_velocity, y_velocity, z_velocity = (provisional[0], provisional[1], provisional[2])
    west_plane = from_px(x_velocity[-1:], 1)
    south_plane = from_py(y_velocity[:, -1:], 1)
    x_before = jnp.concatenate([west_plane, x_velocity[:-1]], axis=0)
    y_before = jnp.concatenate([south_plane, y_velocity[:, :-1]], axis=1)
    diverge = (
        x_velocity
        - x_before
        + (y_velocity - y_before)
        + (z_velocity - below_level(z_velocity)) / thickness
    )
    pressure = solve_pressure(diverge, thickness, spacing)
    east_plane = from_px(pressure[:1], -1)
    north_plane = from_py(pressure[:, :1], -1)
    east_pressure = jnp.concatenate([pressure[1:], east_plane], axis=0)
    north_pressure = jnp.concatenate([pressure[:, 1:], north_plane], axis=1)
    upper_pressure = jnp.concatenate(
        [pressure[..., 1:], jnp.zeros_like(pressure[..., :1])], axis=-1
    )
    corrected_x = fluid_mask * (x_velocity - (east_pressure - pressure))
    corrected_y = fluid_mask * (y_velocity - (north_pressure - pressure))
    corrected_z = fluid_mask * (z_velocity - (upper_pressure - pressure) / spacing)
    return (jnp.stack([corrected_x, corrected_y, corrected_z]), pressure)


def per_device(state, memory, level_steps, building_height):
    thickness, spacing = level_geometry(level_steps)
    levels = jnp.arange(state.shape[3], dtype=jnp.int32)
    fluid_mask = jnp.where(levels[None, None, :] >= building_height[:, :, None], 1.0, 0.0).astype(
        jnp.float32
    )
    forcing = jnp.zeros_like(state).at[2].set(BUOYANCY * state[3])
    extended = with_rims(state)
    provisional = advance(
        state, memory, extended, extended[:3], forcing, fluid_mask, thickness, spacing
    )
    corrected, pressure = project(provisional[:3], fluid_mask, thickness, spacing)
    scalars = provisional[3:]
    return (jnp.concatenate([corrected, scalars]), pressure)


def solution(mesh):
    return jax.shard_map(
        per_device,
        mesh=mesh,
        in_specs=(P(None, "px", "py", None), P(None, "px", "py", None), P(), P("px", "py")),
        out_specs=(P(None, "px", "py", None), P("px", "py", None)),
        check_vma=False,
    )
```

profile of v0, /device:TPU:1, one launch (start us, length us, event | category | flops | bytes accessed | tf_op | source)
XLA Modules:
  0.0 192.5 jit_solution(7139016491490544730)
XLA Ops:
  2.3 3.2 %collective-permute-start = (f32[5,1,16,192]{3,1,2,0:T(1,128)}, f32[5,1,16,192]{3,1,2,0:T(1,128)}, u32[]{:S(2)}, u32[]{:S(2)}) collective-permute-start(f32[5,1,16,192]{3,1,2,0:T(1,128)} %copy.98), channel_id=1, source_target_pairs={{16,0},{32,16},{48,32},{64,48},{80,64},{96,80},{112,96},{128,112},... | collective-permute-start | bytes 184328 | tf_op jit(solution)/shard_map/ppermute | solution.py:23
  7.1 2.1 %copy.116 = f32[5,16,16,192]{3,1,2,0:T(8,128)S(1)} copy(f32[5,16,16,192]{3,2,1,0:T(8,128)} %param.6) | data formatting | bytes 1966080 | tf_op args[0]
  33.9 5.3 %collective-permute-start.2 = (f32[5,18,1,192]{3,1,2,0:T(8,128)S(1)}, f32[5,18,1,192]{3,1,2,0:T(8,128)S(1)}, u32[]{:S(2)}, u32[]{:S(2)}) collective-permute-start(f32[5,18,1,192]{3,1,2,0:T(8,128)S(1)} %get-tuple-element.57), channel_id=1, source_target_pairs={{1,0},{2,1},{3,2},{4,3},{5,4},{6,5},{7,6},{8,7},{9,8},{10,9},{11,1... | collective-permute-start | bytes 207368 | tf_op jit(solution)/shard_map/ppermute | solution.py:23
  42.0 3.4 %fusion.8 = f32[5,16,16,192]{3,1,2,0:T(8,128)S(1)} fusion(f32[5,16,16,192]{3,1,2,0:T(8,128)S(1)} %copy.116, f32[5,1,16,192]{3,1,2,0:T(1,128)} %collective-permute-done, f32[5,16,16,192]{3,1,2,0:T(8,128)S(1)} %get-tuple-element.54, f32[5,16,16,191]{3,1,2,0:T(8,128)S(1)} %bitcast.147, f32[5,18,17,192]{3,1,2,0:T(8,128)S(1)} %maximum_maximum_fusion, ...), kind=kLoop, calls=%fused_computation.15 | loop fusion | flops 7372800 | bytes 7850240 | tf_op jit(solution)/shard_map/sub | solution.py:98
  45.5 2.1 %fusion.16 = f32[5,16,16,192]{3,1,2,0:T(8,128)S(1)} fusion(f32[5,16,16,192]{3,2,1,0:T(8,128)S(1)} %copy-done.12, f32[5,16,16,192]{3,1,2,0:T(8,128)S(1)} %fusion.36, f32[16,16,192]{2,0,1:T(8,128)S(1)} %copy-done.16, f32[5,16,16,192]{3,2,1,0:T(8,128)S(1)} %copy-done), kind=kLoop, calls=%fused_computation.26 | loop fusion | flops 1228800 | bytes 4128768 | tf_op jit(solution)/shard_map/add | solution.py:104
  50.8 3.2 %collective-permute-done.5 = f32[16,1,192]{2,0,1:T(8,128)S(1)} collective-permute-done((f32[16,1,192]{2,0,1:T(8,128)S(1)}, f32[16,1,192]{2,0,1:T(8,128)S(1)}, u32[]{:S(2)}, u32[]{:S(2)}) %collective-permute-start.5) | collective-permute-done | bytes 12320 | tf_op jit(solution)/shard_map/ppermute | solution.py:31
  54.8 8.7 %all-to-all-start = ((f32[16,16,192]{2,0,1:T(8,128)}), f32[16,16,192]{2,0,1:T(8,128)S(1)}, u32[]{:S(2)}, u32[]{:S(2)}) async-start(f32[16,16,192]{2,0,1:T(8,128)} %fusion.39), calls=%async_computation | async-start | bytes 524288 | tf_op jit(solution)/shard_map/all_to_all | solution.py:163
  64.2 8.0 %all-to-all-done = f32[16,16,192]{2,0,1:T(8,128)S(1)} async-done(((f32[16,16,192]{2,0,1:T(8,128)}), f32[16,16,192]{2,0,1:T(8,128)S(1)}, u32[]{:S(2)}, u32[]{:S(2)}) %all-to-all-start) | async-done | bytes 196640 | tf_op jit(solution)/shard_map/all_to_all | solution.py:163
  73.9 5.0 %all-to-all-start.1 = ((f32[256,2,1,192]{3,1,2,0:T(2,128)}), f32[256,2,1,192]{3,1,2,0:T(2,128)}, u32[]{:S(2)}, u32[]{:S(2)}) async-start(f32[256,2,1,192]{3,1,2,0:T(2,128)} %copy.127), calls=%async_computation.1 | async-start | bytes 1048576 | tf_op jit(solution)/shard_map/all_to_all | solution.py:190
  79.0 1.9 %fusion.57 = (f32[256,256,1]{1,0,2:T(8,128)S(1)}, f32[256,256,1]{1,0,2:T(8,128)}, f32[256,256,1]{1,0,2:T(8,128)}) fusion(s32[256]{0:T(256)S(1)} %fusion.63), kind=kLoop, calls=%fused_computation.157 | loop fusion | flops 983040 | bytes 787456 | tf_op jit(solution)/shard_map/neg | solution.py:177
  80.9 9.4 %all-to-all-done.1 = f32[256,2,1,192]{3,1,2,0:T(2,128)} async-done(((f32[256,2,1,192]{3,1,2,0:T(2,128)}), f32[256,2,1,192]{3,1,2,0:T(2,128)}, u32[]{:S(2)}, u32[]{:S(2)}) %all-to-all-start.1) | async-done | bytes 393248 | tf_op jit(solution)/shard_map/all_to_all | solution.py:190
  92.5 5.8 %all-to-all-start.2 = ((f32[16,2,16,192]{3,2,1,0:T(8,128)}), f32[16,2,16,192]{3,2,1,0:T(8,128)}, u32[]{:S(2)}, u32[]{:S(2)}) async-start(f32[16,2,16,192]{3,2,1,0:T(8,128)} %copy.129), calls=%async_computation.2 | async-start | bytes 1048576 | tf_op jit(solution)/shard_map/all_to_all | solution.py:189
  98.4 2.0 %pad_maximum_fusion.9 = (f32[256,256,2]{1,0,2:T(8,128)S(1)}, f32[256,256,2]{1,0,2:T(8,128)}) fusion(f32[256,256,1]{1,0,2:T(8,128)S(1)} %get-tuple-element.139, f32[256,256,1]{1,0,2:T(8,128)} %get-tuple-element.141, f32[256,256,1]{1,0,2:T(8,128)} %get-tuple-element.140), kind=kLoop, calls=%fused_computation.42 | loop fusion | flops 262144 | bytes 1835008 | tf_op jit(solution)/shard_map/stack | solution.py:177
  100.4 2.1 %copy.119 = f32[256,256,2]{0,2,1:T(2,128)} copy(f32[256,256,2]{1,0,2:T(8,128)} %get-tuple-element.87) | data formatting | bytes 1048576 | tf_op jit(solution)/shard_map/stack | solution.py:177
  102.4 2.2 %stack.57 = f32[256,1,512]{0,2,1:T(8,128)} reshape(f32[256,256,2]{0,2,1:T(2,128)} %copy.119) | data formatting | bytes 1048576 | tf_op jit(solution)/shard_map/stack | solution.py:176
  104.6 2.1 %copy.121 = f32[256,1,512]{2,0,1:T(8,128)} copy(f32[256,1,512]{0,2,1:T(8,128)} %stack.57) | data formatting | bytes 1048576 | tf_op jit(solution)/shard_map/stack | solution.py:176
  124.9 2.0 %convolution_bitcast_fusion = f32[256,2,1,192]{0,3,1,2:T(8,128)} fusion(f32[256,1,512]{2,0,1:T(8,128)S(1)} %copy-done.3, f32[256,1,512]{2,0,1:T(8,128)S(1)} %copy-done.4, f32[512,192]{1,0:T(8,128)S(1)} %reshape.627), kind=kOutput, calls=%fused_computation.29 | convolution fusion | flops 604241920 | bytes 1835008 | tf_op jit(solution)/shard_map/dot_general | solution.py:212
  128.1 16.6 %all_to_all.102 = f32[256,2,1,192]{3,1,2,0:T(2,128)S(1)} all-to-all(f32[256,2,1,192]{3,1,2,0:T(2,128)S(1)} %copy.134), channel_id=1, replica_groups=mesh['px'=16,'py'=16] {'px'}, dimensions={0} | all-to-all | bytes 786432 | tf_op jit(solution)/shard_map/all_to_all | solution.py:217
  145.8 6.4 %all-to-all-start.4 = ((f32[16,2,16,192]{3,2,1,0:T(8,128)}), f32[16,2,16,192]{3,2,1,0:T(8,128)S(1)}, u32[]{:S(2)}, u32[]{:S(2)}) async-start(f32[16,2,16,192]{3,2,1,0:T(8,128)} %copy.136), calls=%async_computation.4 | async-start | bytes 1048576 | tf_op jit(solution)/shard_map/all_to_all | solution.py:216
  153.6 14.1 %all-to-all-done.4 = f32[16,2,16,192]{3,2,1,0:T(8,128)S(1)} async-done(((f32[16,2,16,192]{3,2,1,0:T(8,128)}), f32[16,2,16,192]{3,2,1,0:T(8,128)S(1)}, u32[]{:S(2)}, u32[]{:S(2)}) %all-to-all-start.4) | async-done | bytes 393248 | tf_op jit(solution)/shard_map/all_to_all | solution.py:216
  169.6 7.1 %all-to-all-start.5 = ((f32[256,1,192]{2,1,0:T(1,128)}), f32[256,1,192]{2,1,0:T(1,128)S(1)}, u32[]{:S(2)}, u32[]{:S(2)}) async-start(f32[256,1,192]{2,1,0:T(1,128)} %copy.138), calls=%async_computation.5 | async-start | bytes 524288 | tf_op jit(solution)/shard_map/all_to_all | solution.py:229
  176.7 8.6 %all-to-all-done.5 = f32[256,1,192]{2,1,0:T(1,128)S(1)} async-done(((f32[256,1,192]{2,1,0:T(1,128)}), f32[256,1,192]{2,1,0:T(1,128)S(1)}, u32[]{:S(2)}, u32[]{:S(2)}) %all-to-all-start.5) | async-done | bytes 196640 | tf_op jit(solution)/shard_map/all_to_all | solution.py:229
  187.7 2.7 %collective-permute-done.6 = f32[1,16,192]{2,0,1:T(1,128)S(1)} collective-permute-done((f32[1,16,192]{2,0,1:T(1,128)S(1)}, f32[1,16,192]{2,0,1:T(1,128)S(1)}, u32[]{:S(2)}, u32[]{:S(2)}) %collective-permute-start.6) | collective-permute-done | bytes 12320 | tf_op jit(solution)/shard_map/ppermute | solution.py:31
  190.7 1.8 copy.140
  (221 shorter events, 65.1 us)
Async XLA Ops:
  2.3 27.9 %collective-permute-start = (f32[5,1,16,192]{3,1,2,0:T(1,128)}, f32[5,1,16,192]{3,1,2,0:T(1,128)}, u32[]{:S(2)}, u32[]{:S(2)}) collective-permute-start(f32[5,1,16,192]{3,1,2,0:T(1,128)} %copy.98), channel_id=1, source_target_pairs={{16,0},{32,16},{48,32},{64,48},{80,64},{96,80},{112,96},{128,112},... | collective-permute-start | bytes 184328 | tf_op jit(solution)/shard_map/ppermute | solution.py:23
  6.2 24.0 %collective-permute-start.1 = (f32[5,1,16,192]{3,1,2,0:T(1,128)}, f32[5,1,16,192]{3,1,2,0:T(1,128)}, u32[]{:S(2)}, u32[]{:S(2)}) collective-permute-start(f32[5,1,16,192]{3,1,2,0:T(1,128)} %copy.100), channel_id=1, source_target_pairs={{0,16},{16,32},{32,48},{48,64},{64,80},{80,96},{96,112},{112,128},... | collective-permute-start | bytes 184328 | tf_op jit(solution)/shard_map/ppermute | solution.py:20
  24.0 2.9 %copy-start.6 = (f32[256,1,1,128]{0,3,2,1:T(8,128)}, f32[256,1,1,128]{0,3,2,1:T(8,128)S(1)}, u32[]{:S(2)}) copy-start(f32[256,1,1,128]{0,3,2,1:T(8,128)S(1)} %get-tuple-element.99) | copy-start | bytes 393220
  24.0 2.9 %copy-start.8 = (f32[256,1,1,128]{0,3,2,1:T(8,128)}, f32[256,1,1,128]{0,3,2,1:T(8,128)S(1)}, u32[]{:S(2)}) copy-start(f32[256,1,1,128]{0,3,2,1:T(8,128)S(1)} %get-tuple-element.98) | copy-start | bytes 393220
  27.6 2.4 %copy-start.14 = (f32[16,16,192]{2,1,0:T(8,128)S(1)}, f32[16,16,192]{2,1,0:T(8,128)}, u32[]{:S(2)}) copy-start(f32[16,16,192]{2,1,0:T(8,128)} %get-tuple-element.63) | copy-start | bytes 589828
  31.0 8.8 %collective-permute-start.3 = (f32[5,18,1,192]{3,1,2,0:T(8,128)S(1)}, f32[5,18,1,192]{3,1,2,0:T(8,128)S(1)}, u32[]{:S(2)}, u32[]{:S(2)}) collective-permute-start(f32[5,18,1,192]{3,1,2,0:T(8,128)S(1)} %get-tuple-element.58), channel_id=1, source_target_pairs={{0,1},{1,2},{2,3},{3,4},{4,5},{5,6},{6,7},{7,8},{8,9},{9,10},{10,1... | collective-permute-start | bytes 207368 | tf_op jit(solution)/shard_map/ppermute | solution.py:20
  33.9 8.1 %collective-permute-start.2 = (f32[5,18,1,192]{3,1,2,0:T(8,128)S(1)}, f32[5,18,1,192]{3,1,2,0:T(8,128)S(1)}, u32[]{:S(2)}, u32[]{:S(2)}) collective-permute-start(f32[5,18,1,192]{3,1,2,0:T(8,128)S(1)} %get-tuple-element.57), channel_id=1, source_target_pairs={{1,0},{2,1},{3,2},{4,3},{5,4},{6,5},{7,6},{8,7},{9,8},{10,9},{11,1... | collective-permute-start | bytes 207368 | tf_op jit(solution)/shard_map/ppermute | solution.py:23
  42.0 3.5 %copy-start.12 = (f32[5,16,16,192]{3,2,1,0:T(8,128)S(1)}, f32[5,16,16,192]{3,2,1,0:T(8,128)}, u32[]{:S(2)}) copy-start(f32[5,16,16,192]{3,2,1,0:T(8,128)} %param.7) | copy-start | bytes 2949124
  42.0 3.5 %copy-start.16 = (f32[16,16,192]{2,0,1:T(8,128)S(1)}, f32[16,16,192]{2,0,1:T(8,128)}, u32[]{:S(2)}) copy-start(f32[16,16,192]{2,0,1:T(8,128)} %select_multiply_fusion.1) | copy-start | bytes 589828
  47.7 3.1 %collective-permute-start.4 = (f32[1,16,192]{2,0,1:T(1,128)S(1)}, f32[1,16,192]{2,0,1:T(1,128)S(1)}, u32[]{:S(2)}, u32[]{:S(2)}) collective-permute-start(f32[1,16,192]{2,0,1:T(1,128)S(1)} %slice_bitcast_fusion.9), channel_id=1, source_target_pairs={{240,0},{0,16},{16,32},{32,48},{48,64},{64,80},{80,96},{96,112},{1... | collective-permute-start | bytes 36872 | tf_op jit(solution)/shard_map/ppermute | solution.py:31
  49.3 4.7 %collective-permute-start.5 = (f32[16,1,192]{2,0,1:T(8,128)S(1)}, f32[16,1,192]{2,0,1:T(8,128)S(1)}, u32[]{:S(2)}, u32[]{:S(2)}) collective-permute-start(f32[16,1,192]{2,0,1:T(8,128)S(1)} %slice.466), channel_id=1, source_target_pairs={{15,0},{0,1},{1,2},{2,3},{3,4},{4,5},{5,6},{6,7},{7,8},{8,9},{9,10... | collective-permute-start | bytes 36872 | tf_op jit(solution)/shard_map/ppermute | solution.py:31
  49.3 14.2 %copy-start.10 = (f32[256,1,1,192]{0,3,2,1:T(8,128)S(1)}, f32[256,1,1,192]{0,3,2,1:T(8,128)}, u32[]{:S(2)}) copy-start(f32[256,1,1,192]{0,3,2,1:T(8,128)} %multiply_add_fusion.7) | copy-start | bytes 589828
  54.8 17.4 %all-to-all-start = ((f32[16,16,192]{2,0,1:T(8,128)}), f32[16,16,192]{2,0,1:T(8,128)S(1)}, u32[]{:S(2)}, u32[]{:S(2)}) async-start(f32[16,16,192]{2,0,1:T(8,128)} %fusion.39), calls=%async_computation | async-start | bytes 524288 | tf_op jit(solution)/shard_map/all_to_all | solution.py:163
  72.2 6.7 %copy-start.13 = (f32[256,1,256]{2,0,1:T(8,128)S(1)}, f32[256,1,256]{2,0,1:T(8,128)}, u32[]{:S(2)}) copy-start(f32[256,1,256]{2,0,1:T(8,128)} %fusion.53) | copy-start | bytes 786436
  73.9 16.4 %all-to-all-start.1 = ((f32[256,2,1,192]{3,1,2,0:T(2,128)}), f32[256,2,1,192]{3,1,2,0:T(2,128)}, u32[]{:S(2)}, u32[]{:S(2)}) async-start(f32[256,2,1,192]{3,1,2,0:T(2,128)} %copy.127), calls=%async_computation.1 | async-start | bytes 1048576 | tf_op jit(solution)/shard_map/all_to_all | solution.py:190
  92.5 22.2 %all-to-all-start.2 = ((f32[16,2,16,192]{3,2,1,0:T(8,128)}), f32[16,2,16,192]{3,2,1,0:T(8,128)}, u32[]{:S(2)}, u32[]{:S(2)}) async-start(f32[16,2,16,192]{3,2,1,0:T(8,128)} %copy.129), calls=%async_computation.2 | async-start | bytes 1048576 | tf_op jit(solution)/shard_map/all_to_all | solution.py:189
  111.5 2.4 %copy-start.7 = (f32[256,1,1,128]{0,3,2,1:T(8,128)S(1)}, f32[256,1,1,128]{0,3,2,1:T(8,128)}, u32[]{:S(2)}) copy-start(f32[256,1,1,128]{0,3,2,1:T(8,128)} %copy-done.6) | copy-start | bytes 393220
  111.7 2.9 %copy-start.11 = (f32[256,1,1,192]{0,3,2,1:T(8,128)S(1)}, f32[256,1,1,192]{0,3,2,1:T(8,128)}, u32[]{:S(2)}) copy-start(f32[256,1,1,192]{0,3,2,1:T(8,128)} %multiply_add_fusion.7) | copy-start | bytes 589828
  111.7 2.9 %copy-start.34 = (f32[256,1,1,64]{0,3,2,1:T(8,128)S(1)}, f32[256,1,1,64]{0,3,2,1:T(8,128)}, u32[]{:S(2)}) copy-start(f32[256,1,1,64]{0,3,2,1:T(8,128)} %get-tuple-element.92) | copy-start | bytes 196612
  111.7 2.9 %copy-start.35 = (f32[256,1,1,64]{0,3,2,1:T(8,128)S(1)}, f32[256,1,1,64]{0,3,2,1:T(8,128)}, u32[]{:S(2)}) copy-start(f32[256,1,1,64]{0,3,2,1:T(8,128)} %get-tuple-element.93) | copy-start | bytes 196612
  145.8 21.9 %all-to-all-start.4 = ((f32[16,2,16,192]{3,2,1,0:T(8,128)}), f32[16,2,16,192]{3,2,1,0:T(8,128)S(1)}, u32[]{:S(2)}, u32[]{:S(2)}) async-start(f32[16,2,16,192]{3,2,1,0:T(8,128)} %copy.136), calls=%async_computation.4 | async-start | bytes 1048576 | tf_op jit(solution)/shard_map/all_to_all | solution.py:216
  169.6 15.8 %all-to-all-start.5 = ((f32[256,1,192]{2,1,0:T(1,128)}), f32[256,1,192]{2,1,0:T(1,128)S(1)}, u32[]{:S(2)}, u32[]{:S(2)}) async-start(f32[256,1,192]{2,1,0:T(1,128)} %copy.138), calls=%async_computation.5 | async-start | bytes 524288 | tf_op jit(solution)/shard_map/all_to_all | solution.py:229
  185.7 4.7 %collective-permute-start.6 = (f32[1,16,192]{2,0,1:T(1,128)S(1)}, f32[1,16,192]{2,0,1:T(1,128)S(1)}, u32[]{:S(2)}, u32[]{:S(2)}) collective-permute-start(f32[1,16,192]{2,0,1:T(1,128)S(1)} %slice_bitcast_fusion.8), channel_id=1, source_target_pairs={{16,0},{32,16},{48,32},{64,48},{80,64},{96,80},{112,96},{128,112},... | collective-permute-start | bytes 36872 | tf_op jit(solution)/shard_map/ppermute | solution.py:31
  186.8 3.7 %collective-permute-start.7 = (f32[16,1,192]{2,0,1:T(8,128)S(1)}, f32[16,1,192]{2,0,1:T(8,128)S(1)}, u32[]{:S(2)}, u32[]{:S(2)}) collective-permute-start(f32[16,1,192]{2,0,1:T(8,128)S(1)} %slice.531), channel_id=1, source_target_pairs={{1,0},{2,1},{3,2},{4,3},{5,4},{6,5},{7,6},{8,7},{9,8},{10,9},{11,1... | collective-permute-start | bytes 36872 | tf_op jit(solution)/shard_map/ppermute | solution.py:31
  (28 other events, 37.5 us)
where the time goes:
time: 194 us; the launch traced here: 193 us
  waiting for transfers between devices  48.2 us (25%)
  starting transfers between devices  46.3 us (24%)
  local copies, waits for them, and re-layouts  40.9 us (21%)
  other arithmetic  33.9 us (17%)
  blocking collectives  16.6 us (9%)
  matrix products  4.96 us (3%)
    all_to_all x1, blocking collectives, solve_pressure(): lax.all_to_all(back_lines, 'px', split_axis=0, concat_axis=2, tiled=True)  16.6 us
    all_to_all x1, waiting for transfers between devices, solve_pressure(): lax.all_to_all(lax.all_to_all(back_lines, 'px', split_axis=0, concat_axis...  14.1 us
    unnamed x83, local copies, waits for them, and re-layouts  11.1 us
    all_to_all x1, waiting for transfers between devices, solve_pressure(): lax.all_to_all(spectrum_x, 'px', split_axis=0, concat_axis=2, tiled=True)  9.44 us
    all_to_all x1, starting transfers between devices, solve_pressure(): lax.all_to_all(diverge, 'px', split_axis=1, concat_axis=0, tiled=True)  8.7 us
    all_to_all x1, waiting for transfers between devices, solve_pressure(): lax.all_to_all(pressure_lines, 'px', split_axis=0, concat_axis=1, tiled=T...  8.64 us
    ppermute x2, starting transfers between devices, with_halo(): lax.ppermute(lax.slice_in_dim(block, 0, width, axis=dim), axis, backward)  8.55 us
    all_to_all x1, waiting for transfers between devices, solve_pressure(): lax.all_to_all(diverge, 'px', split_axis=1, concat_axis=0, tiled=True)  8.01 us
  transfers between devices with their start and end apart: 13, of which 8 were waited for; matrix products, arithmetic and copies ran while one was open for 25% of the time, Pallas kernels for 0%

commit v1 on v0

v1 whole, which is shorter than its diff:
```python
import jax
import jax.numpy as jnp
import numpy as np
from jax import lax
from jax.experimental import pallas as pl
from jax.experimental.pallas import tpu as pltpu
from jax.sharding import PartitionSpec as P

RK_KEEP = -5.0 / 9.0
RK_STEP = 15.0 / 16.0
TIME_STEP = 0.1
DIFFUSION = 0.05
BUOYANCY = 0.3
HIGHEST = lax.Precision.HIGHEST

TILE = 16
LINE = 256
LEVELS = 192
WIDE = 256
CHUNK = LEVELS // TILE
FIRST = 192
SECOND = 208
STRIDES = (1, 2, 4, 8, 16, 32, 64, 128)


def tables():
    n = np.arange(LINE)
    angles = 2.0 * np.pi / LINE * (np.outer(n, n) % LINE)
    basis = (np.cos(angles) + np.sin(angles)) / np.sqrt(LINE)
    following = (n // TILE + 1) * TILE % LINE
    after = basis[following]
    chunk_lane = np.arange(WIDE)
    unpack = np.zeros((2, 128, WIDE))
    for which, lane in enumerate((FIRST, SECOND)):
        for z in range(LEVELS):
            unpack[which, lane - 128 + z % CHUNK, z] = 1.0
    pack = np.swapaxes(unpack, 1, 2)
    as32 = lambda a: np.ascontiguousarray(a, dtype=np.float32)
    return as32(basis), as32(after), as32(unpack), as32(pack)


BASIS, AFTER, UNPACK, PACK = tables()


def product(a, b, contract=((1,), (0,))):
    return lax.dot_general(
        a, b, (contract, ((), ())), precision=HIGHEST, preferred_element_type=jnp.float32
    )


def chunk_mask(shape, owner):
    lane = lax.broadcasted_iota(jnp.int32, shape, 1)
    row = lax.broadcasted_iota(jnp.int32, shape, 0)
    start = (row % TILE if owner == "low" else row // TILE) * CHUNK
    return (lane >= start) & (lane < start + CHUNK)


def lanes_up(a):
    return jnp.concatenate([a[:, 1:], a[:, -1:]], axis=1)


def lanes_down(a):
    return jnp.concatenate([jnp.zeros_like(a[:, :1]), a[:, :-1]], axis=1)


def edges_kernel(state, west, east, south, north):
    west[...] = state[:, 0]
    east[...] = state[:, TILE - 1]
    south[...] = state[:, :, 0]
    north[...] = state[:, :, TILE - 1]


def advance_fields(fields, state, memory, west, east, south, north, inv_rows, height, store):
    inv_thick = inv_rows[0:1, :]
    inv_space = inv_rows[1:2, :]
    level = lax.broadcasted_iota(jnp.int32, (TILE, LEVELS), 1)

    def x_faces(s, e, u):
        return e * (DIFFUSION - 0.5 * u) - s * (DIFFUSION + 0.5 * u)

    before = {f: x_faces(west[f], state[f, 0], west[0]) for f in fields}
    for x in range(TILE):
        u = state[0, x]
        v = state[1, x]
        w = state[2, x]
        u_to, u_from = DIFFUSION - 0.5 * u, DIFFUSION + 0.5 * u
        v_to, v_from = DIFFUSION - 0.5 * v, DIFFUSION + 0.5 * v
        w_to, w_from = DIFFUSION * inv_space - 0.5 * w, DIFFUSION * inv_space + 0.5 * w
        v_south = south[1, x : x + 1]
        fluid = jnp.where(level >= height[x], RK_STEP * TIME_STEP, 0.0)
        for f in fields:
            s = state[f, x]
            e = state[f, x + 1] if x < TILE - 1 else east[f]
            x_face = e * u_to - s * u_from
            upper_y = jnp.concatenate([s[1:], north[f, x : x + 1]], axis=0)
            y_face = upper_y * v_to - s * v_from
            first_y = x_faces(south[f, x : x + 1], s[:1], v_south)
            y_below = jnp.concatenate([first_y, y_face[:-1]], axis=0)
            z_face = lanes_up(s) * w_to - s * w_from
            change = (x_face - before[f]) + (y_face - y_below)
            change = change + (z_face - lanes_down(z_face)) * inv_thick
            if f == 2:
                change = change + BUOYANCY * state[3, x]
            before[f] = x_face
            store(f, x, s + (RK_STEP * RK_KEEP) * memory[f, x] + fluid * change)


def momentum_kernel(
    state, memory, west, east, south, north, inv_rows, height, pack, provisional, message
):
    def store(f, x, value):
        provisional[f, x] = value

    advance_fields(
        (0, 1, 2), state, memory, west, east, south, north, inv_rows, height, store
    )
    inv_thick = inv_rows[0:1, :]
    zeros = jnp.zeros((TILE, WIDE - LEVELS), jnp.float32)
    last_u = jnp.concatenate([provisional[0, TILE - 1], zeros], axis=1)
    u_packed = jnp.where(
        chunk_mask((LINE, WIDE), "high"), jnp.concatenate([last_u] * TILE, axis=0), 0.0
    )
    v_rows = []
    for x in range(TILE):
        last_v = jnp.broadcast_to(provisional[1, x, TILE - 1 :], (TILE, LEVELS))
        v_rows.append(jnp.concatenate([last_v, zeros], axis=1))
    v_packed = jnp.where(chunk_mask((LINE, WIDE), "low"), jnp.concatenate(v_rows, axis=0), 0.0)
    upper = product(v_packed, pack[0]) + product(u_packed, pack[1])
    for x in range(TILE):
        u = provisional[0, x]
        v = provisional[1, x]
        w = provisional[2, x]
        v_before = jnp.concatenate([jnp.zeros_like(v[:1]), v[:-1]], axis=0)
        diverge = (v - v_before) + (w - lanes_down(w)) * inv_thick
        diverge = diverge + (u - provisional[0, x - 1] if x else u)
        message[x, :, :128] = diverge[:, :128]
        message[x, :, 128:] = (
            jnp.concatenate([diverge[:, 128:], zeros], axis=1)
            + upper[x * TILE : (x + 1) * TILE]
        )


def scalars_kernel(state, memory, west, east, south, north, inv_rows, height, out):
    def store(f, x, value):
        out[f - 3, x] = value

    advance_fields((3, 4), state, memory, west, east, south, north, inv_rows, height, store)


def forward_y_kernel(lines, basis, after, unpack, spectrum):
    values = lines[...]
    extra = jnp.where(
        chunk_mask((LINE, WIDE), "low"), product(values[:, 128:], unpack[0]), 0.0
    )
    total = product(basis[...], values) - product(after[...], extra, ((0,), (0,)))
    spectrum[:, 0, :] = total


def rows_down(a, stride):
    return jnp.concatenate([jnp.zeros_like(a[:stride]), a[:-stride]], axis=0)


def rows_up(a, stride):
    return jnp.concatenate([a[stride:], jnp.zeros_like(a[:stride])], axis=0)


def factors_kernel(columns, shift, lower, upper, inverse):
    below = jnp.broadcast_to(columns[:, 0:1], (LEVELS, LINE))
    above = jnp.broadcast_to(columns[:, 2:3], (LEVELS, LINE))
    diagonal = columns[:, 1:2] - shift[...]
    for step, stride in enumerate(STRIDES):
        reciprocal = 1.0 / diagonal
        low = -below * rows_down(reciprocal, stride)
        high = -above * rows_up(reciprocal, stride)
        lower[step] = low
        upper[step] = high
        diagonal = diagonal + low * rows_down(above, stride) + high * rows_up(below, stride)
        below = low * rows_down(below, stride)
        above = high * rows_up(above, stride)
    inverse[...] = 1.0 / diagonal


def solve_kernel(lines, basis, after, unpack, pack, lower, upper, inverse, result):
    values = lines[:, 0, :]
    mask = chunk_mask((LINE, WIDE), "low")
    extra = jnp.where(mask, product(values[:, 128:], unpack[1]), 0.0)
    main = product(values, basis[...], ((0,), (0,)))
    fix = product(extra, after[...], ((0,), (0,)))
    right = main[:LEVELS] - fix[:LEVELS]
    for step, stride in enumerate(STRIDES):
        right = (
            right
            + lower[step] * rows_down(right, stride)
            + upper[step] * rows_up(right, stride)
        )
    solved = right * inverse[...]
    solved = jnp.concatenate([solved, jnp.zeros((WIDE - LEVELS, LINE), jnp.float32)], axis=0)
    back = product(basis[...], solved, ((1,), (1,)))
    beside = jnp.where(mask, product(after[...], solved, ((1,), (1,))), 0.0)
    result[:, 0, :128] = back[:, :128]
    result[:, 0, 128:] = back[:, 128:] + product(beside, pack[0])


def backward_y_kernel(lines, basis, after, pack, message):
    values = lines[:, 0, :]
    back = product(basis[...], values)
    beside = jnp.where(
        chunk_mask((LINE, WIDE), "low"), product(after[...], values), 0.0
    )
    message[:, :128] = back[:, :128]
    message[:, 128:] = back[:, 128:] + product(beside, pack[1])


def correct_kernel(message, provisional, scalars, inv_rows, height, unpack, updated, pressure):
    inv_space = inv_rows[1:2, :]
    level = lax.broadcasted_iota(jnp.int32, (TILE, LEVELS), 1)
    packed = message[:, :, 128:].reshape(LINE, 128)
    east = jnp.where(chunk_mask((LINE, WIDE), "high"), product(packed, unpack[0]), 0.0)
    east = east.reshape(TILE, TILE, WIDE).sum(axis=0)[:, :LEVELS]
    north = jnp.where(chunk_mask((LINE, WIDE), "low"), product(packed, unpack[1]), 0.0)
    north = north.reshape(TILE, TILE, WIDE).sum(axis=1)[:, :LEVELS]
    for x in range(TILE):
        p = message[x, :, :LEVELS]
        p_east = message[x + 1, :, :LEVELS] if x < TILE - 1 else east
        p_north = jnp.concatenate([p[1:], north[x : x + 1]], axis=0)
        p_upper = jnp.concatenate([p[:, 1:], jnp.zeros_like(p[:, :1])], axis=1)
        fluid = level >= height[x]
        updated[0, x] = jnp.where(fluid, provisional[0, x] - (p_east - p), 0.0)
        updated[1, x] = jnp.where(fluid, provisional[1, x] - (p_north - p), 0.0)
        updated[2, x] = jnp.where(fluid, provisional[2, x] - (p_upper - p) * inv_space, 0.0)
        updated[3, x] = scalars[0, x]
        updated[4, x] = scalars[1, x]
        pressure[x] = p


def shaped(*shape):
    return jax.ShapeDtypeStruct(shape, jnp.float32)


def call(kernel, out_shape, *operands, flops=0):
    count = sum(int(np.prod(a.shape)) for a in operands) * 4
    return pl.pallas_call(
        kernel,
        out_shape=out_shape,
        name=kernel.__name__,
        compiler_params=pltpu.CompilerParams(vmem_limit_bytes=40 * 1024 * 1024),
        cost_estimate=pl.CostEstimate(flops=flops, bytes_accessed=count, transcendentals=0),
    )(*operands)


def passed(block, axis, distance):
    count = lax.axis_size(axis)
    return lax.ppermute(block, axis, [((i - distance) % count, i) for i in range(count)])


def eigenvalues(frequency):
    return 2.0 - 2.0 * jnp.cos((2.0 * jnp.pi / LINE) * frequency.astype(jnp.float32))


def per_device(state, memory, level_steps, building_height):
    plane = shaped(5, TILE, LEVELS)
    edges = call(edges_kernel, [plane] * 4, state)
    west = passed(edges[1], "px", 1)
    east = passed(edges[0], "px", -1)
    south = passed(edges[3], "py", 1)
    north = passed(edges[2], "py", -1)

    thickness = level_steps.astype(jnp.float32)
    spacing = jnp.concatenate([0.5 * (thickness[:-1] + thickness[1:]), thickness[-1:]])
    inv_rows = jnp.stack([1.0 / thickness, 1.0 / spacing])
    height = building_height[:, :, None]
    upward = 1.0 / (thickness * spacing)
    downward = jnp.concatenate(
        [jnp.zeros_like(thickness[:1]), 1.0 / (thickness[1:] * spacing[:-1])]
    )
    above = jnp.concatenate([upward[:-1], jnp.zeros_like(thickness[:1])])
    columns = jnp.stack([downward, -(upward + downward), above], axis=1)
    own_y = lax.axis_index("px") * lax.axis_size("py") + lax.axis_index("py")
    shift = eigenvalues(jnp.arange(LINE, dtype=jnp.int32)) + eigenvalues(own_y)
    basis, after, unpack, pack = (jnp.asarray(a) for a in (BASIS, AFTER, UNPACK, PACK))

    halos = (west, east, south, north)
    provisional, message = call(
        momentum_kernel,
        [shaped(3, TILE, TILE, LEVELS), shaped(TILE, TILE, WIDE)],
        state, memory, *halos, inv_rows, height, pack,
        flops=10**7,
    )
    scalars = call(
        scalars_kernel, shaped(2, TILE, TILE, LEVELS), state, memory, *halos, inv_rows, height,
        flops=10**7,
    )
    factors = call(
        factors_kernel,
        [shaped(len(STRIDES), LEVELS, LINE), shaped(len(STRIDES), LEVELS, LINE), shaped(LEVELS, LINE)],
        columns, shift.reshape(1, LINE),
        flops=10**7,
    )
    lines = lax.all_to_all(message, "py", split_axis=0, concat_axis=0, tiled=True)
    spectrum = call(
        forward_y_kernel, shaped(LINE, 1, WIDE), lines.reshape(LINE, WIDE), basis, after, unpack
    )
    lines = lax.all_to_all(spectrum, ("px", "py"), split_axis=0, concat_axis=0, tiled=True)
    solved = call(
        solve_kernel, shaped(LINE, 1, WIDE), lines, basis, after, unpack, pack, *factors
    )
    lines = lax.all_to_all(solved, ("px", "py"), split_axis=0, concat_axis=0, tiled=True)
    message = call(backward_y_kernel, shaped(LINE, WIDE), lines, basis, after, pack)
    message = lax.all_to_all(
        message.reshape(TILE, TILE, WIDE), "py", split_axis=0, concat_axis=0, tiled=True
    )
    return call(
        correct_kernel,
        [shaped(5, TILE, TILE, LEVELS), shaped(TILE, TILE, LEVELS)],
        message, provisional, scalars, inv_rows, height, unpack,
    )


def solution(mesh):
    return jax.shard_map(
        per_device,
        mesh=mesh,
        in_specs=(P(None, "px", "py", None), P(None, "px", "py", None), P(), P("px", "py")),
        out_specs=(P(None, "px", "py", None), P("px", "py", None)),
        check_vma=False,
    )
```

time: 194 us -> 115 us (0.59)
  other arithmetic: 33.9 us -> 2.36 us
  waiting for transfers between devices: 48.2 us -> 17.5 us
  local copies, waits for them, and re-layouts: 40.9 us -> 15.9 us
  blocking collectives: 16.6 us -> 38.1 us
  starting transfers between devices: 46.3 us -> 25.5 us
  Pallas kernels: 0 us -> 14.2 us
  matrix products: 4.96 us -> 0 us
    all_to_all x5 -> x2, waiting for transfers between devices: 40.2 us -> 17.5 us  [the longest x1 11.9 us: per_device(): lax.all_to_all(spectrum, ('px', 'py'), split_axis=0, concat_axis=0, tiled...]
    all_to_all x1 -> x2, blocking collectives: 16.6 us -> 38.1 us  [the longest x1 21.6 us: per_device(): lax.all_to_all(solved, ('px', 'py'), split_axis=0, concat_axis=0, tiled=T...]
    all_to_all x5 -> x2, starting transfers between devices: 33 us -> 15.7 us  [the longest x1 11.5 us: per_device(): lax.all_to_all(spectrum, ('px', 'py'), split_axis=0, concat_axis=0, tiled...]
    pallas_call x0 -> x8, Pallas kernels: none -> 14.2 us  [call(): pl.pallas_call(kernel, out_shape=out_shape, name=kernel.__name__, compile...]
    mul x17 -> x0, other arithmetic: 12.9 us -> none  [the longest x7 6.51 us: cyclic_solve(): lower_factor * shifted_down(right_side, stride, 0.0)]
    another operation x10 -> x1, local copies, waits for them, and re-layouts: 11.3 us -> 0.12 us  [per_device(): columns = jnp.stack([downward, -(upward + downward), above], axis=1)]
    slice x45 -> x1, local copies, waits for them, and re-layouts: 8.66 us -> 0.59 us  [per_device(): thickness[-1:]]
    ppermute x8 -> x4, waiting for transfers between devices: 7.97 us -> 0.01 us  [passed(): lax.ppermute(block, axis, [((i - distance) % count, i) for i in range(cou...]
  transfers between devices with their start and end apart: 13 -> 6, of which waited for: 8 -> 2; matrix products, arithmetic and copies ran while one was open for 25% -> 3% of each run, Pallas kernels for 0% -> 2%
where the time goes in v1:
time: 115 us
  blocking collectives  38.1 us (33%)
  starting transfers between devices  25.5 us (22%)
  waiting for transfers between devices  17.5 us (15%)
  local copies, waits for them, and re-layouts  15.9 us (14%)
  Pallas kernels  14.2 us (12%)
  other arithmetic  2.36 us (2%)
    all_to_all x1, blocking collectives, per_device(): lax.all_to_all(solved, ('px', 'py'), split_axis=0, concat_axis=0, tiled=T...  21.6 us
    all_to_all x1, blocking collectives, per_device(): lax.all_to_all(message, 'py', split_axis=0, concat_axis=0, tiled=True)  16.5 us
    unnamed x54, local copies, waits for them, and re-layouts  15 us
    pallas_call x8, Pallas kernels, call(): pl.pallas_call(kernel, out_shape=out_shape, name=kernel.__name__, compile...  14.2 us
    all_to_all x1, waiting for transfers between devices, per_device(): lax.all_to_all(spectrum, ('px', 'py'), split_axis=0, concat_axis=0, tiled...  11.9 us
    all_to_all x1, starting transfers between devices, per_device(): lax.all_to_all(spectrum, ('px', 'py'), split_axis=0, concat_axis=0, tiled...  11.5 us
    ppermute x4, starting transfers between devices, passed(): lax.ppermute(block, axis, [((i - distance) % count, i) for i in range(cou...  9.82 us
    all_to_all x1, waiting for transfers between devices, per_device(): lax.all_to_all(message.reshape(TILE, TILE, WIDE), 'py', split_axis=0, con...  5.55 us
  transfers between devices with their start and end apart: 6, of which 2 were waited for; matrix products, arithmetic and copies ran while one was open for 3% of the time, Pallas kernels for 2%

profile of v1, /device:TPU:1, one launch (start us, length us, event | category | flops | bytes accessed | tf_op | source)
XLA Modules:
  0.0 114.5 jit_solution(13298750428193172919)
XLA Ops:
  0.6 1.3 %copy-done = f32[5,16,16,192]{3,2,1,0:T(8,128)S(1)} copy-done((f32[5,16,16,192]{3,2,1,0:T(8,128)S(1)}, f32[5,16,16,192]{3,2,1,0:T(8,128)}, u32[]{:S(2)}) %copy-start) | copy-done | bytes 983064
  2.0 4.2 %collective-permute-start = (f32[5,16,192]{2,1,0:T(8,128)S(1)}, f32[5,16,192]{2,1,0:T(8,128)S(1)}, u32[]{:S(2)}, u32[]{:S(2)}) collective-permute-start(f32[5,16,192]{2,1,0:T(8,128)S(1)} %get-tuple-element.11), channel_id=1, source_target_pairs={{240,0},{0,16},{16,32},{32,48},{48,64},{64,80},{80,96},{96,112},{1... | collective-permute-start | bytes 184328 | tf_op jit(solution)/shard_map/ppermute | solution.py:253
  6.6 5.3 %collective-permute-start.3 = (f32[5,16,192]{2,1,0:T(8,128)S(1)}, f32[5,16,192]{2,1,0:T(8,128)S(1)}, u32[]{:S(2)}, u32[]{:S(2)}) collective-permute-start(f32[5,16,192]{2,1,0:T(8,128)S(1)} %get-tuple-element.14), channel_id=1, source_target_pairs={{1,0},{2,1},{3,2},{4,3},{5,4},{6,5},{7,6},{8,7},{9,8},{10,9},{11,1... | collective-permute-start | bytes 184328 | tf_op jit(solution)/shard_map/ppermute | solution.py:253
  14.9 1.3 %copy-done.2 = f32[5,16,16,192]{3,2,1,0:T(8,128)S(1)} copy-done((f32[5,16,16,192]{3,2,1,0:T(8,128)S(1)}, f32[5,16,16,192]{3,2,1,0:T(8,128)}, u32[]{:S(2)}) %copy-start.2) | copy-done | bytes 983064
  16.3 0.9 copy-done.5
  17.2 3.3 %momentum_kernel.1 = (f32[3,16,16,192]{3,2,1,0:T(8,128)S(1)}, f32[16,16,256]{2,1,0:T(8,128)S(1)}) custom-call(f32[5,16,16,192]{3,2,1,0:T(8,128)S(1)} %copy-done.1, f32[5,16,16,192]{3,2,1,0:T(8,128)S(1)} %copy-done.2, f32[5,16,192]{2,1,0:T(8,128)S(1)} %collective-permute-done.west, f32[5,16,192]{2,1,0:T(8,128)S(1)} %collective-permute-done.1.east, ...), custom_call_target="tpu_custom_call" | custom-call | flops 10000000 | bytes 2476544 | tf_op jit(solution)/shard_map/momentum_kernel/pallas_call | solution.py:242
  21.5 16.5 %all_to_all.20 = f32[16,16,256]{2,1,0:T(8,128)S(1)} all-to-all(f32[16,16,256]{2,1,0:T(8,128)S(1)} %get-tuple-element.15), channel_id=1, replica_groups=mesh['px'=16,'py'=16] {'py'}, dimensions={0} | all-to-all | bytes 524288 | tf_op jit(solution)/shard_map/all_to_all | solution.py:299
  38.0 1.7 %forward_y_kernel.1 = f32[256,1,256]{2,1,0:T(1,128)} custom-call(f32[256,256]{1,0:T(8,128)S(1)} %bitcast.11, f32[256,256]{1,0:T(8,128)S(1)} %copy-done.7, f32[256,256]{1,0:T(8,128)S(1)} %copy-done.8, f32[2,128,256]{2,1,0:T(8,128)S(1)} %copy-done.4), custom_call_target="tpu_custom_call" | custom-call | bytes 1048576 | tf_op jit(solution)/shard_map/forward_y_kernel/pallas_call | solution.py:242
  39.7 11.5 %all-to-all-start.1 = ((f32[256,1,256]{2,1,0:T(1,128)}), f32[256,1,256]{2,1,0:T(1,128)S(1)}, u32[]{:S(2)}, u32[]{:S(2)}) async-start(f32[256,1,256]{2,1,0:T(1,128)} %forward_y_kernel.1), calls=%async_computation.1 | async-start | bytes 524288 | tf_op jit(solution)/shard_map/all_to_all | solution.py:303
  51.5 0.9 factors_kernel.1
  52.5 1.2 %copy-done.10 = f32[8,192,256]{2,1,0:T(8,128)} copy-done((f32[8,192,256]{2,1,0:T(8,128)}, f32[8,192,256]{2,1,0:T(8,128)S(1)}, u32[]{:S(2)}) %copy-start.10) | copy-done | bytes 1572888
  53.7 1.1 copy-done.12
  54.8 11.9 %all-to-all-done.1.lines = f32[256,1,256]{2,1,0:T(1,128)S(1)} async-done(((f32[256,1,256]{2,1,0:T(1,128)}), f32[256,1,256]{2,1,0:T(1,128)S(1)}, u32[]{:S(2)}, u32[]{:S(2)}) %all-to-all-start.1) | async-done | bytes 262176 | tf_op jit(solution)/shard_map/all_to_all | solution.py:303
  66.8 1.4 %copy-done.11 = f32[8,192,256]{2,1,0:T(8,128)S(1)} copy-done((f32[8,192,256]{2,1,0:T(8,128)S(1)}, f32[8,192,256]{2,1,0:T(8,128)}, u32[]{:S(2)}) %copy-start.11) | copy-done | bytes 1572888
  68.2 1.4 %copy-done.13 = f32[8,192,256]{2,1,0:T(8,128)S(1)} copy-done((f32[8,192,256]{2,1,0:T(8,128)S(1)}, f32[8,192,256]{2,1,0:T(8,128)}, u32[]{:S(2)}) %copy-start.13) | copy-done | bytes 1572888
  69.6 2.6 %solve_kernel.1 = f32[256,1,256]{2,1,0:T(1,128)S(1)} custom-call(f32[256,1,256]{2,1,0:T(1,128)S(1)} %all-to-all-done.1.lines, f32[256,256]{1,0:T(8,128)S(1)} %copy-done.7, f32[256,256]{1,0:T(8,128)S(1)} %copy-done.8, f32[2,128,256]{2,1,0:T(8,128)S(1)} %copy-done.4, f32[2,256,128]{2,1,0:T(8,128)S(1)} %copy-done.6, f32[8,192,256]{2,1,0:T(8,128)S(1)} %copy-done.11, ...), custom_call_target="tpu_custom_call" | custom-call | bytes 4653056 | tf_op jit(solution)/shard_map/solve_kernel/pallas_call | solution.py:242
  72.1 21.6 %all_to_all.21.lines = f32[256,1,256]{2,1,0:T(1,128)S(1)} all-to-all(f32[256,1,256]{2,1,0:T(1,128)S(1)} %solve_kernel.1), channel_id=1, replica_groups=mesh['px'=16,'py'=16] {'px','py'}, dimensions={0} | all-to-all | bytes 524288 | tf_op jit(solution)/shard_map/all_to_all | solution.py:307
  93.7 1.3 %backward_y_kernel.1 = f32[256,256]{1,0:T(8,128)S(1)} custom-call(f32[256,1,256]{2,1,0:T(1,128)S(1)} %all_to_all.21.lines, f32[256,256]{1,0:T(8,128)S(1)} %copy-done.7, f32[256,256]{1,0:T(8,128)S(1)} %copy-done.9, f32[2,256,128]{2,1,0:T(8,128)S(1)} %copy-done.6), custom_call_target="tpu_custom_call" | custom-call | bytes 1048576 | tf_op jit(solution)/shard_map/backward_y_kernel/pallas_call | solution.py:242
  95.8 4.2 %all-to-all-start.3 = ((f32[16,16,256]{2,1,0:T(8,128)}), f32[16,16,256]{2,1,0:T(8,128)}, u32[]{:S(2)}, u32[]{:S(2)}) async-start(f32[16,16,256]{2,1,0:T(8,128)} %bitcast.10), calls=%async_computation.3 | async-start | bytes 524288 | tf_op jit(solution)/shard_map/all_to_all | solution.py:309
  100.9 0.9 copy-done.20
  103.6 1.6 %scalars_kernel.1.scalars = f32[2,16,16,192]{3,2,1,0:T(8,128)S(1)} custom-call(f32[5,16,16,192]{3,2,1,0:T(8,128)S(1)} %copy-done.1, f32[5,16,16,192]{3,2,1,0:T(8,128)S(1)} %copy-done.3, f32[5,16,192]{2,1,0:T(8,128)S(1)} %copy-done.18, f32[5,16,192]{2,1,0:T(8,128)S(1)} %copy-done.20, f32[5,16,192]{2,1,0:T(8,128)S(1)} %copy-done.22, ...), custom_call_target="tpu_custom_call" | custom-call | flops 10000000 | bytes 2214400 | tf_op jit(solution)/shard_map/scalars_kernel/pallas_call | solution.py:242
  105.1 5.6 %all-to-all-done.3.message = f32[16,16,256]{2,1,0:T(8,128)} async-done(((f32[16,16,256]{2,1,0:T(8,128)}), f32[16,16,256]{2,1,0:T(8,128)}, u32[]{:S(2)}, u32[]{:S(2)}) %all-to-all-start.3) | async-done | bytes 262176 | tf_op jit(solution)/shard_map/all_to_all | solution.py:309
  110.7 1.1 copy-done.16
  111.8 2.7 %correct_kernel.1 = (f32[5,16,16,192]{3,2,1,0:T(8,128)}, f32[16,16,192]{2,1,0:T(8,128)}) custom-call(f32[16,16,256]{2,1,0:T(8,128)} %all-to-all-done.3.message, f32[3,16,16,192]{3,2,1,0:T(8,128)S(1)} %copy-done.16, f32[2,16,16,192]{3,2,1,0:T(8,128)S(1)} %scalars_kernel.1.scalars, f32[2,192]{1,0:T(2,128)S(1)} %pad_maximum_fusion.1.inv_rows, ...), custom_call_target="tpu_custom_call" | custom-call | bytes 1509888 | tf_op jit(solution)/shard_map/correct_kernel/pallas_call | solution.py:242
  (63 shorter events, 7.9 us)
Async XLA Ops:
  0.6 1.3 %copy-start = (f32[5,16,16,192]{3,2,1,0:T(8,128)S(1)}, f32[5,16,16,192]{3,2,1,0:T(8,128)}, u32[]{:S(2)}) copy-start(f32[5,16,16,192]{3,2,1,0:T(8,128)} %state.5) | copy-start | bytes 2949124
  1.9 11.3 %copy-start.25 = (s32[16,16]{1,0:T(8,128)S(1)}, s32[16,16]{1,0:T(8,128)}, u32[]{:S(2)}) copy-start(s32[16,16]{1,0:T(8,128)} %param.11) | copy-start | bytes 3076
  1.9 11.4 %copy-start.26 = (s32[192]{0:T(256)S(1)}, s32[192]{0:T(256)}, u32[]{:S(2)}) copy-start(s32[192]{0:T(256)} %param.10) | copy-start | bytes 2308
  2.0 13.0 %copy-start.1 = (f32[5,16,16,192]{3,2,1,0:T(8,128)S(1)}, f32[5,16,16,192]{3,2,1,0:T(8,128)}, u32[]{:S(2)}) copy-start(f32[5,16,16,192]{3,2,1,0:T(8,128)} %state.5) | copy-start | bytes 2949124
  2.0 12.8 %collective-permute-start = (f32[5,16,192]{2,1,0:T(8,128)S(1)}, f32[5,16,192]{2,1,0:T(8,128)S(1)}, u32[]{:S(2)}, u32[]{:S(2)}) collective-permute-start(f32[5,16,192]{2,1,0:T(8,128)S(1)} %get-tuple-element.11), channel_id=1, source_target_pairs={{240,0},{0,16},{16,32},{32,48},{48,64},{64,80},{80,96},{96,112},{1... | collective-permute-start | bytes 184328 | tf_op jit(solution)/shard_map/ppermute | solution.py:253
  6.3 8.6 %collective-permute-start.1 = (f32[5,16,192]{2,1,0:T(8,128)S(1)}, f32[5,16,192]{2,1,0:T(8,128)S(1)}, u32[]{:S(2)}, u32[]{:S(2)}) collective-permute-start(f32[5,16,192]{2,1,0:T(8,128)S(1)} %get-tuple-element.12), channel_id=1, source_target_pairs={{16,0},{32,16},{48,32},{64,48},{80,64},{96,80},{112,96},{128,112},... | collective-permute-start | bytes 184328 | tf_op jit(solution)/shard_map/ppermute | solution.py:253
  6.3 8.6 %collective-permute-start.2 = (f32[5,16,192]{2,1,0:T(8,128)S(1)}, f32[5,16,192]{2,1,0:T(8,128)S(1)}, u32[]{:S(2)}, u32[]{:S(2)}) collective-permute-start(f32[5,16,192]{2,1,0:T(8,128)S(1)} %get-tuple-element.13), channel_id=1, source_target_pairs={{15,0},{0,1},{1,2},{2,3},{3,4},{4,5},{5,6},{6,7},{7,8},{8,9},{9,10... | collective-permute-start | bytes 184328 | tf_op jit(solution)/shard_map/ppermute | solution.py:253
  6.6 8.3 %collective-permute-start.3 = (f32[5,16,192]{2,1,0:T(8,128)S(1)}, f32[5,16,192]{2,1,0:T(8,128)S(1)}, u32[]{:S(2)}, u32[]{:S(2)}) collective-permute-start(f32[5,16,192]{2,1,0:T(8,128)S(1)} %get-tuple-element.14), channel_id=1, source_target_pairs={{1,0},{2,1},{3,2},{4,3},{5,4},{6,5},{7,6},{8,7},{9,8},{10,9},{11,1... | collective-permute-start | bytes 184328 | tf_op jit(solution)/shard_map/ppermute | solution.py:253
  14.9 5.7 %copy-start.17 = (f32[5,16,192]{2,1,0:T(8,128)}, f32[5,16,192]{2,1,0:T(8,128)S(1)}, u32[]{:S(2)}) copy-start(f32[5,16,192]{2,1,0:T(8,128)S(1)} %collective-permute-done.west) | copy-start | bytes 184324
  14.9 5.7 %copy-start.19 = (f32[5,16,192]{2,1,0:T(8,128)}, f32[5,16,192]{2,1,0:T(8,128)S(1)}, u32[]{:S(2)}) copy-start(f32[5,16,192]{2,1,0:T(8,128)S(1)} %collective-permute-done.1.east) | copy-start | bytes 184324
  14.9 5.7 %copy-start.21 = (f32[5,16,192]{2,1,0:T(8,128)}, f32[5,16,192]{2,1,0:T(8,128)S(1)}, u32[]{:S(2)}) copy-start(f32[5,16,192]{2,1,0:T(8,128)S(1)} %collective-permute-done.2.south) | copy-start | bytes 184324
  14.9 1.4 %copy-start.2 = (f32[5,16,16,192]{3,2,1,0:T(8,128)S(1)}, f32[5,16,16,192]{3,2,1,0:T(8,128)}, u32[]{:S(2)}) copy-start(f32[5,16,16,192]{3,2,1,0:T(8,128)} %memory.3) | copy-start | bytes 2949124
  17.2 3.4 %copy-start.23 = (f32[5,16,192]{2,1,0:T(8,128)}, f32[5,16,192]{2,1,0:T(8,128)S(1)}, u32[]{:S(2)}) copy-start(f32[5,16,192]{2,1,0:T(8,128)S(1)} %collective-permute-done.3.north) | copy-start | bytes 184324
  17.2 20.8 %copy-start.4 = (f32[2,128,256]{2,1,0:T(8,128)S(1)}, f32[2,128,256]{2,1,0:T(8,128)}, u32[]{:S(2)}) copy-start(f32[2,128,256]{2,1,0:T(8,128)} %constant.32.clone.unpack) | copy-start | bytes 786436
  17.2 20.8 %copy-start.7 = (f32[256,256]{1,0:T(8,128)S(1)}, f32[256,256]{1,0:T(8,128)}, u32[]{:S(2)}) copy-start(f32[256,256]{1,0:T(8,128)} %constant.30.clone.basis) | copy-start | bytes 786436
  17.2 20.8 %copy-start.8 = (f32[256,256]{1,0:T(8,128)S(1)}, f32[256,256]{1,0:T(8,128)}, u32[]{:S(2)}) copy-start(f32[256,256]{1,0:T(8,128)} %constant.31.clone.after) | copy-start | bytes 786436
  21.5 45.2 %copy-start.6 = (f32[2,256,128]{2,1,0:T(8,128)S(1)}, f32[2,256,128]{2,1,0:T(8,128)}, u32[]{:S(2)}) copy-start(f32[2,256,128]{2,1,0:T(8,128)} %constant.33.clone.pack) | copy-start | bytes 786436
  39.7 27.1 %all-to-all-start.1 = ((f32[256,1,256]{2,1,0:T(1,128)}), f32[256,1,256]{2,1,0:T(1,128)S(1)}, u32[]{:S(2)}, u32[]{:S(2)}) async-start(f32[256,1,256]{2,1,0:T(1,128)} %forward_y_kernel.1), calls=%async_computation.1 | async-start | bytes 524288 | tf_op jit(solution)/shard_map/all_to_all | solution.py:303
  52.5 1.2 %copy-start.10 = (f32[8,192,256]{2,1,0:T(8,128)}, f32[8,192,256]{2,1,0:T(8,128)S(1)}, u32[]{:S(2)}) copy-start(f32[8,192,256]{2,1,0:T(8,128)S(1)} %get-tuple-element.16.lower) | copy-start | bytes 4718596
  66.8 1.4 %copy-start.11 = (f32[8,192,256]{2,1,0:T(8,128)S(1)}, f32[8,192,256]{2,1,0:T(8,128)}, u32[]{:S(2)}) copy-start(f32[8,192,256]{2,1,0:T(8,128)} %copy-done.10) | copy-start | bytes 4718596
  68.2 1.4 %copy-start.13 = (f32[8,192,256]{2,1,0:T(8,128)S(1)}, f32[8,192,256]{2,1,0:T(8,128)}, u32[]{:S(2)}) copy-start(f32[8,192,256]{2,1,0:T(8,128)} %copy-done.12) | copy-start | bytes 4718596
  69.6 24.2 %copy-start.9 = (f32[256,256]{1,0:T(8,128)S(1)}, f32[256,256]{1,0:T(8,128)}, u32[]{:S(2)}) copy-start(f32[256,256]{1,0:T(8,128)} %constant.31.clone.after) | copy-start | bytes 786436
  72.1 27.9 %copy-start.3 = (f32[5,16,16,192]{3,2,1,0:T(8,128)S(1)}, f32[5,16,16,192]{3,2,1,0:T(8,128)}, u32[]{:S(2)}) copy-start(f32[5,16,16,192]{3,2,1,0:T(8,128)} %memory.3) | copy-start | bytes 2949124
  95.8 14.9 %all-to-all-start.3 = ((f32[16,16,256]{2,1,0:T(8,128)}), f32[16,16,256]{2,1,0:T(8,128)}, u32[]{:S(2)}, u32[]{:S(2)}) async-start(f32[16,16,256]{2,1,0:T(8,128)} %bitcast.10), calls=%async_computation.3 | async-start | bytes 524288 | tf_op jit(solution)/shard_map/all_to_all | solution.py:309
  (9 other events, 8.4 us)

commit v2 on v1

v2 whole, which is shorter than its diff:
```python
import jax
import jax.numpy as jnp
import numpy as np
from jax import lax
from jax.experimental import pallas as pl
from jax.experimental.pallas import tpu as pltpu
from jax.sharding import PartitionSpec as P

RK_KEEP = -5.0 / 9.0
RK_STEP = 15.0 / 16.0
TIME_STEP = 0.1
DIFFUSION = 0.05
BUOYANCY = 0.3
HIGHEST = lax.Precision.HIGHEST

TILE = 16
LINE = 256
LEVELS = 192
WIDE = 256
CHUNK = LEVELS // TILE
FIRST = 192
SECOND = 208
UNROLL = 3
MOST_VMEM = 50331648
STRIDES = (1, 2, 4, 8, 16, 32, 64, 128)


def tables():
    n = np.arange(LINE)
    angles = 2.0 * np.pi / LINE * (np.outer(n, n) % LINE)
    basis = (np.cos(angles) + np.sin(angles)) / np.sqrt(LINE)
    after = basis[(n[:TILE] + 1) * TILE % LINE]
    return basis.astype(np.float32), after.astype(np.float32)


BASIS, AFTER = tables()


def product(a, b, contract=((1,), (0,))):
    return lax.dot_general(
        a, b, (contract, ((), ())), precision=HIGHEST, preferred_element_type=jnp.float32
    )


def picked(values, places):
    high = values.astype(jnp.bfloat16)
    rest = values - high.astype(jnp.float32)
    middle = rest.astype(jnp.bfloat16)
    low = (rest - middle.astype(jnp.float32)).astype(jnp.bfloat16)
    dots = [
        jnp.dot(part, places, preferred_element_type=jnp.float32) for part in (low, middle, high)
    ]
    return (dots[0] + dots[1]) + dots[2]


def chunk_place(shape, level_dim, first):
    level = lax.broadcasted_iota(jnp.int32, shape, level_dim)
    lane = lax.broadcasted_iota(jnp.int32, shape, 1 - level_dim)
    chunk = jnp.floor((level.astype(jnp.float32) + 0.5) * (1.0 / CHUNK)).astype(jnp.int32)
    here = (level - chunk * CHUNK + (first - 128) == lane) & (level < LEVELS)
    return jnp.where(here, 1.0, 0.0).astype(jnp.bfloat16)


def pack_places(first):
    return chunk_place((WIDE, 128), 0, first)


def unpack_places(first):
    return chunk_place((128, WIDE), 1, first)


def each_block(rows):
    return jnp.concatenate(
        [jnp.broadcast_to(rows[b : b + 1], (TILE, rows.shape[1])) for b in range(TILE)], axis=0
    )


def level_rows(level_steps):
    thickness = level_steps[...].astype(jnp.float32)
    spacing = 0.5 * (thickness + lanes_up(thickness))
    return thickness, spacing


def chunk_mask(shape, owner):
    lane = lax.broadcasted_iota(jnp.int32, shape, 1)
    row = lax.broadcasted_iota(jnp.int32, shape, 0)
    start = (row % TILE if owner == "low" else row // TILE) * CHUNK
    return (lane >= start) & (lane < start + CHUNK)


def lanes_up(a):
    return jnp.concatenate([a[:, 1:], a[:, -1:]], axis=1)


def lanes_down(a):
    return jnp.concatenate([jnp.zeros_like(a[:, :1]), a[:, :-1]], axis=1)


def edges_kernel(state, west, east, south, north):
    west[...] = state[:, 0]
    east[...] = state[:, TILE - 1]
    south[...] = state[:, :, 0]
    north[...] = state[:, :, TILE - 1]


def advance_fields(fields, state, memory, west, east, south, north, level_steps, fluid, store):
    thickness, spacing = level_rows(level_steps)
    inv_thick = 1.0 / thickness
    inv_space = 1.0 / spacing

    def x_faces(s, e, u):
        return e * (DIFFUSION - 0.5 * u) - s * (DIFFUSION + 0.5 * u)

    def plane(x, before, east_of):
        u = state[0, x]
        v = state[1, x]
        w = state[2, x]
        u_to, u_from = DIFFUSION - 0.5 * u, DIFFUSION + 0.5 * u
        v_to, v_from = DIFFUSION - 0.5 * v, DIFFUSION + 0.5 * v
        w_to, w_from = DIFFUSION * inv_space - 0.5 * w, DIFFUSION * inv_space + 0.5 * w
        v_south = south[1, pl.ds(x, 1)]
        factor = (RK_STEP * TIME_STEP) * fluid[x]
        faces = []
        for i, f in enumerate(fields):
            s = state[f, x]
            x_face = east_of(f) * u_to - s * u_from
            upper_y = jnp.concatenate([s[1:], north[f, pl.ds(x, 1)]], axis=0)
            y_face = upper_y * v_to - s * v_from
            first_y = x_faces(south[f, pl.ds(x, 1)], s[:1], v_south)
            y_below = jnp.concatenate([first_y, y_face[:-1]], axis=0)
            z_face = lanes_up(s) * w_to - s * w_from
            change = (x_face - before[i]) + (y_face - y_below)
            change = change + (z_face - lanes_down(z_face)) * inv_thick
            if f == 2:
                change = change + BUOYANCY * state[3, x]
            faces.append(x_face)
            store(f, x, s + (RK_STEP * RK_KEEP) * memory[f, x] + factor * change)
        return tuple(faces)

    before = tuple(x_faces(west[f], state[f, 0], west[0]) for f in fields)
    before = lax.fori_loop(
        0, TILE - 1, lambda x, b: plane(x, b, lambda f: state[f, x + 1]), before, unroll=UNROLL
    )
    plane(TILE - 1, before, lambda f: east[f])


PART = 4


def parts_of(x):
    return pl.ds(x + 1 - PART, PART) if x % PART == PART - 1 else None


def fill_fluid(height, fluid):
    heights = each_block(height[...].astype(jnp.float32))
    row = lax.broadcasted_iota(jnp.int32, (LINE, TILE), 0)
    own = row % TILE == lax.broadcasted_iota(jnp.int32, (LINE, TILE), 1)
    bottom = jnp.sum(jnp.where(own, heights, 0.0), axis=1, keepdims=True)
    level = lax.broadcasted_iota(jnp.int32, (TILE, LEVELS), 1).astype(jnp.float32)
    for x in range(TILE):
        fluid[x] = jnp.where(level >= bottom[x * TILE : (x + 1) * TILE], 1.0, 0.0)


def momentum_kernel(
    state, memory, west, east, south, north, level_steps, height, message, provisional, fluid
):
    fill_fluid(height, fluid)

    def store(f, x, value):
        provisional[f, x] = value

    advance_fields(
        (0, 1, 2), state, memory, west, east, south, north, level_steps, fluid, store
    )
    inv_thick = 1.0 / level_rows(level_steps)[0]
    zeros = jnp.zeros((TILE, WIDE - LEVELS), jnp.float32)
    last_u = jnp.concatenate([provisional[0, TILE - 1], zeros], axis=1)
    u_packed = jnp.where(
        chunk_mask((LINE, WIDE), "high"), jnp.concatenate([last_u] * TILE, axis=0), 0.0
    )
    v_rows = []
    for x in range(TILE):
        last_v = jnp.broadcast_to(provisional[1, x, TILE - 1 :], (TILE, LEVELS))
        v_rows.append(jnp.concatenate([last_v, zeros], axis=1))
    v_packed = jnp.where(chunk_mask((LINE, WIDE), "low"), jnp.concatenate(v_rows, axis=0), 0.0)
    upper = picked(v_packed, pack_places(FIRST)) + picked(u_packed, pack_places(SECOND))
    for x in range(TILE):
        u = provisional[0, x]
        v = provisional[1, x]
        w = provisional[2, x]
        v_before = jnp.concatenate([jnp.zeros_like(v[:1]), v[:-1]], axis=0)
        diverge = (v - v_before) + (w - lanes_down(w)) * inv_thick
        diverge = diverge + (u - provisional[0, x - 1] if x else u)
        message[x, :, :128] = diverge[:, :128]
        message[x, :, 128:] = (
            jnp.concatenate([diverge[:, 128:], zeros], axis=1)
            + upper[x * TILE : (x + 1) * TILE]
        )


def loaded(pairs, sems):
    copies = [pltpu.make_async_copy(a, b, sems.at[i]) for i, (a, b) in enumerate(pairs)]
    for copy in copies:
        copy.start()
    return copies


def unpacked(values, first):
    mask = chunk_mask((LINE, WIDE), "low")
    spread = jnp.where(mask, picked(values[:, 128:], unpack_places(first)), 0.0)
    return spread.reshape(TILE, TILE, WIDE).sum(axis=1)


def repacked(rows, first):
    chunks = jnp.where(chunk_mask((LINE, WIDE), "low"), each_block(rows), 0.0)
    return picked(chunks, pack_places(first))


def forward_y_kernel(lines, basis, after, spectrum):
    values = lines[...]
    extra = unpacked(values, FIRST)
    total = product(basis[...], values) - product(after[...], extra, ((0,), (0,)))
    spectrum[:, 0, :] = total


def column_of(row):
    shape = (LEVELS, LEVELS)
    own = lax.broadcasted_iota(jnp.int32, shape, 0) == lax.broadcasted_iota(jnp.int32, shape, 1)
    return jnp.sum(jnp.where(own, row, 0.0), axis=1, keepdims=True)


def reduced(diagonal, coupling, right):
    for stride in STRIDES:
        shared = LEVELS - stride
        reciprocal = 1.0 / diagonal
        near = coupling[:shared]
        from_above = near * reciprocal[stride:]
        from_below = near * reciprocal[:shared]
        gap = jnp.zeros((stride, right.shape[1]), jnp.float32)
        low = lambda a: jnp.concatenate([a, gap], axis=0)
        high = lambda a: jnp.concatenate([gap, a], axis=0)
        right = right - low(from_above * right[stride:]) - high(from_below * right[:shared])
        diagonal = diagonal - low(near * from_above) - high(near * from_below)
        if shared > stride:
            coupling = low(-from_above * coupling[stride:])
    return right / diagonal


def side_kernel(
    state, memory, west, east, south, north, level_steps, height,
    provisional, updated, fluid,
    state_here, memory_here, halo_here, fluid_here, fields, sems,
):
    halos = (west, east, south, north)
    pairs = [(state, state_here), (memory, memory_here)]
    pairs += [(halo, halo_here.at[i]) for i, halo in enumerate(halos)]
    arriving = loaded(pairs, sems)
    fill_fluid(height, fluid_here)
    leaving = loaded([(fluid_here, fluid)], sems.at[pl.ds(6, 1)])
    for copy in arriving:
        copy.wait()

    def store(f, x, value):
        fields[f, x] = value

    advance_fields(
        (0, 1, 2, 3, 4), state_here, memory_here, *[halo_here.at[i] for i in range(4)],
        level_steps, fluid_here, store,
    )
    pairs = [(fields.at[0:3], provisional), (fields.at[3:5], updated.at[3:5])]
    leaving += loaded(pairs, sems.at[pl.ds(7, 2)])
    for copy in leaving:
        copy.wait()


def solve_kernel(lines, basis, after, level_steps, shift, result):
    thickness, spacing = level_rows(level_steps)
    level = lax.broadcasted_iota(jnp.int32, (1, LEVELS), 1)
    inv_space = 1.0 / spacing
    thick = column_of(thickness)
    diagonal = column_of(inv_space + lanes_down(inv_space)) + thick * shift[...]
    between = column_of(jnp.where(level < LEVELS - 1, -inv_space, 0.0))
    coupling = jnp.broadcast_to(between, (LEVELS, LINE))
    values = lines[:, 0, :]
    extra = unpacked(values, SECOND)
    main = product(values, basis[...], ((0,), (0,)))
    fix = product(extra, after[...], ((0,), (0,)))
    right = thick * (fix[:LEVELS] - main[:LEVELS])
    solved = reduced(diagonal, coupling, right)
    solved = jnp.concatenate([solved, jnp.zeros((WIDE - LEVELS, LINE), jnp.float32)], axis=0)
    back = product(basis[...], solved, ((1,), (1,)))
    beside = product(after[...], solved, ((1,), (1,)))
    result[:, 0, :128] = back[:, :128]
    result[:, 0, 128:] = back[:, 128:] + repacked(beside, FIRST)


def backward_y_kernel(lines, basis, after, message):
    values = lines[:, 0, :]
    back = product(basis[...], values)
    beside = product(after[...], values)
    message[:, :128] = back[:, :128]
    message[:, 128:] = back[:, 128:] + repacked(beside, SECOND)


def correct_kernel(
    message, provisional, level_steps, fluid, updated_in, updated, pressure, fields, cells, sems
):
    copies = []
    inv_space = 1.0 / level_rows(level_steps)[1]
    packed = message[:, :, 128:].reshape(LINE, 128)
    east = jnp.where(chunk_mask((LINE, WIDE), "high"), picked(packed, unpack_places(FIRST)), 0.0)
    east = east.reshape(TILE, TILE, WIDE).sum(axis=0)[:, :LEVELS]
    north = unpacked(message[...].reshape(LINE, WIDE), SECOND)[:, :LEVELS]
    for x in range(TILE):
        p = message[x, :, :LEVELS]
        p_east = message[x + 1, :, :LEVELS] if x < TILE - 1 else east
        p_north = jnp.concatenate([p[1:], north[x : x + 1]], axis=0)
        p_upper = jnp.concatenate([p[:, 1:], jnp.zeros_like(p[:, :1])], axis=1)
        open_cell = fluid[x]
        fields[0, x] = open_cell * (provisional[0, x] - (p_east - p))
        fields[1, x] = open_cell * (provisional[1, x] - (p_north - p))
        fields[2, x] = open_cell * (provisional[2, x] - (p_upper - p) * inv_space)
        cells[x] = p
        part = parts_of(x)
        if part is not None:
            pairs = [(fields.at[:, part], updated.at[0:3, part]), (cells.at[part], pressure.at[part])]
            copies += loaded(pairs, sems.at[pl.ds(x // PART * 2, 2)])
    for copy in copies:
        copy.wait()


def shaped(*shape):
    return jax.ShapeDtypeStruct(shape, jnp.float32)


def call(kernel, out_shape, *operands, flops=0, vmem=12 * 1024 * 1024, **options):
    here = pl.BlockSpec(memory_space=pltpu.VMEM)
    options.setdefault("in_specs", [here] * len(operands))
    options.setdefault("out_specs", jax.tree.map(lambda _: here, out_shape))
    count = sum(int(np.prod(a.shape)) for a in operands) * 4
    return pl.pallas_call(
        kernel,
        out_shape=out_shape,
        name=kernel.__name__,
        compiler_params=pltpu.CompilerParams(vmem_limit_bytes=vmem),
        cost_estimate=pl.CostEstimate(flops=flops, bytes_accessed=count, transcendentals=0),
        **options,
    )(*operands)


def passed(block, axis, distance):
    count = lax.axis_size(axis)
    return lax.ppermute(block, axis, [((i - distance) % count, i) for i in range(count)])


def eigenvalues(frequency):
    return 2.0 - 2.0 * jnp.cos((2.0 * jnp.pi / LINE) * frequency.astype(jnp.float32))


def per_device(state, memory, level_steps, building_height):
    plane = shaped(5, TILE, LEVELS)
    edges = call(edges_kernel, [plane] * 4, state)
    west = passed(edges[1], "px", 1)
    east = passed(edges[0], "px", -1)
    south = passed(edges[3], "py", 1)
    north = passed(edges[2], "py", -1)

    steps = level_steps.reshape(1, LEVELS)
    own_y = lax.axis_index("px") * lax.axis_size("py") + lax.axis_index("py")
    shift = eigenvalues(jnp.arange(LINE, dtype=jnp.int32)) + eigenvalues(own_y)
    basis, after = jnp.asarray(BASIS), jnp.asarray(AFTER)
    vmem, hbm = pl.BlockSpec(memory_space=pltpu.VMEM), pl.BlockSpec(memory_space=pltpu.HBM)
    scratch = lambda *shape: pltpu.VMEM(shape, jnp.float32)
    sems = pltpu.SemaphoreType.DMA

    halos = (west, east, south, north)
    message = call(
        momentum_kernel,
        shaped(TILE, TILE, WIDE),
        state, memory, *halos, steps, building_height,
        flops=10**7,
        scratch_shapes=[scratch(3, TILE, TILE, LEVELS), scratch(TILE, TILE, LEVELS)],
    )
    provisional, updated, fluid = call(
        side_kernel,
        [
            shaped(3, TILE, TILE, LEVELS),
            shaped(5, TILE, TILE, LEVELS),
            shaped(TILE, TILE, LEVELS),
        ],
        state, memory, *halos, steps, building_height,
        flops=2 * 10**7,
        vmem=MOST_VMEM,
        in_specs=[hbm] * 6 + [vmem] * 2,
        out_specs=[hbm] * 3,
        scratch_shapes=[
            scratch(5, TILE, TILE, LEVELS),
            scratch(5, TILE, TILE, LEVELS),
            scratch(4, 5, TILE, LEVELS),
            scratch(TILE, TILE, LEVELS),
            scratch(5, TILE, TILE, LEVELS),
            sems((9,)),
        ],
    )
    lines = lax.all_to_all(message, "py", split_axis=0, concat_axis=0, tiled=True)
    spectrum = call(
        forward_y_kernel, shaped(LINE, 1, WIDE), lines.reshape(LINE, WIDE), basis, after
    )
    lines = lax.all_to_all(spectrum, ("px", "py"), split_axis=0, concat_axis=0, tiled=True)
    lines, provisional = lax.optimization_barrier((lines, provisional))
    solved = call(
        solve_kernel, shaped(LINE, 1, WIDE), lines, basis, after, steps, shift.reshape(1, LINE)
    )
    lines = lax.all_to_all(solved, ("px", "py"), split_axis=0, concat_axis=0, tiled=True)
    message = call(backward_y_kernel, shaped(LINE, WIDE), lines, basis, after)
    message = lax.all_to_all(
        message.reshape(TILE, TILE, WIDE), "py", split_axis=0, concat_axis=0, tiled=True
    )
    return call(
        correct_kernel,
        [shaped(5, TILE, TILE, LEVELS), shaped(TILE, TILE, LEVELS)],
        message, provisional, steps, fluid, updated,
        in_specs=[vmem] * 4 + [hbm],
        out_specs=[hbm] * 2,
        input_output_aliases={4: 0},
        scratch_shapes=[
            scratch(3, TILE, TILE, LEVELS), scratch(TILE, TILE, LEVELS), sems((2 * TILE // PART,))
        ],
    )


def solution(mesh):
    return jax.shard_map(
        per_device,
        mesh=mesh,
        in_specs=(P(None, "px", "py", None), P(None, "px", "py", None), P(), P("px", "py")),
        out_specs=(P(None, "px", "py", None), P("px", "py", None)),
        check_vma=False,
    )
```

time: 115 us -> 102 us (0.89)
  blocking collectives: 38.1 us -> 52.3 us
  local copies, waits for them, and re-layouts: 15.9 us -> 2.94 us
  waiting for transfers between devices: 17.5 us -> 12.1 us
  starting transfers between devices: 25.5 us -> 21.2 us
  other arithmetic: 2.36 us -> 0.06 us
  Pallas kernels: 14.2 us -> 12.1 us
    all_to_all x0 -> x1, blocking collectives: none -> 13.3 us  [per_device(): lax.all_to_all(message.reshape(TILE, TILE, WIDE), 'py', split_axis=0, con...]
    unnamed x54 -> x22, local copies, waits for them, and re-layouts: 15 us -> 2.94 us
    all_to_all x1 -> x0, waiting for transfers between devices: 5.55 us -> none  [per_device(): lax.all_to_all(message.reshape(TILE, TILE, WIDE), 'py', split_axis=0, con...]
    all_to_all x1 -> x0, starting transfers between devices: 4.19 us -> none  [per_device(): lax.all_to_all(message.reshape(TILE, TILE, WIDE), 'py', split_axis=0, con...]
    pallas_call x8 -> x7, Pallas kernels: 14.2 us -> 12.1 us  [call(): pl.pallas_call(kernel, out_shape=out_shape, name=kernel.__name__, compile...]
    ppermute x4, waiting for transfers between devices: 0.01 us -> 1.83 us  [passed(): lax.ppermute(block, axis, [((i - distance) % count, i) for i in range(cou...]
    all_to_all x1, waiting for transfers between devices: 11.9 us -> 10.3 us  [per_device(): lax.all_to_all(spectrum, ('px', 'py'), split_axis=0, concat_axis=0, tiled...]
    all_to_all x1, blocking collectives: 16.5 us -> 17.8 us  [per_device(): lax.all_to_all(message, 'py', split_axis=0, concat_axis=0, tiled=True)]
  transfers between devices with their start and end apart: 6 -> 5, of which waited for: 2 -> 3; matrix products, arithmetic and copies ran while one was open for 3% -> 0% of each run, Pallas kernels for 2% -> 3%
where the time goes in v2:
time: 102 us
  blocking collectives  52.3 us (51%)
  starting transfers between devices  21.2 us (21%)
  Pallas kernels  12.1 us (12%)
  waiting for transfers between devices  12.1 us (12%)
  local copies, waits for them, and re-layouts  2.94 us (3%)
    all_to_all x1, blocking collectives, per_device(): lax.all_to_all(solved, ('px', 'py'), split_axis=0, concat_axis=0, tiled=T...  21.3 us
    all_to_all x1, blocking collectives, per_device(): lax.all_to_all(message, 'py', split_axis=0, concat_axis=0, tiled=True)  17.8 us
    all_to_all x1, blocking collectives, per_device(): lax.all_to_all(message.reshape(TILE, TILE, WIDE), 'py', split_axis=0, con...  13.3 us
    pallas_call x7, Pallas kernels, call(): pl.pallas_call(kernel, out_shape=out_shape, name=kernel.__name__, compile...  12.1 us
    all_to_all x1, starting transfers between devices, per_device(): lax.all_to_all(spectrum, ('px', 'py'), split_axis=0, concat_axis=0, tiled...  11.4 us
    all_to_all x1, waiting for transfers between devices, per_device(): lax.all_to_all(spectrum, ('px', 'py'), split_axis=0, concat_axis=0, tiled...  10.3 us
    ppermute x4, starting transfers between devices, passed(): lax.ppermute(block, axis, [((i - distance) % count, i) for i in range(cou...  9.82 us
    unnamed x22, local copies, waits for them, and re-layouts  2.94 us
  transfers between devices with their start and end apart: 5, of which 3 were waited for; matrix products, arithmetic and copies ran while one was open for 0% of the time, Pallas kernels for 3%

profile of v2, /device:TPU:1, one launch (start us, length us, event | category | flops | bytes accessed | tf_op | source)
XLA Modules:
  0.0 101.6 jit_solution(16992892434058847902)
XLA Ops:
  0.6 0.0 copy-start
  0.6 1.3 %copy-done = f32[5,16,16,192]{3,2,1,0:T(8,128)S(1)} copy-done((f32[5,16,16,192]{3,2,1,0:T(8,128)S(1)}, f32[5,16,16,192]{3,2,1,0:T(8,128)}, u32[]{:S(2)}) %copy-start) | copy-done | bytes 983064
  2.0 0.1 edges_kernel.1
  2.0 4.2 %collective-permute-start = (f32[5,16,192]{2,1,0:T(8,128)S(1)}, f32[5,16,192]{2,1,0:T(8,128)S(1)}, u32[]{:S(2)}, u32[]{:S(2)}) collective-permute-start(f32[5,16,192]{2,1,0:T(8,128)S(1)} %get-tuple-element.11), channel_id=1, source_target_pairs={{240,0},{0,16},{16,32},{32,48},{48,64},{64,80},{80,96},{96,112},{1... | collective-permute-start | bytes 184328 | tf_op jit(solution)/shard_map/ppermute | solution.py:353
  6.3 0.3 collective-permute-start.2
  6.6 5.3 %collective-permute-start.3 = (f32[5,16,192]{2,1,0:T(8,128)S(1)}, f32[5,16,192]{2,1,0:T(8,128)S(1)}, u32[]{:S(2)}, u32[]{:S(2)}) collective-permute-start(f32[5,16,192]{2,1,0:T(8,128)S(1)} %get-tuple-element.14), channel_id=1, source_target_pairs={{1,0},{2,1},{3,2},{4,3},{5,4},{6,5},{7,6},{8,7},{9,8},{10,9},{11,1... | collective-permute-start | bytes 184328 | tf_op jit(solution)/shard_map/ppermute | solution.py:353
  11.9 0.4 collective-permute-done.1.east
  12.3 1.4 %collective-permute-done.2.south = f32[5,16,192]{2,1,0:T(8,128)S(1)} collective-permute-done((f32[5,16,192]{2,1,0:T(8,128)S(1)}, f32[5,16,192]{2,1,0:T(8,128)S(1)}, u32[]{:S(2)}, u32[]{:S(2)}) %collective-permute-start.2) | collective-permute-done | bytes 61472 | tf_op jit(solution)/shard_map/ppermute | solution.py:353
  13.7 0.0 copy-start.3
  13.7 0.0 copy-start.8
  13.7 1.8 %momentum_kernel.1 = f32[16,16,256]{2,1,0:T(8,128)S(1)} custom-call(f32[5,16,16,192]{3,2,1,0:T(8,128)S(1)} %copy-done, f32[5,16,16,192]{3,2,1,0:T(8,128)S(1)} %copy-done.2, f32[5,16,192]{2,1,0:T(8,128)S(1)} %collective-permute-done.west, f32[5,16,192]{2,1,0:T(8,128)S(1)} %collective-permute-done.1.east, f32[5,16,192]{2,1,0:T(8,128)S(1)} %collective-permute-done.2.south, ...), custom_call_target="tpu_custom_call" | custom-call | flops 10000000 | bytes 2213632 | tf_op jit(solution)/shard_map/momentum_kernel/pallas_call | solution.py:341
  15.6 17.8 %all_to_all.20 = f32[16,16,256]{2,1,0:T(8,128)S(1)} all-to-all(f32[16,16,256]{2,1,0:T(8,128)S(1)} %momentum_kernel.1), channel_id=1, replica_groups=mesh['px'=16,'py'=16] {'py'}, dimensions={0} | all-to-all | bytes 524288 | tf_op jit(solution)/shard_map/all_to_all | solution.py:405
  33.3 1.6 %forward_y_kernel.1 = f32[256,1,256]{2,1,0:T(1,128)} custom-call(f32[256,256]{1,0:T(8,128)S(1)} %bitcast.4, f32[256,256]{1,0:T(8,128)S(1)} %copy-done.3, f32[16,256]{1,0:T(8,128)S(1)} %copy-done.8), custom_call_target="tpu_custom_call" | custom-call | bytes 540672 | tf_op jit(solution)/shard_map/forward_y_kernel/pallas_call | solution.py:341
  34.9 11.4 %all-to-all-start.1 = ((f32[256,1,256]{2,1,0:T(1,128)}), f32[256,1,256]{2,1,0:T(1,128)S(1)}, u32[]{:S(2)}, u32[]{:S(2)}) async-start(f32[256,1,256]{2,1,0:T(1,128)} %forward_y_kernel.1), calls=%async_computation.1 | async-start | bytes 524288 | tf_op jit(solution)/shard_map/all_to_all | solution.py:409
  46.4 0.1 subtract_add_fusion.shift
  46.5 3.5 %side_kernel.1 = (f32[3,16,16,192]{3,2,1,0:T(8,128)S(1)}, f32[5,16,16,192]{3,2,1,0:T(8,128)}, f32[16,16,192]{2,1,0:T(8,128)S(1)}) custom-call(f32[5,16,16,192]{3,2,1,0:T(8,128)S(1)} %copy-done.1, f32[5,16,16,192]{3,2,1,0:T(8,128)S(1)} %copy-done.2, f32[5,16,192]{2,1,0:T(8,128)S(1)} %collective-permute-done.west, ...), custom_call_target="tpu_custom_call" | custom-call | flops 20000000 | bytes 2213632 | tf_op jit(solution)/shard_map/side_kernel/pallas_call | solution.py:341
  50.0 0.9 copy-done.4
  50.9 0.7 copy-done.6
  51.6 10.3 %all-to-all-done.1.lines = f32[256,1,256]{2,1,0:T(1,128)S(1)} async-done(((f32[256,1,256]{2,1,0:T(1,128)}), f32[256,1,256]{2,1,0:T(1,128)S(1)}, u32[]{:S(2)}, u32[]{:S(2)}) %all-to-all-start.1) | async-done | bytes 262176 | tf_op jit(solution)/shard_map/all_to_all | solution.py:409
  61.9 2.9 %solve_kernel.1 = f32[256,1,256]{2,1,0:T(1,128)S(1)} custom-call(f32[256,1,256]{2,1,0:T(1,128)S(1)} %all-to-all-done.1.lines, f32[256,256]{1,0:T(8,128)S(1)} %copy-done.3, f32[16,256]{1,0:T(8,128)S(1)} %copy-done.8, s32[1,192]{1,0:T(1,128)S(1)} %bitcast.7, f32[1,256]{1,0:T(1,128)S(1)} %subtract_add_fusion.shift), custom_call_target="tpu_custom_call" | custom-call | bytes 542464 | tf_op jit(solution)/shard_map/solve_kernel/pallas_call | solution.py:341
  64.8 21.3 %all_to_all.21.lines = f32[256,1,256]{2,1,0:T(1,128)S(1)} all-to-all(f32[256,1,256]{2,1,0:T(1,128)S(1)} %solve_kernel.1), channel_id=1, replica_groups=mesh['px'=16,'py'=16] {'px','py'}, dimensions={0} | all-to-all | bytes 524288 | tf_op jit(solution)/shard_map/all_to_all | solution.py:414
  86.1 0.8 backward_y_kernel.1
  86.9 13.3 %all_to_all.22.message = f32[16,16,256]{2,1,0:T(8,128)S(1)} all-to-all(f32[16,16,256]{2,1,0:T(8,128)S(1)} %bitcast.3), channel_id=1, replica_groups=mesh['px'=16,'py'=16] {'py'}, dimensions={0} | all-to-all | bytes 524288 | tf_op jit(solution)/shard_map/all_to_all | solution.py:416
  100.1 1.4 %correct_kernel.1 = (f32[5,16,16,192]{3,2,1,0:T(8,128)}, f32[16,16,192]{2,1,0:T(8,128)}) custom-call(f32[16,16,256]{2,1,0:T(8,128)S(1)} %all_to_all.22.message, f32[3,16,16,192]{3,2,1,0:T(8,128)S(1)} %copy-done.5, s32[1,192]{1,0:T(1,128)S(1)} %bitcast.8, f32[16,16,192]{2,1,0:T(8,128)S(1)} %copy-done.7, ...), custom_call_target="tpu_custom_call", output_to_operand_aliasing={{0}: (4, {})} | custom-call | bytes 2032384 | tf_op jit(solution)/shard_map/correct_kernel/pallas_call | solution.py:341
  (19 shorter events, 0.0 us)
Async XLA Ops:
  0.6 1.3 %copy-start = (f32[5,16,16,192]{3,2,1,0:T(8,128)S(1)}, f32[5,16,16,192]{3,2,1,0:T(8,128)}, u32[]{:S(2)}) copy-start(f32[5,16,16,192]{3,2,1,0:T(8,128)} %state.5) | copy-start | bytes 2949124
  1.9 11.8 %copy-start.2 = (f32[5,16,16,192]{3,2,1,0:T(8,128)S(1)}, f32[5,16,16,192]{3,2,1,0:T(8,128)}, u32[]{:S(2)}) copy-start(f32[5,16,16,192]{3,2,1,0:T(8,128)} %memory.3) | copy-start | bytes 2949124
  2.0 11.8 %copy-start.9 = (s32[16,16]{1,0:T(8,128)S(1)}, s32[16,16]{1,0:T(8,128)}, u32[]{:S(2)}) copy-start(s32[16,16]{1,0:T(8,128)} %height.3) | copy-start | bytes 3076
  2.0 11.8 %copy-start.10 = (s32[192]{0:T(256)S(1)}, s32[192]{0:T(256)}, u32[]{:S(2)}) copy-start(s32[192]{0:T(256)} %param.8) | copy-start | bytes 2308
  2.0 9.8 %collective-permute-start = (f32[5,16,192]{2,1,0:T(8,128)S(1)}, f32[5,16,192]{2,1,0:T(8,128)S(1)}, u32[]{:S(2)}, u32[]{:S(2)}) collective-permute-start(f32[5,16,192]{2,1,0:T(8,128)S(1)} %get-tuple-element.11), channel_id=1, source_target_pairs={{240,0},{0,16},{16,32},{32,48},{48,64},{64,80},{80,96},{96,112},{1... | collective-permute-start | bytes 184328 | tf_op jit(solution)/shard_map/ppermute | solution.py:353
  6.3 6.1 %collective-permute-start.1 = (f32[5,16,192]{2,1,0:T(8,128)S(1)}, f32[5,16,192]{2,1,0:T(8,128)S(1)}, u32[]{:S(2)}, u32[]{:S(2)}) collective-permute-start(f32[5,16,192]{2,1,0:T(8,128)S(1)} %get-tuple-element.12), channel_id=1, source_target_pairs={{16,0},{32,16},{48,32},{64,48},{80,64},{96,80},{112,96},{128,112},... | collective-permute-start | bytes 184328 | tf_op jit(solution)/shard_map/ppermute | solution.py:353
  6.3 7.4 %collective-permute-start.2 = (f32[5,16,192]{2,1,0:T(8,128)S(1)}, f32[5,16,192]{2,1,0:T(8,128)S(1)}, u32[]{:S(2)}, u32[]{:S(2)}) collective-permute-start(f32[5,16,192]{2,1,0:T(8,128)S(1)} %get-tuple-element.13), channel_id=1, source_target_pairs={{15,0},{0,1},{1,2},{2,3},{3,4},{4,5},{5,6},{6,7},{7,8},{8,9},{9,10... | collective-permute-start | bytes 184328 | tf_op jit(solution)/shard_map/ppermute | solution.py:353
  6.6 7.1 %collective-permute-start.3 = (f32[5,16,192]{2,1,0:T(8,128)S(1)}, f32[5,16,192]{2,1,0:T(8,128)S(1)}, u32[]{:S(2)}, u32[]{:S(2)}) collective-permute-start(f32[5,16,192]{2,1,0:T(8,128)S(1)} %get-tuple-element.14), channel_id=1, source_target_pairs={{1,0},{2,1},{3,2},{4,3},{5,4},{6,5},{7,6},{8,7},{9,8},{10,9},{11,1... | collective-permute-start | bytes 184328 | tf_op jit(solution)/shard_map/ppermute | solution.py:353
  13.7 19.6 %copy-start.3 = (f32[256,256]{1,0:T(8,128)S(1)}, f32[256,256]{1,0:T(8,128)}, u32[]{:S(2)}) copy-start(f32[256,256]{1,0:T(8,128)} %constant.19.clone.basis) | copy-start | bytes 786436
  13.7 19.6 %copy-start.8 = (f32[16,256]{1,0:T(8,128)S(1)}, f32[16,256]{1,0:T(8,128)}, u32[]{:S(2)}) copy-start(f32[16,256]{1,0:T(8,128)} %constant.20.clone.after) | copy-start | bytes 49156
  15.5 30.9 %copy-start.1 = (f32[5,16,16,192]{3,2,1,0:T(8,128)S(1)}, f32[5,16,16,192]{3,2,1,0:T(8,128)}, u32[]{:S(2)}) copy-start(f32[5,16,16,192]{3,2,1,0:T(8,128)} %state.5) | copy-start | bytes 2949124
  34.9 27.0 %all-to-all-start.1 = ((f32[256,1,256]{2,1,0:T(1,128)}), f32[256,1,256]{2,1,0:T(1,128)S(1)}, u32[]{:S(2)}, u32[]{:S(2)}) async-start(f32[256,1,256]{2,1,0:T(1,128)} %forward_y_kernel.1), calls=%async_computation.1 | async-start | bytes 524288 | tf_op jit(solution)/shard_map/all_to_all | solution.py:409
  50.0 0.9 copy-start.4
  50.9 0.7 copy-start.6
  61.9 38.2 %copy-start.5 = (f32[3,16,16,192]{3,2,1,0:T(8,128)S(1)}, f32[3,16,16,192]{3,2,1,0:T(8,128)}, u32[]{:S(2)}) copy-start(f32[3,16,16,192]{3,2,1,0:T(8,128)} %copy-done.4) | copy-start | bytes 1769476
  61.9 38.2 %copy-start.7 = (f32[16,16,192]{2,1,0:T(8,128)S(1)}, f32[16,16,192]{2,1,0:T(8,128)}, u32[]{:S(2)}) copy-start(f32[16,16,192]{2,1,0:T(8,128)} %copy-done.6) | copy-start | bytes 589828

commit v3 on v2

--- a/solution.py
+++ b/solution.py
@@ -21,7 +21,7 @@
 FIRST = 192
 SECOND = 208
 UNROLL = 3
-MOST_VMEM = 50331648
+MOST_VMEM = 48 * 1024 * 1024
 STRIDES = (1, 2, 4, 8, 16, 32, 64, 128)
 
 
@@ -73,6 +73,10 @@
     return jnp.concatenate(
         [jnp.broadcast_to(rows[b : b + 1], (TILE, rows.shape[1])) for b in range(TILE)], axis=0
     )
+
+
+def every_block(rows):
+    return jnp.concatenate([rows] * TILE, axis=0)
 
 
 def level_rows(level_steps):
@@ -175,15 +179,11 @@
     inv_thick = 1.0 / level_rows(level_steps)[0]
     zeros = jnp.zeros((TILE, WIDE - LEVELS), jnp.float32)
     last_u = jnp.concatenate([provisional[0, TILE - 1], zeros], axis=1)
-    u_packed = jnp.where(
-        chunk_mask((LINE, WIDE), "high"), jnp.concatenate([last_u] * TILE, axis=0), 0.0
-    )
-    v_rows = []
-    for x in range(TILE):
-        last_v = jnp.broadcast_to(provisional[1, x, TILE - 1 :], (TILE, LEVELS))
-        v_rows.append(jnp.concatenate([last_v, zeros], axis=1))
-    v_packed = jnp.where(chunk_mask((LINE, WIDE), "low"), jnp.concatenate(v_rows, axis=0), 0.0)
-    upper = picked(v_packed, pack_places(FIRST)) + picked(u_packed, pack_places(SECOND))
+    u_packed = jnp.where(chunk_mask((LINE, WIDE), "low"), each_block(last_u), 0.0)
+    last_v = jnp.concatenate([provisional[1, :, TILE - 1], zeros], axis=1)
+    v_packed = jnp.where(chunk_mask((LINE, WIDE), "high"), every_block(last_v), 0.0)
+    upper = picked(u_packed, pack_places(FIRST)) + picked(v_packed, pack_places(SECOND))
+    upper = upper.reshape(TILE, TILE, 128)
     for x in range(TILE):
         u = provisional[0, x]
         v = provisional[1, x]
@@ -191,11 +191,8 @@
         v_before = jnp.concatenate([jnp.zeros_like(v[:1]), v[:-1]], axis=0)
         diverge = (v - v_before) + (w - lanes_down(w)) * inv_thick
         diverge = diverge + (u - provisional[0, x - 1] if x else u)
-        message[x, :, :128] = diverge[:, :128]
-        message[x, :, 128:] = (
-            jnp.concatenate([diverge[:, 128:], zeros], axis=1)
-            + upper[x * TILE : (x + 1) * TILE]
-        )
+        message[:, x, :128] = diverge[:, :128]
+        message[:, x, 128:] = jnp.concatenate([diverge[:, 128:], zeros], axis=1) + upper[:, x]
 
 
 def loaded(pairs, sems):
@@ -205,10 +202,10 @@
     return copies
 
 
-def unpacked(values, first):
-    mask = chunk_mask((LINE, WIDE), "low")
+def unpacked(values, first, owner):
+    mask = chunk_mask((LINE, WIDE), owner)
     spread = jnp.where(mask, picked(values[:, 128:], unpack_places(first)), 0.0)
-    return spread.reshape(TILE, TILE, WIDE).sum(axis=1)
+    return spread.reshape(TILE, TILE, WIDE).sum(axis=1 if owner == "low" else 0)
 
 
 def repacked(rows, first):
@@ -216,9 +213,9 @@
     return picked(chunks, pack_places(first))
 
 
-def forward_y_kernel(lines, basis, after, spectrum):
+def forward_kernel(lines, basis, after, spectrum):
     values = lines[...]
-    extra = unpacked(values, FIRST)
+    extra = unpacked(values, FIRST, "low")
     total = product(basis[...], values) - product(after[...], extra, ((0,), (0,)))
     spectrum[:, 0, :] = total
 
@@ -248,15 +245,14 @@
 
 def side_kernel(
     state, memory, west, east, south, north, level_steps, height,
-    provisional, updated, fluid,
-    state_here, memory_here, halo_here, fluid_here, fields, sems,
+    provisional, updated, fluid_kept, state_here, memory_here, halo_here, fluid, fields, sems,
 ):
     halos = (west, east, south, north)
     pairs = [(state, state_here), (memory, memory_here)]
     pairs += [(halo, halo_here.at[i]) for i, halo in enumerate(halos)]
     arriving = loaded(pairs, sems)
-    fill_fluid(height, fluid_here)
-    leaving = loaded([(fluid_here, fluid)], sems.at[pl.ds(6, 1)])
+    fill_fluid(height, fluid)
+    leaving = loaded([(fluid, fluid_kept)], sems.at[pl.ds(6, 1)])
     for copy in arriving:
         copy.wait()
 
@@ -265,7 +261,7 @@
 
     advance_fields(
         (0, 1, 2, 3, 4), state_here, memory_here, *[halo_here.at[i] for i in range(4)],
-        level_steps, fluid_here, store,
+        level_steps, fluid, store,
     )
     pairs = [(fields.at[0:3], provisional), (fields.at[3:5], updated.at[3:5])]
     leaving += loaded(pairs, sems.at[pl.ds(7, 2)])
@@ -282,7 +278,7 @@
     between = column_of(jnp.where(level < LEVELS - 1, -inv_space, 0.0))
     coupling = jnp.broadcast_to(between, (LEVELS, LINE))
     values = lines[:, 0, :]
-    extra = unpacked(values, SECOND)
+    extra = unpacked(values, SECOND, "low")
     main = product(values, basis[...], ((0,), (0,)))
     fix = product(extra, after[...], ((0,), (0,)))
     right = thick * (fix[:LEVELS] - main[:LEVELS])
@@ -294,7 +290,7 @@
     result[:, 0, 128:] = back[:, 128:] + repacked(beside, FIRST)
 
 
-def backward_y_kernel(lines, basis, after, message):
+def backward_kernel(lines, basis, after, message):
     values = lines[:, 0, :]
     back = product(basis[...], values)
     beside = product(after[...], values)
@@ -303,17 +299,16 @@
 
 
 def correct_kernel(
-    message, provisional, level_steps, fluid, updated_in, updated, pressure, fields, cells, sems
+    message, provisional, level_steps, fluid, kept, updated, pressure, fields, cells, sems
 ):
     copies = []
     inv_space = 1.0 / level_rows(level_steps)[1]
-    packed = message[:, :, 128:].reshape(LINE, 128)
-    east = jnp.where(chunk_mask((LINE, WIDE), "high"), picked(packed, unpack_places(FIRST)), 0.0)
-    east = east.reshape(TILE, TILE, WIDE).sum(axis=0)[:, :LEVELS]
-    north = unpacked(message[...].reshape(LINE, WIDE), SECOND)[:, :LEVELS]
+    lines = message[...].reshape(LINE, WIDE)
+    north = unpacked(lines, FIRST, "high")[:, :LEVELS]
+    east = unpacked(lines, SECOND, "low")[:, :LEVELS]
     for x in range(TILE):
-        p = message[x, :, :LEVELS]
-        p_east = message[x + 1, :, :LEVELS] if x < TILE - 1 else east
+        p = message[:, x, :LEVELS]
+        p_east = message[:, x + 1, :LEVELS] if x < TILE - 1 else east
         p_north = jnp.concatenate([p[1:], north[x : x + 1]], axis=0)
         p_upper = jnp.concatenate([p[:, 1:], jnp.zeros_like(p[:, :1])], axis=1)
         open_cell = fluid[x]
@@ -366,8 +361,8 @@
     north = passed(edges[2], "py", -1)
 
     steps = level_steps.reshape(1, LEVELS)
-    own_y = lax.axis_index("px") * lax.axis_size("py") + lax.axis_index("py")
-    shift = eigenvalues(jnp.arange(LINE, dtype=jnp.int32)) + eigenvalues(own_y)
+    own_x = lax.axis_index("py") * lax.axis_size("px") + lax.axis_index("px")
+    shift = eigenvalues(jnp.arange(LINE, dtype=jnp.int32)) + eigenvalues(own_x)
     basis, after = jnp.asarray(BASIS), jnp.asarray(AFTER)
     vmem, hbm = pl.BlockSpec(memory_space=pltpu.VMEM), pl.BlockSpec(memory_space=pltpu.HBM)
     scratch = lambda *shape: pltpu.VMEM(shape, jnp.float32)
@@ -402,19 +397,19 @@
             sems((9,)),
         ],
     )
-    lines = lax.all_to_all(message, "py", split_axis=0, concat_axis=0, tiled=True)
+    lines = lax.all_to_all(message, "px", split_axis=0, concat_axis=0, tiled=True)
     spectrum = call(
-        forward_y_kernel, shaped(LINE, 1, WIDE), lines.reshape(LINE, WIDE), basis, after
-    )
-    lines = lax.all_to_all(spectrum, ("px", "py"), split_axis=0, concat_axis=0, tiled=True)
+        forward_kernel, shaped(LINE, 1, WIDE), lines.reshape(LINE, WIDE), basis, after
+    )
+    lines = lax.all_to_all(spectrum, ("py", "px"), split_axis=0, concat_axis=0, tiled=True)
     lines, provisional = lax.optimization_barrier((lines, provisional))
     solved = call(
         solve_kernel, shaped(LINE, 1, WIDE), lines, basis, after, steps, shift.reshape(1, LINE)
     )
-    lines = lax.all_to_all(solved, ("px", "py"), split_axis=0, concat_axis=0, tiled=True)
-    message = call(backward_y_kernel, shaped(LINE, WIDE), lines, basis, after)
+    lines = lax.all_to_all(solved, ("py", "px"), split_axis=0, concat_axis=0, tiled=True)
+    message = call(backward_kernel, shaped(LINE, WIDE), lines, basis, after)
     message = lax.all_to_all(
-        message.reshape(TILE, TILE, WIDE), "py", split_axis=0, concat_axis=0, tiled=True
+        message.reshape(TILE, TILE, WIDE), "px", split_axis=0, concat_axis=0, tiled=True
     )
     return call(
         correct_kernel,

time: 102 us -> 97.6 us (0.957)
  starting transfers between devices: 21.2 us -> 18.6 us
  blocking collectives: 52.3 us -> 49.8 us
    all_to_all x1, starting transfers between devices: 11.4 us -> 8.83 us  [per_device(): lax.all_to_all(spectrum, ('py', 'px'), split_axis=0, concat_axis=0, tiled...]
    all_to_all x3, blocking collectives: 52.3 us -> 49.8 us  [the longest x1 20.4 us: per_device(): lax.all_to_all(solved, ('py', 'px'), split_axis=0, concat_axis=0, tiled=T...]
  transfers between devices with their start and end apart: 5 -> 5, of which waited for: 3 -> 3; matrix products, arithmetic and copies ran while one was open for 0% -> 0% of each run, Pallas kernels for 3% -> 4%
where the time goes in v3:
time: 97.6 us; the launch traced here: 97.3 us
  blocking collectives  49.8 us (51%)
  starting transfers between devices  18.6 us (19%)
  Pallas kernels  12.6 us (13%)
  waiting for transfers between devices  12.4 us (13%)
  local copies, waits for them, and re-layouts  2.94 us (3%)
    all_to_all x1, blocking collectives, per_device(): lax.all_to_all(solved, ('py', 'px'), split_axis=0, concat_axis=0, tiled=T...  20.4 us
    all_to_all x1, blocking collectives, per_device(): lax.all_to_all(message, 'px', split_axis=0, concat_axis=0, tiled=True)  17.6 us
    pallas_call x7, Pallas kernels, call(): pl.pallas_call(kernel, out_shape=out_shape, name=kernel.__name__, compile...  12.6 us
    all_to_all x1, blocking collectives, per_device(): lax.all_to_all(message.reshape(TILE, TILE, WIDE), 'px', split_axis=0, con...  11.8 us
    all_to_all x1, waiting for transfers between devices, per_device(): lax.all_to_all(spectrum, ('py', 'px'), split_axis=0, concat_axis=0, tiled...  10.6 us
    ppermute x4, starting transfers between devices, passed(): lax.ppermute(block, axis, [((i - distance) % count, i) for i in range(cou...  9.82 us
    all_to_all x1, starting transfers between devices, per_device(): lax.all_to_all(spectrum, ('py', 'px'), split_axis=0, concat_axis=0, tiled...  8.83 us
    unnamed x22, local copies, waits for them, and re-layouts  2.94 us
  transfers between devices with their start and end apart: 5, of which 3 were waited for; matrix products, arithmetic and copies ran while one was open for 0% of the time, Pallas kernels for 4%

profile of v3, /device:TPU:1, one launch (start us, length us, event | category | flops | bytes accessed | tf_op | source)
XLA Modules:
  0.0 97.3 jit_solution(8713692111224922053)
XLA Ops:
  0.6 1.3 %copy-done = f32[5,16,16,192]{3,2,1,0:T(8,128)S(1)} copy-done((f32[5,16,16,192]{3,2,1,0:T(8,128)S(1)}, f32[5,16,16,192]{3,2,1,0:T(8,128)}, u32[]{:S(2)}) %copy-start) | copy-done | bytes 983064
  2.0 0.1 edges_kernel.1
  2.0 4.2 %collective-permute-start = (f32[5,16,192]{2,1,0:T(8,128)S(1)}, f32[5,16,192]{2,1,0:T(8,128)S(1)}, u32[]{:S(2)}, u32[]{:S(2)}) collective-permute-start(f32[5,16,192]{2,1,0:T(8,128)S(1)} %get-tuple-element.11), channel_id=1, source_target_pairs={{240,0},{0,16},{16,32},{32,48},{48,64},{64,80},{80,96},{96,112},{1... | collective-permute-start | bytes 184328 | tf_op jit(solution)/shard_map/ppermute | solution.py:348
  6.3 0.3 collective-permute-start.2
  6.6 5.3 %collective-permute-start.3 = (f32[5,16,192]{2,1,0:T(8,128)S(1)}, f32[5,16,192]{2,1,0:T(8,128)S(1)}, u32[]{:S(2)}, u32[]{:S(2)}) collective-permute-start(f32[5,16,192]{2,1,0:T(8,128)S(1)} %get-tuple-element.14), channel_id=1, source_target_pairs={{1,0},{2,1},{3,2},{4,3},{5,4},{6,5},{7,6},{8,7},{9,8},{10,9},{11,1... | collective-permute-start | bytes 184328 | tf_op jit(solution)/shard_map/ppermute | solution.py:348
  11.9 0.4 collective-permute-done.1.east
  12.3 1.4 %collective-permute-done.2.south = f32[5,16,192]{2,1,0:T(8,128)S(1)} collective-permute-done((f32[5,16,192]{2,1,0:T(8,128)S(1)}, f32[5,16,192]{2,1,0:T(8,128)S(1)}, u32[]{:S(2)}, u32[]{:S(2)}) %collective-permute-start.2) | collective-permute-done | bytes 61472 | tf_op jit(solution)/shard_map/ppermute | solution.py:348
  13.7 0.0 copy-start.3
  13.7 0.0 copy-start.8
  13.7 2.0 %momentum_kernel.1 = f32[16,16,256]{2,1,0:T(8,128)S(1)} custom-call(f32[5,16,16,192]{3,2,1,0:T(8,128)S(1)} %copy-done, f32[5,16,16,192]{3,2,1,0:T(8,128)S(1)} %copy-done.2, f32[5,16,192]{2,1,0:T(8,128)S(1)} %collective-permute-done.west, f32[5,16,192]{2,1,0:T(8,128)S(1)} %collective-permute-done.1.east, f32[5,16,192]{2,1,0:T(8,128)S(1)} %collective-permute-done.2.south, ...), custom_call_target="tpu_custom_call" | custom-call | flops 10000000 | bytes 2213632 | tf_op jit(solution)/shard_map/momentum_kernel/pallas_call | solution.py:336
  15.8 0.0 copy-start.1
  15.8 17.6 %all_to_all.20 = f32[16,16,256]{2,1,0:T(8,128)S(1)} all-to-all(f32[16,16,256]{2,1,0:T(8,128)S(1)} %momentum_kernel.1), channel_id=1, replica_groups=mesh['px'=16,'py'=16] {'px'}, dimensions={0} | all-to-all | bytes 524288 | tf_op jit(solution)/shard_map/all_to_all | solution.py:400
  33.4 1.6 %forward_kernel.1 = f32[256,1,256]{2,1,0:T(1,128)} custom-call(f32[256,256]{1,0:T(8,128)S(1)} %bitcast.4, f32[256,256]{1,0:T(8,128)S(1)} %copy-done.3, f32[16,256]{1,0:T(8,128)S(1)} %copy-done.8), custom_call_target="tpu_custom_call" | custom-call | bytes 540672 | tf_op jit(solution)/shard_map/forward_kernel/pallas_call | solution.py:336
  35.0 8.8 %all-to-all-start.1 = ((f32[256,1,256]{2,1,0:T(1,128)}), f32[256,1,256]{2,1,0:T(1,128)S(1)}, u32[]{:S(2)}, u32[]{:S(2)}) async-start(f32[256,1,256]{2,1,0:T(1,128)} %forward_kernel.1), calls=%async_computation.1 | async-start | bytes 524288 | tf_op jit(solution)/shard_map/all_to_all | solution.py:404
  43.9 0.1 subtract_add_fusion.shift
  44.0 3.5 %side_kernel.1 = (f32[3,16,16,192]{3,2,1,0:T(8,128)S(1)}, f32[5,16,16,192]{3,2,1,0:T(8,128)}, f32[16,16,192]{2,1,0:T(8,128)S(1)}) custom-call(f32[5,16,16,192]{3,2,1,0:T(8,128)S(1)} %copy-done.1, f32[5,16,16,192]{3,2,1,0:T(8,128)S(1)} %copy-done.2, f32[5,16,192]{2,1,0:T(8,128)S(1)} %collective-permute-done.west, ...), custom_call_target="tpu_custom_call" | custom-call | flops 20000000 | bytes 2213632 | tf_op jit(solution)/shard_map/side_kernel/pallas_call | solution.py:336
  47.5 0.9 copy-done.4
  48.4 0.7 copy-done.6
  49.1 10.6 %all-to-all-done.1.lines = f32[256,1,256]{2,1,0:T(1,128)S(1)} async-done(((f32[256,1,256]{2,1,0:T(1,128)}), f32[256,1,256]{2,1,0:T(1,128)S(1)}, u32[]{:S(2)}, u32[]{:S(2)}) %all-to-all-start.1) | async-done | bytes 262176 | tf_op jit(solution)/shard_map/all_to_all | solution.py:404
  59.7 2.9 %solve_kernel.1 = f32[256,1,256]{2,1,0:T(1,128)S(1)} custom-call(f32[256,1,256]{2,1,0:T(1,128)S(1)} %all-to-all-done.1.lines, f32[256,256]{1,0:T(8,128)S(1)} %copy-done.3, f32[16,256]{1,0:T(8,128)S(1)} %copy-done.8, s32[1,192]{1,0:T(1,128)S(1)} %bitcast.7, f32[1,256]{1,0:T(1,128)S(1)} %subtract_add_fusion.shift), custom_call_target="tpu_custom_call" | custom-call | bytes 542464 | tf_op jit(solution)/shard_map/solve_kernel/pallas_call | solution.py:336
  62.6 20.4 %all_to_all.21.lines = f32[256,1,256]{2,1,0:T(1,128)S(1)} all-to-all(f32[256,1,256]{2,1,0:T(1,128)S(1)} %solve_kernel.1), channel_id=1, replica_groups=mesh['px'=16,'py'=16] {'py','px'}, dimensions={0} | all-to-all | bytes 524288 | tf_op jit(solution)/shard_map/all_to_all | solution.py:409
  83.0 0.8 backward_kernel.1
  83.8 11.8 %all_to_all.22.message = f32[16,16,256]{2,1,0:T(8,128)S(1)} all-to-all(f32[16,16,256]{2,1,0:T(8,128)S(1)} %bitcast.3), channel_id=1, replica_groups=mesh['px'=16,'py'=16] {'px'}, dimensions={0} | all-to-all | bytes 524288 | tf_op jit(solution)/shard_map/all_to_all | solution.py:411
  95.6 1.7 %correct_kernel.1 = (f32[5,16,16,192]{3,2,1,0:T(8,128)}, f32[16,16,192]{2,1,0:T(8,128)}) custom-call(f32[16,16,256]{2,1,0:T(8,128)S(1)} %all_to_all.22.message, f32[3,16,16,192]{3,2,1,0:T(8,128)S(1)} %copy-done.5, s32[1,192]{1,0:T(1,128)S(1)} %bitcast.8, f32[16,16,192]{2,1,0:T(8,128)S(1)} %copy-done.7, ...), custom_call_target="tpu_custom_call", output_to_operand_aliasing={{0}: (4, {})} | custom-call | bytes 2032384 | tf_op jit(solution)/shard_map/correct_kernel/pallas_call | solution.py:336
  (19 shorter events, 0.0 us)
Async XLA Ops:
  0.6 1.3 %copy-start = (f32[5,16,16,192]{3,2,1,0:T(8,128)S(1)}, f32[5,16,16,192]{3,2,1,0:T(8,128)}, u32[]{:S(2)}) copy-start(f32[5,16,16,192]{3,2,1,0:T(8,128)} %state.5) | copy-start | bytes 2949124
  1.9 11.8 %copy-start.2 = (f32[5,16,16,192]{3,2,1,0:T(8,128)S(1)}, f32[5,16,16,192]{3,2,1,0:T(8,128)}, u32[]{:S(2)}) copy-start(f32[5,16,16,192]{3,2,1,0:T(8,128)} %memory.3) | copy-start | bytes 2949124
  2.0 11.8 %copy-start.9 = (s32[16,16]{1,0:T(8,128)S(1)}, s32[16,16]{1,0:T(8,128)}, u32[]{:S(2)}) copy-start(s32[16,16]{1,0:T(8,128)} %height.3) | copy-start | bytes 3076
  2.0 11.8 %copy-start.10 = (s32[192]{0:T(256)S(1)}, s32[192]{0:T(256)}, u32[]{:S(2)}) copy-start(s32[192]{0:T(256)} %param.8) | copy-start | bytes 2308
  2.0 9.8 %collective-permute-start = (f32[5,16,192]{2,1,0:T(8,128)S(1)}, f32[5,16,192]{2,1,0:T(8,128)S(1)}, u32[]{:S(2)}, u32[]{:S(2)}) collective-permute-start(f32[5,16,192]{2,1,0:T(8,128)S(1)} %get-tuple-element.11), channel_id=1, source_target_pairs={{240,0},{0,16},{16,32},{32,48},{48,64},{64,80},{80,96},{96,112},{1... | collective-permute-start | bytes 184328 | tf_op jit(solution)/shard_map/ppermute | solution.py:348
  6.3 6.1 %collective-permute-start.1 = (f32[5,16,192]{2,1,0:T(8,128)S(1)}, f32[5,16,192]{2,1,0:T(8,128)S(1)}, u32[]{:S(2)}, u32[]{:S(2)}) collective-permute-start(f32[5,16,192]{2,1,0:T(8,128)S(1)} %get-tuple-element.12), channel_id=1, source_target_pairs={{16,0},{32,16},{48,32},{64,48},{80,64},{96,80},{112,96},{128,112},... | collective-permute-start | bytes 184328 | tf_op jit(solution)/shard_map/ppermute | solution.py:348
  6.3 7.4 %collective-permute-start.2 = (f32[5,16,192]{2,1,0:T(8,128)S(1)}, f32[5,16,192]{2,1,0:T(8,128)S(1)}, u32[]{:S(2)}, u32[]{:S(2)}) collective-permute-start(f32[5,16,192]{2,1,0:T(8,128)S(1)} %get-tuple-element.13), channel_id=1, source_target_pairs={{15,0},{0,1},{1,2},{2,3},{3,4},{4,5},{5,6},{6,7},{7,8},{8,9},{9,10... | collective-permute-start | bytes 184328 | tf_op jit(solution)/shard_map/ppermute | solution.py:348
  6.6 7.1 %collective-permute-start.3 = (f32[5,16,192]{2,1,0:T(8,128)S(1)}, f32[5,16,192]{2,1,0:T(8,128)S(1)}, u32[]{:S(2)}, u32[]{:S(2)}) collective-permute-start(f32[5,16,192]{2,1,0:T(8,128)S(1)} %get-tuple-element.14), channel_id=1, source_target_pairs={{1,0},{2,1},{3,2},{4,3},{5,4},{6,5},{7,6},{8,7},{9,8},{10,9},{11,1... | collective-permute-start | bytes 184328 | tf_op jit(solution)/shard_map/ppermute | solution.py:348
  13.7 19.7 %copy-start.3 = (f32[256,256]{1,0:T(8,128)S(1)}, f32[256,256]{1,0:T(8,128)}, u32[]{:S(2)}) copy-start(f32[256,256]{1,0:T(8,128)} %constant.19.clone.basis) | copy-start | bytes 786436
  13.7 19.7 %copy-start.8 = (f32[16,256]{1,0:T(8,128)S(1)}, f32[16,256]{1,0:T(8,128)}, u32[]{:S(2)}) copy-start(f32[16,256]{1,0:T(8,128)} %constant.20.clone.after) | copy-start | bytes 49156
  15.8 28.2 %copy-start.1 = (f32[5,16,16,192]{3,2,1,0:T(8,128)S(1)}, f32[5,16,16,192]{3,2,1,0:T(8,128)}, u32[]{:S(2)}) copy-start(f32[5,16,16,192]{3,2,1,0:T(8,128)} %state.5) | copy-start | bytes 2949124
  35.0 24.7 %all-to-all-start.1 = ((f32[256,1,256]{2,1,0:T(1,128)}), f32[256,1,256]{2,1,0:T(1,128)S(1)}, u32[]{:S(2)}, u32[]{:S(2)}) async-start(f32[256,1,256]{2,1,0:T(1,128)} %forward_kernel.1), calls=%async_computation.1 | async-start | bytes 524288 | tf_op jit(solution)/shard_map/all_to_all | solution.py:404
  47.5 0.9 copy-start.4
  48.4 0.7 copy-start.6
  59.7 35.9 %copy-start.5 = (f32[3,16,16,192]{3,2,1,0:T(8,128)S(1)}, f32[3,16,16,192]{3,2,1,0:T(8,128)}, u32[]{:S(2)}) copy-start(f32[3,16,16,192]{3,2,1,0:T(8,128)} %copy-done.4) | copy-start | bytes 1769476
  59.7 35.9 %copy-start.7 = (f32[16,16,192]{2,1,0:T(8,128)S(1)}, f32[16,16,192]{2,1,0:T(8,128)}, u32[]{:S(2)}) copy-start(f32[16,16,192]{2,1,0:T(8,128)} %copy-done.6) | copy-start | bytes 589828

commit v4 on v3

--- a/solution.py
+++ b/solution.py
@@ -107,13 +107,17 @@
     north[...] = state[:, :, TILE - 1]
 
 
-def advance_fields(fields, state, memory, west, east, south, north, level_steps, fluid, store):
+def faces(s, e, u):
+    return e * (DIFFUSION - 0.5 * u) - s * (DIFFUSION + 0.5 * u)
+
+
+def advance_fields(fields, state, memory, halos, level_steps, fluid, store):
     thickness, spacing = level_rows(level_steps)
     inv_thick = 1.0 / thickness
     inv_space = 1.0 / spacing
-
-    def x_faces(s, e, u):
-        return e * (DIFFUSION - 0.5 * u) - s * (DIFFUSION + 0.5 * u)
+    nothing = jnp.zeros((TILE, LEVELS), jnp.float32)
+    if halos:
+        west, east, south, north = halos
 
     def plane(x, before, east_of):
         u = state[0, x]
@@ -122,30 +126,34 @@
         u_to, u_from = DIFFUSION - 0.5 * u, DIFFUSION + 0.5 * u
         v_to, v_from = DIFFUSION - 0.5 * v, DIFFUSION + 0.5 * v
         w_to, w_from = DIFFUSION * inv_space - 0.5 * w, DIFFUSION * inv_space + 0.5 * w
-        v_south = south[1, pl.ds(x, 1)]
         factor = (RK_STEP * TIME_STEP) * fluid[x]
-        faces = []
+        after = []
         for i, f in enumerate(fields):
             s = state[f, x]
-            x_face = east_of(f) * u_to - s * u_from
-            upper_y = jnp.concatenate([s[1:], north[f, pl.ds(x, 1)]], axis=0)
-            y_face = upper_y * v_to - s * v_from
-            first_y = x_faces(south[f, pl.ds(x, 1)], s[:1], v_south)
+            x_face = east_of(f) * u_to - s * u_from if east_of else nothing
+            last_y, first_y = nothing[:1], nothing[:1]
+            if halos:
+                last_y = faces(s[TILE - 1 :], north[f, pl.ds(x, 1)], v[TILE - 1 :])
+                first_y = faces(south[f, pl.ds(x, 1)], s[:1], south[1, pl.ds(x, 1)])
+            y_face = jnp.concatenate([s[1:], s[:1]], axis=0) * v_to - s * v_from
+            y_above = jnp.concatenate([y_face[:-1], last_y], axis=0)
             y_below = jnp.concatenate([first_y, y_face[:-1]], axis=0)
             z_face = lanes_up(s) * w_to - s * w_from
-            change = (x_face - before[i]) + (y_face - y_below)
+            change = (x_face - before[i]) + (y_above - y_below)
             change = change + (z_face - lanes_down(z_face)) * inv_thick
             if f == 2:
                 change = change + BUOYANCY * state[3, x]
-            faces.append(x_face)
+            after.append(x_face)
             store(f, x, s + (RK_STEP * RK_KEEP) * memory[f, x] + factor * change)
-        return tuple(faces)
-
-    before = tuple(x_faces(west[f], state[f, 0], west[0]) for f in fields)
+        return tuple(after)
+
+    before = tuple(
+        faces(west[f], state[f, 0], west[0]) if halos else nothing for f in fields
+    )
     before = lax.fori_loop(
         0, TILE - 1, lambda x, b: plane(x, b, lambda f: state[f, x + 1]), before, unroll=UNROLL
     )
-    plane(TILE - 1, before, lambda f: east[f])
+    plane(TILE - 1, before, (lambda f: east[f]) if halos else None)
 
 
 PART = 4
@@ -165,17 +173,29 @@
         fluid[x] = jnp.where(level >= bottom[x * TILE : (x + 1) * TILE], 1.0, 0.0)
 
 
-def momentum_kernel(
-    state, memory, west, east, south, north, level_steps, height, message, provisional, fluid
-):
+def interior_kernel(state, memory, level_steps, height, provisional, fluid):
     fill_fluid(height, fluid)
 
     def store(f, x, value):
         provisional[f, x] = value
 
-    advance_fields(
-        (0, 1, 2), state, memory, west, east, south, north, level_steps, fluid, store
-    )
+    advance_fields((0, 1, 2), state, memory, None, level_steps, fluid, store)
+
+
+def momentum_kernel(
+    state, inner, fluid, west, east, south, north, level_steps, message, provisional
+):
+    provisional[...] = inner[...]
+    last, factor = TILE - 1, RK_STEP * TIME_STEP
+    for f in range(3):
+        provisional[f, 0] -= factor * fluid[0] * faces(west[f], state[f, 0], west[0])
+        provisional[f, last] += factor * fluid[last] * faces(
+            state[f, last], east[f], state[0, last]
+        )
+        provisional[f, :, 0] -= factor * fluid[:, 0] * faces(south[f], state[f, :, 0], south[1])
+        provisional[f, :, last] += factor * fluid[:, last] * faces(
+            state[f, :, last], north[f], state[1, :, last]
+        )
     inv_thick = 1.0 / level_rows(level_steps)[0]
     zeros = jnp.zeros((TILE, WIDE - LEVELS), jnp.float32)
     last_u = jnp.concatenate([provisional[0, TILE - 1], zeros], axis=1)
@@ -260,7 +280,7 @@
         fields[f, x] = value
 
     advance_fields(
-        (0, 1, 2, 3, 4), state_here, memory_here, *[halo_here.at[i] for i in range(4)],
+        (0, 1, 2, 3, 4), state_here, memory_here, [halo_here.at[i] for i in range(4)],
         level_steps, fluid, store,
     )
     pairs = [(fields.at[0:3], provisional), (fields.at[3:5], updated.at[3:5])]
@@ -369,12 +389,18 @@
     sems = pltpu.SemaphoreType.DMA
 
     halos = (west, east, south, north)
+    inner, fluid = call(
+        interior_kernel,
+        [shaped(3, TILE, TILE, LEVELS), shaped(TILE, TILE, LEVELS)],
+        state, memory, steps, building_height,
+        flops=10**7,
+    )
     message = call(
         momentum_kernel,
         shaped(TILE, TILE, WIDE),
-        state, memory, *halos, steps, building_height,
+        state, inner, fluid, *halos, steps,
         flops=10**7,
-        scratch_shapes=[scratch(3, TILE, TILE, LEVELS), scratch(TILE, TILE, LEVELS)],
+        scratch_shapes=[scratch(3, TILE, TILE, LEVELS)],
     )
     provisional, updated, fluid = call(
         side_kernel,

time: 97.6 us -> 96.5 us (0.989)
  waiting for transfers between devices: 12.4 us -> 10.9 us
    ppermute x4, waiting for transfers between devices: 1.83 us -> 0.45 us  [passed(): lax.ppermute(block, axis, [((i - distance) % count, i) for i in range(cou...]
    pallas_call x7 -> x8, Pallas kernels: 12.6 us -> 13.1 us  [call(): pl.pallas_call(kernel, out_shape=out_shape, name=kernel.__name__, compile...]
  transfers between devices with their start and end apart: 5 -> 5, of which waited for: 3 -> 2; matrix products, arithmetic and copies ran while one was open for 0% -> 0% of each run, Pallas kernels for 4% -> 5%
where the time goes in v4:
time: 96.5 us; the launch traced here: 96.2 us
  blocking collectives  49.8 us (52%)
  starting transfers between devices  18.7 us (19%)
  Pallas kernels  13.1 us (14%)
  waiting for transfers between devices  10.9 us (11%)
  local copies, waits for them, and re-layouts  2.92 us (3%)
    all_to_all x1, blocking collectives, per_device(): lax.all_to_all(solved, ('py', 'px'), split_axis=0, concat_axis=0, tiled=T...  20.4 us
    all_to_all x1, blocking collectives, per_device(): lax.all_to_all(message, 'px', split_axis=0, concat_axis=0, tiled=True)  17.6 us
    pallas_call x8, Pallas kernels, call(): pl.pallas_call(kernel, out_shape=out_shape, name=kernel.__name__, compile...  13.1 us
    all_to_all x1, blocking collectives, per_device(): lax.all_to_all(message.reshape(TILE, TILE, WIDE), 'px', split_axis=0, con...  11.8 us
    all_to_all x1, waiting for transfers between devices, per_device(): lax.all_to_all(spectrum, ('py', 'px'), split_axis=0, concat_axis=0, tiled...  10.5 us
    ppermute x4, starting transfers between devices, passed(): lax.ppermute(block, axis, [((i - distance) % count, i) for i in range(cou...  9.82 us
    all_to_all x1, starting transfers between devices, per_device(): lax.all_to_all(spectrum, ('py', 'px'), split_axis=0, concat_axis=0, tiled...  8.83 us
    unnamed x22, local copies, waits for them, and re-layouts  2.92 us
  transfers between devices with their start and end apart: 5, of which 2 were waited for; matrix products, arithmetic and copies ran while one was open for 0% of the time, Pallas kernels for 5%

profile of v4, /device:TPU:1, one launch (start us, length us, event | category | flops | bytes accessed | tf_op | source)
XLA Modules:
  0.0 96.2 jit_solution(8447963521677477864)
XLA Ops:
  0.6 0.0 copy-start
  0.6 1.3 %copy-done = f32[5,16,16,192]{3,2,1,0:T(8,128)S(1)} copy-done((f32[5,16,16,192]{3,2,1,0:T(8,128)S(1)}, f32[5,16,16,192]{3,2,1,0:T(8,128)}, u32[]{:S(2)}) %copy-start) | copy-done | bytes 983064
  2.0 0.1 edges_kernel.1
  2.0 4.2 %collective-permute-start = (f32[5,16,192]{2,1,0:T(8,128)S(1)}, f32[5,16,192]{2,1,0:T(8,128)S(1)}, u32[]{:S(2)}, u32[]{:S(2)}) collective-permute-start(f32[5,16,192]{2,1,0:T(8,128)S(1)} %get-tuple-element.15), channel_id=1, source_target_pairs={{240,0},{0,16},{16,32},{32,48},{48,64},{64,80},{80,96},{96,112},{1... | collective-permute-start | bytes 184328 | tf_op jit(solution)/shard_map/ppermute | solution.py:368
  6.3 0.0 collective-permute-start.1
  6.3 0.3 collective-permute-start.2
  6.6 5.3 %collective-permute-start.3 = (f32[5,16,192]{2,1,0:T(8,128)S(1)}, f32[5,16,192]{2,1,0:T(8,128)S(1)}, u32[]{:S(2)}, u32[]{:S(2)}) collective-permute-start(f32[5,16,192]{2,1,0:T(8,128)S(1)} %get-tuple-element.18), channel_id=1, source_target_pairs={{1,0},{2,1},{3,2},{4,3},{5,4},{6,5},{7,6},{8,7},{9,8},{10,9},{11,1... | collective-permute-start | bytes 184328 | tf_op jit(solution)/shard_map/ppermute | solution.py:368
  11.9 1.4 %interior_kernel.1 = (f32[3,16,16,192]{3,2,1,0:T(8,128)S(1)}, f32[16,16,192]{2,1,0:T(8,128)S(1)}) custom-call(f32[5,16,16,192]{3,2,1,0:T(8,128)S(1)} %copy-done, f32[5,16,16,192]{3,2,1,0:T(8,128)S(1)} %copy-done.2, s32[1,192]{1,0:T(1,128)S(1)} %bitcast.5, s32[16,16]{1,0:T(8,128)S(1)} %copy-done.9), custom_call_target="tpu_custom_call" | custom-call | flops 10000000 | bytes 1967872 | tf_op jit(solution)/shard_map/interior_kernel/pallas_call | solution.py:356
  13.3 0.4 collective-permute-done.2.south
  13.7 1.0 %momentum_kernel.1 = f32[16,16,256]{2,1,0:T(8,128)S(1)} custom-call(f32[5,16,16,192]{3,2,1,0:T(8,128)S(1)} %copy-done, f32[3,16,16,192]{3,2,1,0:T(8,128)S(1)} %get-tuple-element.13.inner, f32[16,16,192]{2,1,0:T(8,128)S(1)} %get-tuple-element.14.fluid, f32[5,16,192]{2,1,0:T(8,128)S(1)} %collective-permute-done.west, ...), custom_call_target="tpu_custom_call" | custom-call | flops 10000000 | bytes 2016000 | tf_op jit(solution)/shard_map/momentum_kernel/pallas_call | solution.py:356
  14.7 0.0 copy-start.1
  14.7 17.6 %all_to_all.20 = f32[16,16,256]{2,1,0:T(8,128)S(1)} all-to-all(f32[16,16,256]{2,1,0:T(8,128)S(1)} %momentum_kernel.1), channel_id=1, replica_groups=mesh['px'=16,'py'=16] {'px'}, dimensions={0} | all-to-all | bytes 524288 | tf_op jit(solution)/shard_map/all_to_all | solution.py:426
  32.4 1.6 %forward_kernel.1 = f32[256,1,256]{2,1,0:T(1,128)} custom-call(f32[256,256]{1,0:T(8,128)S(1)} %bitcast.4, f32[256,256]{1,0:T(8,128)S(1)} %copy-done.3, f32[16,256]{1,0:T(8,128)S(1)} %copy-done.8), custom_call_target="tpu_custom_call" | custom-call | bytes 540672 | tf_op jit(solution)/shard_map/forward_kernel/pallas_call | solution.py:356
  33.9 8.8 %all-to-all-start.1 = ((f32[256,1,256]{2,1,0:T(1,128)}), f32[256,1,256]{2,1,0:T(1,128)S(1)}, u32[]{:S(2)}, u32[]{:S(2)}) async-start(f32[256,1,256]{2,1,0:T(1,128)} %forward_kernel.1), calls=%async_computation.1 | async-start | bytes 524288 | tf_op jit(solution)/shard_map/all_to_all | solution.py:430
  42.9 0.1 subtract_add_fusion.shift
  42.9 3.7 %side_kernel.1 = (f32[3,16,16,192]{3,2,1,0:T(8,128)S(1)}, f32[5,16,16,192]{3,2,1,0:T(8,128)}, f32[16,16,192]{2,1,0:T(8,128)S(1)}) custom-call(f32[5,16,16,192]{3,2,1,0:T(8,128)S(1)} %copy-done.1, f32[5,16,16,192]{3,2,1,0:T(8,128)S(1)} %copy-done.2, f32[5,16,192]{2,1,0:T(8,128)S(1)} %collective-permute-done.west, ...), custom_call_target="tpu_custom_call" | custom-call | flops 20000000 | bytes 2213632 | tf_op jit(solution)/shard_map/side_kernel/pallas_call | solution.py:356
  46.6 0.9 copy-done.4
  47.5 0.7 copy-done.6
  48.2 10.5 %all-to-all-done.1.lines = f32[256,1,256]{2,1,0:T(1,128)S(1)} async-done(((f32[256,1,256]{2,1,0:T(1,128)}), f32[256,1,256]{2,1,0:T(1,128)S(1)}, u32[]{:S(2)}, u32[]{:S(2)}) %all-to-all-start.1) | async-done | bytes 262176 | tf_op jit(solution)/shard_map/all_to_all | solution.py:430
  58.7 2.9 %solve_kernel.1 = f32[256,1,256]{2,1,0:T(1,128)S(1)} custom-call(f32[256,1,256]{2,1,0:T(1,128)S(1)} %all-to-all-done.1.lines, f32[256,256]{1,0:T(8,128)S(1)} %copy-done.3, f32[16,256]{1,0:T(8,128)S(1)} %copy-done.8, s32[1,192]{1,0:T(1,128)S(1)} %bitcast.8, f32[1,256]{1,0:T(1,128)S(1)} %subtract_add_fusion.shift), custom_call_target="tpu_custom_call" | custom-call | bytes 542464 | tf_op jit(solution)/shard_map/solve_kernel/pallas_call | solution.py:356
  61.6 20.4 %all_to_all.21.lines = f32[256,1,256]{2,1,0:T(1,128)S(1)} all-to-all(f32[256,1,256]{2,1,0:T(1,128)S(1)} %solve_kernel.1), channel_id=1, replica_groups=mesh['px'=16,'py'=16] {'py','px'}, dimensions={0} | all-to-all | bytes 524288 | tf_op jit(solution)/shard_map/all_to_all | solution.py:435
  81.9 0.8 backward_kernel.1
  82.7 11.8 %all_to_all.22.message = f32[16,16,256]{2,1,0:T(8,128)S(1)} all-to-all(f32[16,16,256]{2,1,0:T(8,128)S(1)} %bitcast.3), channel_id=1, replica_groups=mesh['px'=16,'py'=16] {'px'}, dimensions={0} | all-to-all | bytes 524288 | tf_op jit(solution)/shard_map/all_to_all | solution.py:437
  94.5 1.7 %correct_kernel.1 = (f32[5,16,16,192]{3,2,1,0:T(8,128)}, f32[16,16,192]{2,1,0:T(8,128)}) custom-call(f32[16,16,256]{2,1,0:T(8,128)S(1)} %all_to_all.22.message, f32[3,16,16,192]{3,2,1,0:T(8,128)S(1)} %copy-done.5, s32[1,192]{1,0:T(1,128)S(1)} %bitcast.9, f32[16,16,192]{2,1,0:T(8,128)S(1)} %copy-done.7, ...), custom_call_target="tpu_custom_call", output_to_operand_aliasing={{0}: (4, {})} | custom-call | bytes 2032384 | tf_op jit(solution)/shard_map/correct_kernel/pallas_call | solution.py:356
  (20 shorter events, 0.0 us)
Async XLA Ops:
  0.6 1.3 %copy-start = (f32[5,16,16,192]{3,2,1,0:T(8,128)S(1)}, f32[5,16,16,192]{3,2,1,0:T(8,128)}, u32[]{:S(2)}) copy-start(f32[5,16,16,192]{3,2,1,0:T(8,128)} %state.7) | copy-start | bytes 2949124
  1.9 9.9 %copy-start.2 = (f32[5,16,16,192]{3,2,1,0:T(8,128)S(1)}, f32[5,16,16,192]{3,2,1,0:T(8,128)}, u32[]{:S(2)}) copy-start(f32[5,16,16,192]{3,2,1,0:T(8,128)} %memory.3) | copy-start | bytes 2949124
  2.0 9.9 %copy-start.9 = (s32[16,16]{1,0:T(8,128)S(1)}, s32[16,16]{1,0:T(8,128)}, u32[]{:S(2)}) copy-start(s32[16,16]{1,0:T(8,128)} %height.3) | copy-start | bytes 3076
  2.0 9.9 %copy-start.10 = (s32[192]{0:T(256)S(1)}, s32[192]{0:T(256)}, u32[]{:S(2)}) copy-start(s32[192]{0:T(256)} %param.8) | copy-start | bytes 2308
  2.0 11.2 %collective-permute-start = (f32[5,16,192]{2,1,0:T(8,128)S(1)}, f32[5,16,192]{2,1,0:T(8,128)S(1)}, u32[]{:S(2)}, u32[]{:S(2)}) collective-permute-start(f32[5,16,192]{2,1,0:T(8,128)S(1)} %get-tuple-element.15), channel_id=1, source_target_pairs={{240,0},{0,16},{16,32},{32,48},{48,64},{64,80},{80,96},{96,112},{1... | collective-permute-start | bytes 184328 | tf_op jit(solution)/shard_map/ppermute | solution.py:368
  6.3 7.0 %collective-permute-start.1 = (f32[5,16,192]{2,1,0:T(8,128)S(1)}, f32[5,16,192]{2,1,0:T(8,128)S(1)}, u32[]{:S(2)}, u32[]{:S(2)}) collective-permute-start(f32[5,16,192]{2,1,0:T(8,128)S(1)} %get-tuple-element.16), channel_id=1, source_target_pairs={{16,0},{32,16},{48,32},{64,48},{80,64},{96,80},{112,96},{128,112},... | collective-permute-start | bytes 184328 | tf_op jit(solution)/shard_map/ppermute | solution.py:368
  6.3 7.4 %collective-permute-start.2 = (f32[5,16,192]{2,1,0:T(8,128)S(1)}, f32[5,16,192]{2,1,0:T(8,128)S(1)}, u32[]{:S(2)}, u32[]{:S(2)}) collective-permute-start(f32[5,16,192]{2,1,0:T(8,128)S(1)} %get-tuple-element.17), channel_id=1, source_target_pairs={{15,0},{0,1},{1,2},{2,3},{3,4},{4,5},{5,6},{6,7},{7,8},{8,9},{9,10... | collective-permute-start | bytes 184328 | tf_op jit(solution)/shard_map/ppermute | solution.py:368
  6.6 7.1 %collective-permute-start.3 = (f32[5,16,192]{2,1,0:T(8,128)S(1)}, f32[5,16,192]{2,1,0:T(8,128)S(1)}, u32[]{:S(2)}, u32[]{:S(2)}) collective-permute-start(f32[5,16,192]{2,1,0:T(8,128)S(1)} %get-tuple-element.18), channel_id=1, source_target_pairs={{1,0},{2,1},{3,2},{4,3},{5,4},{6,5},{7,6},{8,7},{9,8},{10,9},{11,1... | collective-permute-start | bytes 184328 | tf_op jit(solution)/shard_map/ppermute | solution.py:368
  13.7 18.7 %copy-start.3 = (f32[256,256]{1,0:T(8,128)S(1)}, f32[256,256]{1,0:T(8,128)}, u32[]{:S(2)}) copy-start(f32[256,256]{1,0:T(8,128)} %constant.19.clone.basis) | copy-start | bytes 786436
  13.7 18.7 %copy-start.8 = (f32[16,256]{1,0:T(8,128)S(1)}, f32[16,256]{1,0:T(8,128)}, u32[]{:S(2)}) copy-start(f32[16,256]{1,0:T(8,128)} %constant.20.clone.after) | copy-start | bytes 49156
  14.7 28.2 %copy-start.1 = (f32[5,16,16,192]{3,2,1,0:T(8,128)S(1)}, f32[5,16,16,192]{3,2,1,0:T(8,128)}, u32[]{:S(2)}) copy-start(f32[5,16,16,192]{3,2,1,0:T(8,128)} %state.7) | copy-start | bytes 2949124
  33.9 24.7 %all-to-all-start.1 = ((f32[256,1,256]{2,1,0:T(1,128)}), f32[256,1,256]{2,1,0:T(1,128)S(1)}, u32[]{:S(2)}, u32[]{:S(2)}) async-start(f32[256,1,256]{2,1,0:T(1,128)} %forward_kernel.1), calls=%async_computation.1 | async-start | bytes 524288 | tf_op jit(solution)/shard_map/all_to_all | solution.py:430
  46.6 0.9 copy-start.4
  47.5 0.7 copy-start.6
  58.7 35.9 %copy-start.5 = (f32[3,16,16,192]{3,2,1,0:T(8,128)S(1)}, f32[3,16,16,192]{3,2,1,0:T(8,128)}, u32[]{:S(2)}) copy-start(f32[3,16,16,192]{3,2,1,0:T(8,128)} %copy-done.4) | copy-start | bytes 1769476
  58.7 35.9 %copy-start.7 = (f32[16,16,192]{2,1,0:T(8,128)S(1)}, f32[16,16,192]{2,1,0:T(8,128)}, u32[]{:S(2)}) copy-start(f32[16,16,192]{2,1,0:T(8,128)} %copy-done.6) | copy-start | bytes 589828

commit v5 on v4

--- a/solution.py
+++ b/solution.py
@@ -100,11 +100,17 @@
     return jnp.concatenate([jnp.zeros_like(a[:, :1]), a[:, :-1]], axis=1)
 
 
-def edges_kernel(state, west, east, south, north):
-    west[...] = state[:, 0]
-    east[...] = state[:, TILE - 1]
-    south[...] = state[:, :, 0]
-    north[...] = state[:, :, TILE - 1]
+def odd(axis):
+    return lax.rem(lax.axis_index(axis), 2) == 1
+
+
+def edges_kernel(state, x_outer, x_inner, y_outer, y_inner):
+    low, high = state[:, 0], state[:, TILE - 1]
+    x_outer[...] = jnp.where(odd("px"), high, low)
+    x_inner[...] = jnp.where(odd("px"), low, high)
+    low, high = state[:, :, 0], state[:, :, TILE - 1]
+    y_outer[...] = jnp.where(odd("py"), high, low)
+    y_inner[...] = jnp.where(odd("py"), low, high)
 
 
 def faces(s, e, u):
@@ -183,9 +189,14 @@
 
 
 def momentum_kernel(
-    state, inner, fluid, west, east, south, north, level_steps, message, provisional
+    state, inner, fluid, x_outer, x_inner, y_outer, y_inner, level_steps, message, provisional
 ):
     provisional[...] = inner[...]
+    odd_x, odd_y = odd("px"), odd("py")
+    west = [jnp.where(odd_x, x_inner[f], x_outer[f]) for f in range(3)]
+    east = [jnp.where(odd_x, x_outer[f], x_inner[f]) for f in range(3)]
+    south = [jnp.where(odd_y, y_inner[f], y_outer[f]) for f in range(3)]
+    north = [jnp.where(odd_y, y_outer[f], y_inner[f]) for f in range(3)]
     last, factor = TILE - 1, RK_STEP * TIME_STEP
     for f in range(3):
         provisional[f, 0] -= factor * fluid[0] * faces(west[f], state[f, 0], west[0])
@@ -264,12 +275,13 @@
 
 
 def side_kernel(
-    state, memory, west, east, south, north, level_steps, height,
+    state, memory, x_outer, x_inner, y_outer, y_inner, level_steps, height,
     provisional, updated, fluid_kept, state_here, memory_here, halo_here, fluid, fields, sems,
 ):
-    halos = (west, east, south, north)
     pairs = [(state, state_here), (memory, memory_here)]
-    pairs += [(halo, halo_here.at[i]) for i, halo in enumerate(halos)]
+    first_x, first_y = odd("px").astype(jnp.int32), odd("py").astype(jnp.int32)
+    pairs += [(x_outer, halo_here.at[first_x]), (x_inner, halo_here.at[1 - first_x])]
+    pairs += [(y_outer, halo_here.at[2 + first_y]), (y_inner, halo_here.at[3 - first_y])]
     arriving = loaded(pairs, sems)
     fill_fluid(height, fluid)
     leaving = loaded([(fluid, fluid_kept)], sems.at[pl.ds(6, 1)])
@@ -363,9 +375,10 @@
     )(*operands)
 
 
-def passed(block, axis, distance):
+def swapped(block, axis, outer):
     count = lax.axis_size(axis)
-    return lax.ppermute(block, axis, [((i - distance) % count, i) for i in range(count)])
+    partner = [((i + outer) ^ 1) - outer for i in range(count)]
+    return lax.ppermute(block, axis, [(i, p % count) for i, p in enumerate(partner)])
 
 
 def eigenvalues(frequency):
@@ -375,10 +388,10 @@
 def per_device(state, memory, level_steps, building_height):
     plane = shaped(5, TILE, LEVELS)
     edges = call(edges_kernel, [plane] * 4, state)
-    west = passed(edges[1], "px", 1)
-    east = passed(edges[0], "px", -1)
-    south = passed(edges[3], "py", 1)
-    north = passed(edges[2], "py", -1)
+    halos = [
+        swapped(edges[i], axis, outer)
+        for i, (axis, outer) in enumerate([("px", 1), ("px", 0), ("py", 1), ("py", 0)])
+    ]
 
     steps = level_steps.reshape(1, LEVELS)
     own_x = lax.axis_index("py") * lax.axis_size("px") + lax.axis_index("px")
@@ -388,7 +401,6 @@
     scratch = lambda *shape: pltpu.VMEM(shape, jnp.float32)
     sems = pltpu.SemaphoreType.DMA
 
-    halos = (west, east, south, north)
     inner, fluid = call(
         interior_kernel,
         [shaped(3, TILE, TILE, LEVELS), shaped(TILE, TILE, LEVELS)],

time: 96.5 us -> 94.9 us (0.983)
  blocking collectives: 49.8 us -> 46 us
  waiting for transfers between devices: 10.9 us -> 13.5 us
    all_to_all x1, blocking collectives: 17.6 us -> 13.9 us  [per_device(): lax.all_to_all(message, 'px', split_axis=0, concat_axis=0, tiled=True)]
    all_to_all x1, starting transfers between devices: 8.83 us -> 6.06 us  [per_device(): lax.all_to_all(spectrum, ('py', 'px'), split_axis=0, concat_axis=0, tiled...]
    ppermute x4, waiting for transfers between devices: 0.45 us -> 2.94 us  [swapped(): lax.ppermute(block, axis, [(i, p % count) for i, p in enumerate(partner)])]
    ppermute x4, starting transfers between devices: 9.82 us -> 12.1 us  [swapped(): lax.ppermute(block, axis, [(i, p % count) for i, p in enumerate(partner)])]
  transfers between devices with their start and end apart: 5 -> 5, of which waited for: 2 -> 3; matrix products, arithmetic and copies ran while one was open for 0% -> 0% of each run, Pallas kernels for 5% -> 5%
where the time goes in v5:
time: 94.9 us; the launch traced here: 94.6 us
  blocking collectives  46 us (48%)
  starting transfers between devices  18.2 us (19%)
  waiting for transfers between devices  13.5 us (14%)
  Pallas kernels  13.1 us (14%)
  local copies, waits for them, and re-layouts  2.92 us (3%)
    all_to_all x1, blocking collectives, per_device(): lax.all_to_all(solved, ('py', 'px'), split_axis=0, concat_axis=0, tiled=T...  20.4 us
    all_to_all x1, blocking collectives, per_device(): lax.all_to_all(message, 'px', split_axis=0, concat_axis=0, tiled=True)  13.9 us
    pallas_call x8, Pallas kernels, call(): pl.pallas_call(kernel, out_shape=out_shape, name=kernel.__name__, compile...  13.1 us
    ppermute x4, starting transfers between devices, swapped(): lax.ppermute(block, axis, [(i, p % count) for i, p in enumerate(partner)])  12.1 us
    all_to_all x1, blocking collectives, per_device(): lax.all_to_all(message.reshape(TILE, TILE, WIDE), 'px', split_axis=0, con...  11.8 us
    all_to_all x1, waiting for transfers between devices, per_device(): lax.all_to_all(spectrum, ('py', 'px'), split_axis=0, concat_axis=0, tiled...  10.5 us
    all_to_all x1, starting transfers between devices, per_device(): lax.all_to_all(spectrum, ('py', 'px'), split_axis=0, concat_axis=0, tiled...  6.06 us
    ppermute x4, waiting for transfers between devices, swapped(): lax.ppermute(block, axis, [(i, p % count) for i, p in enumerate(partner)])  2.94 us
  transfers between devices with their start and end apart: 5, of which 3 were waited for; matrix products, arithmetic and copies ran while one was open for 0% of the time, Pallas kernels for 5%

profile of v5, /device:TPU:1, one launch (start us, length us, event | category | flops | bytes accessed | tf_op | source)
XLA Modules:
  0.0 94.6 jit_solution(17472639764956534311)
XLA Ops:
  0.6 0.0 copy-start
  0.6 1.3 %copy-done = f32[5,16,16,192]{3,2,1,0:T(8,128)S(1)} copy-done((f32[5,16,16,192]{3,2,1,0:T(8,128)S(1)}, f32[5,16,16,192]{3,2,1,0:T(8,128)}, u32[]{:S(2)}) %copy-start) | copy-done | bytes 983064
  2.0 0.1 edges_kernel.1
  2.1 4.2 %collective-permute-start = (f32[5,16,192]{2,1,0:T(8,128)S(1)}, f32[5,16,192]{2,1,0:T(8,128)S(1)}, u32[]{:S(2)}, u32[]{:S(2)}) collective-permute-start(f32[5,16,192]{2,1,0:T(8,128)S(1)} %get-tuple-element.15), channel_id=1, source_target_pairs={{0,240},{16,32},{32,16},{48,64},{64,48},{80,96},{96,80},{112,128},... | collective-permute-start | bytes 184328 | tf_op jit(solution)/shard_map/ppermute | solution.py:381
  6.3 2.3 %collective-permute-start.1 = (f32[5,16,192]{2,1,0:T(8,128)S(1)}, f32[5,16,192]{2,1,0:T(8,128)S(1)}, u32[]{:S(2)}, u32[]{:S(2)}) collective-permute-start(f32[5,16,192]{2,1,0:T(8,128)S(1)} %get-tuple-element.16), channel_id=1, source_target_pairs={{0,16},{16,0},{32,48},{48,32},{64,80},{80,64},{96,112},{112,96},{1... | collective-permute-start | bytes 184328 | tf_op jit(solution)/shard_map/ppermute | solution.py:381
  8.6 5.6 %collective-permute-start.2 = (f32[5,16,192]{2,1,0:T(8,128)S(1)}, f32[5,16,192]{2,1,0:T(8,128)S(1)}, u32[]{:S(2)}, u32[]{:S(2)}) collective-permute-start(f32[5,16,192]{2,1,0:T(8,128)S(1)} %get-tuple-element.17), channel_id=1, source_target_pairs={{0,15},{1,2},{2,1},{3,4},{4,3},{5,6},{6,5},{7,8},{8,7},{9,10},{10,... | collective-permute-start | bytes 184328 | tf_op jit(solution)/shard_map/ppermute | solution.py:381
  14.2 1.4 %interior_kernel.1 = (f32[3,16,16,192]{3,2,1,0:T(8,128)S(1)}, f32[16,16,192]{2,1,0:T(8,128)S(1)}) custom-call(f32[5,16,16,192]{3,2,1,0:T(8,128)S(1)} %copy-done, f32[5,16,16,192]{3,2,1,0:T(8,128)S(1)} %copy-done.2, s32[1,192]{1,0:T(1,128)S(1)} %bitcast.5, s32[16,16]{1,0:T(8,128)S(1)} %copy-done.9), custom_call_target="tpu_custom_call" | custom-call | flops 10000000 | bytes 1967872 | tf_op jit(solution)/shard_map/interior_kernel/pallas_call | solution.py:368
  15.6 1.4 %collective-permute-done.2.y_outer = f32[5,16,192]{2,1,0:T(8,128)S(1)} collective-permute-done((f32[5,16,192]{2,1,0:T(8,128)S(1)}, f32[5,16,192]{2,1,0:T(8,128)S(1)}, u32[]{:S(2)}, u32[]{:S(2)}) %collective-permute-start.2) | collective-permute-done | bytes 61472 | tf_op jit(solution)/shard_map/ppermute | solution.py:381
  17.0 1.5 %collective-permute-done.3.y_inner = f32[5,16,192]{2,1,0:T(8,128)S(1)} collective-permute-done((f32[5,16,192]{2,1,0:T(8,128)S(1)}, f32[5,16,192]{2,1,0:T(8,128)S(1)}, u32[]{:S(2)}, u32[]{:S(2)}) %collective-permute-start.3) | collective-permute-done | bytes 61472 | tf_op jit(solution)/shard_map/ppermute | solution.py:381
  18.5 1.0 %momentum_kernel.1 = f32[16,16,256]{2,1,0:T(8,128)S(1)} custom-call(f32[5,16,16,192]{3,2,1,0:T(8,128)S(1)} %copy-done, f32[3,16,16,192]{3,2,1,0:T(8,128)S(1)} %get-tuple-element.13.inner, f32[16,16,192]{2,1,0:T(8,128)S(1)} %get-tuple-element.14.fluid, f32[5,16,192]{2,1,0:T(8,128)S(1)} %collective-permute-done.x_outer, ...), custom_call_target="tpu_custom_call" | custom-call | flops 10000000 | bytes 2016000 | tf_op jit(solution)/shard_map/momentum_kernel/pallas_call | solution.py:368
  19.6 0.0 copy-start.1
  19.6 13.9 %all_to_all.20 = f32[16,16,256]{2,1,0:T(8,128)S(1)} all-to-all(f32[16,16,256]{2,1,0:T(8,128)S(1)} %momentum_kernel.1), channel_id=1, replica_groups=mesh['px'=16,'py'=16] {'px'}, dimensions={0} | all-to-all | bytes 524288 | tf_op jit(solution)/shard_map/all_to_all | solution.py:438
  33.4 1.6 %forward_kernel.1 = f32[256,1,256]{2,1,0:T(1,128)} custom-call(f32[256,256]{1,0:T(8,128)S(1)} %bitcast.4, f32[256,256]{1,0:T(8,128)S(1)} %copy-done.3, f32[16,256]{1,0:T(8,128)S(1)} %copy-done.8), custom_call_target="tpu_custom_call" | custom-call | bytes 540672 | tf_op jit(solution)/shard_map/forward_kernel/pallas_call | solution.py:368
  35.0 6.1 %all-to-all-start.1 = ((f32[256,1,256]{2,1,0:T(1,128)}), f32[256,1,256]{2,1,0:T(1,128)S(1)}, u32[]{:S(2)}, u32[]{:S(2)}) async-start(f32[256,1,256]{2,1,0:T(1,128)} %forward_kernel.1), calls=%async_computation.1 | async-start | bytes 524288 | tf_op jit(solution)/shard_map/all_to_all | solution.py:442
  41.2 0.1 subtract_add_fusion.shift
  41.2 3.7 %side_kernel.1 = (f32[3,16,16,192]{3,2,1,0:T(8,128)S(1)}, f32[5,16,16,192]{3,2,1,0:T(8,128)}, f32[16,16,192]{2,1,0:T(8,128)S(1)}) custom-call(f32[5,16,16,192]{3,2,1,0:T(8,128)S(1)} %copy-done.1, f32[5,16,16,192]{3,2,1,0:T(8,128)S(1)} %copy-done.2, f32[5,16,192]{2,1,0:T(8,128)S(1)} %collective-permute-done.x_outer, ...), custom_call_target="tpu_custom_call" | custom-call | flops 20000000 | bytes 2213632 | tf_op jit(solution)/shard_map/side_kernel/pallas_call | solution.py:368
  44.9 0.9 copy-done.4
  45.8 0.7 copy-done.6
  46.5 10.5 %all-to-all-done.1.lines = f32[256,1,256]{2,1,0:T(1,128)S(1)} async-done(((f32[256,1,256]{2,1,0:T(1,128)}), f32[256,1,256]{2,1,0:T(1,128)S(1)}, u32[]{:S(2)}, u32[]{:S(2)}) %all-to-all-start.1) | async-done | bytes 262176 | tf_op jit(solution)/shard_map/all_to_all | solution.py:442
  57.0 2.9 %solve_kernel.1 = f32[256,1,256]{2,1,0:T(1,128)S(1)} custom-call(f32[256,1,256]{2,1,0:T(1,128)S(1)} %all-to-all-done.1.lines, f32[256,256]{1,0:T(8,128)S(1)} %copy-done.3, f32[16,256]{1,0:T(8,128)S(1)} %copy-done.8, s32[1,192]{1,0:T(1,128)S(1)} %bitcast.8, f32[1,256]{1,0:T(1,128)S(1)} %subtract_add_fusion.shift), custom_call_target="tpu_custom_call" | custom-call | bytes 542464 | tf_op jit(solution)/shard_map/solve_kernel/pallas_call | solution.py:368
  59.9 20.4 %all_to_all.21.lines = f32[256,1,256]{2,1,0:T(1,128)S(1)} all-to-all(f32[256,1,256]{2,1,0:T(1,128)S(1)} %solve_kernel.1), channel_id=1, replica_groups=mesh['px'=16,'py'=16] {'py','px'}, dimensions={0} | all-to-all | bytes 524288 | tf_op jit(solution)/shard_map/all_to_all | solution.py:447
  80.3 0.8 backward_kernel.1
  81.1 11.8 %all_to_all.22.message = f32[16,16,256]{2,1,0:T(8,128)S(1)} all-to-all(f32[16,16,256]{2,1,0:T(8,128)S(1)} %bitcast.3), channel_id=1, replica_groups=mesh['px'=16,'py'=16] {'px'}, dimensions={0} | all-to-all | bytes 524288 | tf_op jit(solution)/shard_map/all_to_all | solution.py:449
  92.9 1.7 %correct_kernel.1 = (f32[5,16,16,192]{3,2,1,0:T(8,128)}, f32[16,16,192]{2,1,0:T(8,128)}) custom-call(f32[16,16,256]{2,1,0:T(8,128)S(1)} %all_to_all.22.message, f32[3,16,16,192]{3,2,1,0:T(8,128)S(1)} %copy-done.5, s32[1,192]{1,0:T(1,128)S(1)} %bitcast.9, f32[16,16,192]{2,1,0:T(8,128)S(1)} %copy-done.7, ...), custom_call_target="tpu_custom_call", output_to_operand_aliasing={{0}: (4, {})} | custom-call | bytes 2032384 | tf_op jit(solution)/shard_map/correct_kernel/pallas_call | solution.py:368
  (20 shorter events, 0.0 us)
Async XLA Ops:
  0.6 1.3 %copy-start = (f32[5,16,16,192]{3,2,1,0:T(8,128)S(1)}, f32[5,16,16,192]{3,2,1,0:T(8,128)}, u32[]{:S(2)}) copy-start(f32[5,16,16,192]{3,2,1,0:T(8,128)} %state.7) | copy-start | bytes 2949124
  1.9 12.3 %copy-start.2 = (f32[5,16,16,192]{3,2,1,0:T(8,128)S(1)}, f32[5,16,16,192]{3,2,1,0:T(8,128)}, u32[]{:S(2)}) copy-start(f32[5,16,16,192]{3,2,1,0:T(8,128)} %memory.3) | copy-start | bytes 2949124
  2.0 12.3 %copy-start.9 = (s32[16,16]{1,0:T(8,128)S(1)}, s32[16,16]{1,0:T(8,128)}, u32[]{:S(2)}) copy-start(s32[16,16]{1,0:T(8,128)} %height.3) | copy-start | bytes 3076
  2.0 12.3 %copy-start.10 = (s32[192]{0:T(256)S(1)}, s32[192]{0:T(256)}, u32[]{:S(2)}) copy-start(s32[192]{0:T(256)} %param.8) | copy-start | bytes 2308
  2.1 13.5 %collective-permute-start = (f32[5,16,192]{2,1,0:T(8,128)S(1)}, f32[5,16,192]{2,1,0:T(8,128)S(1)}, u32[]{:S(2)}, u32[]{:S(2)}) collective-permute-start(f32[5,16,192]{2,1,0:T(8,128)S(1)} %get-tuple-element.15), channel_id=1, source_target_pairs={{0,240},{16,32},{32,16},{48,64},{64,48},{80,96},{96,80},{112,128},... | collective-permute-start | bytes 184328 | tf_op jit(solution)/shard_map/ppermute | solution.py:381
  6.3 9.3 %collective-permute-start.1 = (f32[5,16,192]{2,1,0:T(8,128)S(1)}, f32[5,16,192]{2,1,0:T(8,128)S(1)}, u32[]{:S(2)}, u32[]{:S(2)}) collective-permute-start(f32[5,16,192]{2,1,0:T(8,128)S(1)} %get-tuple-element.16), channel_id=1, source_target_pairs={{0,16},{16,0},{32,48},{48,32},{64,80},{80,64},{96,112},{112,96},{1... | collective-permute-start | bytes 184328 | tf_op jit(solution)/shard_map/ppermute | solution.py:381
  8.6 8.4 %collective-permute-start.2 = (f32[5,16,192]{2,1,0:T(8,128)S(1)}, f32[5,16,192]{2,1,0:T(8,128)S(1)}, u32[]{:S(2)}, u32[]{:S(2)}) collective-permute-start(f32[5,16,192]{2,1,0:T(8,128)S(1)} %get-tuple-element.17), channel_id=1, source_target_pairs={{0,15},{1,2},{2,1},{3,4},{4,3},{5,6},{6,5},{7,8},{8,7},{9,10},{10,... | collective-permute-start | bytes 184328 | tf_op jit(solution)/shard_map/ppermute | solution.py:381
  14.2 4.3 %collective-permute-start.3 = (f32[5,16,192]{2,1,0:T(8,128)S(1)}, f32[5,16,192]{2,1,0:T(8,128)S(1)}, u32[]{:S(2)}, u32[]{:S(2)}) collective-permute-start(f32[5,16,192]{2,1,0:T(8,128)S(1)} %get-tuple-element.18), channel_id=1, source_target_pairs={{0,1},{1,0},{2,3},{3,2},{4,5},{5,4},{6,7},{7,6},{8,9},{9,8},{10,11... | collective-permute-start | bytes 184328 | tf_op jit(solution)/shard_map/ppermute | solution.py:381
  18.5 14.9 %copy-start.3 = (f32[256,256]{1,0:T(8,128)S(1)}, f32[256,256]{1,0:T(8,128)}, u32[]{:S(2)}) copy-start(f32[256,256]{1,0:T(8,128)} %constant.19.clone.basis) | copy-start | bytes 786436
  18.5 14.9 %copy-start.8 = (f32[16,256]{1,0:T(8,128)S(1)}, f32[16,256]{1,0:T(8,128)}, u32[]{:S(2)}) copy-start(f32[16,256]{1,0:T(8,128)} %constant.20.clone.after) | copy-start | bytes 49156
  19.6 21.7 %copy-start.1 = (f32[5,16,16,192]{3,2,1,0:T(8,128)S(1)}, f32[5,16,16,192]{3,2,1,0:T(8,128)}, u32[]{:S(2)}) copy-start(f32[5,16,16,192]{3,2,1,0:T(8,128)} %state.7) | copy-start | bytes 2949124
  35.0 22.0 %all-to-all-start.1 = ((f32[256,1,256]{2,1,0:T(1,128)}), f32[256,1,256]{2,1,0:T(1,128)S(1)}, u32[]{:S(2)}, u32[]{:S(2)}) async-start(f32[256,1,256]{2,1,0:T(1,128)} %forward_kernel.1), calls=%async_computation.1 | async-start | bytes 524288 | tf_op jit(solution)/shard_map/all_to_all | solution.py:442
  44.9 0.9 copy-start.4
  45.8 0.7 copy-start.6
  57.0 35.9 %copy-start.5 = (f32[3,16,16,192]{3,2,1,0:T(8,128)S(1)}, f32[3,16,16,192]{3,2,1,0:T(8,128)}, u32[]{:S(2)}) copy-start(f32[3,16,16,192]{3,2,1,0:T(8,128)} %copy-done.4) | copy-start | bytes 1769476
  57.0 35.9 %copy-start.7 = (f32[16,16,192]{2,1,0:T(8,128)S(1)}, f32[16,16,192]{2,1,0:T(8,128)}, u32[]{:S(2)}) copy-start(f32[16,16,192]{2,1,0:T(8,128)} %copy-done.6) | copy-start | bytes 589828

commit v6 on v5

--- a/solution.py
+++ b/solution.py
@@ -25,15 +25,14 @@
 STRIDES = (1, 2, 4, 8, 16, 32, 64, 128)
 
 
-def tables():
+def table():
     n = np.arange(LINE)
     angles = 2.0 * np.pi / LINE * (np.outer(n, n) % LINE)
     basis = (np.cos(angles) + np.sin(angles)) / np.sqrt(LINE)
-    after = basis[(n[:TILE] + 1) * TILE % LINE]
-    return basis.astype(np.float32), after.astype(np.float32)
-
-
-BASIS, AFTER = tables()
+    return basis.astype(np.float32)
+
+
+BASIS = table()
 
 
 def product(a, b, contract=((1,), (0,))):
@@ -75,20 +74,15 @@
     )
 
 
-def every_block(rows):
-    return jnp.concatenate([rows] * TILE, axis=0)
-
-
 def level_rows(level_steps):
     thickness = level_steps[...].astype(jnp.float32)
     spacing = 0.5 * (thickness + lanes_up(thickness))
     return thickness, spacing
 
 
-def chunk_mask(shape, owner):
-    lane = lax.broadcasted_iota(jnp.int32, shape, 1)
-    row = lax.broadcasted_iota(jnp.int32, shape, 0)
-    start = (row % TILE if owner == "low" else row // TILE) * CHUNK
+def block_mask():
+    lane = lax.broadcasted_iota(jnp.int32, (TILE, WIDE), 1)
+    start = lax.broadcasted_iota(jnp.int32, (TILE, WIDE), 0) * CHUNK
     return (lane >= start) & (lane < start + CHUNK)
 
 
@@ -209,10 +203,14 @@
         )
     inv_thick = 1.0 / level_rows(level_steps)[0]
     zeros = jnp.zeros((TILE, WIDE - LEVELS), jnp.float32)
+    mask = block_mask()
     last_u = jnp.concatenate([provisional[0, TILE - 1], zeros], axis=1)
-    u_packed = jnp.where(chunk_mask((LINE, WIDE), "low"), each_block(last_u), 0.0)
+    u_packed = jnp.concatenate(
+        [jnp.where(mask, last_u[y : y + 1], 0.0) for y in range(TILE)], axis=0
+    )
     last_v = jnp.concatenate([provisional[1, :, TILE - 1], zeros], axis=1)
-    v_packed = jnp.where(chunk_mask((LINE, WIDE), "high"), every_block(last_v), 0.0)
+    ones = jnp.where(mask, 1.0, 0.0)
+    v_packed = jnp.concatenate([last_v * ones[y : y + 1] for y in range(TILE)], axis=0)
     upper = picked(u_packed, pack_places(FIRST)) + picked(v_packed, pack_places(SECOND))
     upper = upper.reshape(TILE, TILE, 128)
     for x in range(TILE):
@@ -234,21 +232,31 @@
 
 
 def unpacked(values, first, owner):
-    mask = chunk_mask((LINE, WIDE), owner)
-    spread = jnp.where(mask, picked(values[:, 128:], unpack_places(first)), 0.0)
-    return spread.reshape(TILE, TILE, WIDE).sum(axis=1 if owner == "low" else 0)
-
-
-def repacked(rows, first):
-    chunks = jnp.where(chunk_mask((LINE, WIDE), "low"), each_block(rows), 0.0)
-    return picked(chunks, pack_places(first))
-
-
-def forward_kernel(lines, basis, after, spectrum):
-    values = lines[...]
-    extra = unpacked(values, FIRST, "low")
-    total = product(basis[...], values) - product(after[...], extra, ((0,), (0,)))
-    spectrum[:, 0, :] = total
+    spread = picked(values[:, 128:], unpack_places(first)).reshape(TILE, TILE, WIDE)
+    mask = block_mask()
+    if owner == "low":
+        return jnp.where(mask[None], spread, 0.0).sum(axis=1)
+    ones = jnp.where(mask, 1.0, 0.0)
+    return sum(spread[b] * ones[b : b + 1] for b in range(TILE))
+
+
+def lessened(values, first):
+    extra = unpacked(values, first, "low")
+    extra = jnp.concatenate([extra[TILE - 1 :], extra[: TILE - 1]], axis=0)
+    blocks = values.reshape(TILE, TILE, WIDE)
+    start = lax.broadcasted_iota(jnp.int32, blocks.shape, 1) == 0
+    return jnp.where(start, blocks - extra[:, None, :], blocks).reshape(LINE, WIDE)
+
+
+def repacked(back, first):
+    mask = block_mask()
+    rows = [back[b * TILE : b * TILE + 1] for b in range(TILE)]
+    chunks = [jnp.where(mask, row, 0.0) for row in rows[1:] + rows[:1]]
+    return picked(jnp.concatenate(chunks, axis=0), pack_places(first))
+
+
+def forward_kernel(lines, basis, spectrum):
+    spectrum[:, 0, :] = product(basis[...], lessened(lines[...], FIRST))
 
 
 def column_of(row):
@@ -301,7 +309,8 @@
         copy.wait()
 
 
-def solve_kernel(lines, basis, after, level_steps, shift, result):
+def solve_kernel(lines, basis, level_steps, shift, result, tiled):
+    tiled[...] = lines[:, 0, :]
     thickness, spacing = level_rows(level_steps)
     level = lax.broadcasted_iota(jnp.int32, (1, LEVELS), 1)
     inv_space = 1.0 / spacing
@@ -309,25 +318,21 @@
     diagonal = column_of(inv_space + lanes_down(inv_space)) + thick * shift[...]
     between = column_of(jnp.where(level < LEVELS - 1, -inv_space, 0.0))
     coupling = jnp.broadcast_to(between, (LEVELS, LINE))
-    values = lines[:, 0, :]
-    extra = unpacked(values, SECOND, "low")
+    values = lessened(tiled[...], SECOND)
     main = product(values, basis[...], ((0,), (0,)))
-    fix = product(extra, after[...], ((0,), (0,)))
-    right = thick * (fix[:LEVELS] - main[:LEVELS])
+    right = thick * (-main[:LEVELS])
     solved = reduced(diagonal, coupling, right)
     solved = jnp.concatenate([solved, jnp.zeros((WIDE - LEVELS, LINE), jnp.float32)], axis=0)
     back = product(basis[...], solved, ((1,), (1,)))
-    beside = product(after[...], solved, ((1,), (1,)))
     result[:, 0, :128] = back[:, :128]
-    result[:, 0, 128:] = back[:, 128:] + repacked(beside, FIRST)
-
-
-def backward_kernel(lines, basis, after, message):
-    values = lines[:, 0, :]
-    back = product(basis[...], values)
-    beside = product(after[...], values)
+    result[:, 0, 128:] = back[:, 128:] + repacked(back, FIRST)
+
+
+def backward_kernel(lines, basis, message, tiled):
+    tiled[...] = lines[:, 0, :]
+    back = product(basis[...], tiled[...])
     message[:, :128] = back[:, :128]
-    message[:, 128:] = back[:, 128:] + repacked(beside, SECOND)
+    message[:, 128:] = back[:, 128:] + repacked(back, SECOND)
 
 
 def correct_kernel(
@@ -396,7 +401,7 @@
     steps = level_steps.reshape(1, LEVELS)
     own_x = lax.axis_index("py") * lax.axis_size("px") + lax.axis_index("px")
     shift = eigenvalues(jnp.arange(LINE, dtype=jnp.int32)) + eigenvalues(own_x)
-    basis, after = jnp.asarray(BASIS), jnp.asarray(AFTER)
+    basis = jnp.asarray(BASIS)
     vmem, hbm = pl.BlockSpec(memory_space=pltpu.VMEM), pl.BlockSpec(memory_space=pltpu.HBM)
     scratch = lambda *shape: pltpu.VMEM(shape, jnp.float32)
     sems = pltpu.SemaphoreType.DMA
@@ -437,15 +442,18 @@
     )
     lines = lax.all_to_all(message, "px", split_axis=0, concat_axis=0, tiled=True)
     spectrum = call(
-        forward_kernel, shaped(LINE, 1, WIDE), lines.reshape(LINE, WIDE), basis, after
+        forward_kernel, shaped(LINE, 1, WIDE), lines.reshape(LINE, WIDE), basis
     )
     lines = lax.all_to_all(spectrum, ("py", "px"), split_axis=0, concat_axis=0, tiled=True)
     lines, provisional = lax.optimization_barrier((lines, provisional))
     solved = call(
-        solve_kernel, shaped(LINE, 1, WIDE), lines, basis, after, steps, shift.reshape(1, LINE)
+        solve_kernel, shaped(LINE, 1, WIDE), lines, basis, steps, shift.reshape(1, LINE),
+        scratch_shapes=[scratch(LINE, WIDE)],
     )
     lines = lax.all_to_all(solved, ("py", "px"), split_axis=0, concat_axis=0, tiled=True)
-    message = call(backward_kernel, shaped(LINE, WIDE), lines, basis, after)
+    message = call(
+        backward_kernel, shaped(LINE, WIDE), lines, basis, scratch_shapes=[scratch(LINE, WIDE)]
+    )
     message = lax.all_to_all(
         message.reshape(TILE, TILE, WIDE), "px", split_axis=0, concat_axis=0, tiled=True
     )

time: 94.9 us -> 94.2 us (level)
    unnamed x22 -> x20, local copies, waits for them, and re-layouts: 2.92 us -> 2.93 us
where the time goes in v6:
time: 94.2 us; the launch traced here: 94 us
  blocking collectives  46 us (49%)
  starting transfers between devices  18.2 us (19%)
  waiting for transfers between devices  13.5 us (14%)
  Pallas kernels  12.5 us (13%)
  local copies, waits for them, and re-layouts  2.93 us (3%)
    all_to_all x1, blocking collectives, per_device(): lax.all_to_all(solved, ('py', 'px'), split_axis=0, concat_axis=0, tiled=T...  20.4 us
    all_to_all x1, blocking collectives, per_device(): lax.all_to_all(message, 'px', split_axis=0, concat_axis=0, tiled=True)  13.9 us
    pallas_call x8, Pallas kernels, call(): pl.pallas_call(kernel, out_shape=out_shape, name=kernel.__name__, compile...  12.5 us
    ppermute x4, starting transfers between devices, swapped(): lax.ppermute(block, axis, [(i, p % count) for i, p in enumerate(partner)])  12.1 us
    all_to_all x1, blocking collectives, per_device(): lax.all_to_all(message.reshape(TILE, TILE, WIDE), 'px', split_axis=0, con...  11.8 us
    all_to_all x1, waiting for transfers between devices, per_device(): lax.all_to_all(spectrum, ('py', 'px'), split_axis=0, concat_axis=0, tiled...  10.5 us
    all_to_all x1, starting transfers between devices, per_device(): lax.all_to_all(spectrum, ('py', 'px'), split_axis=0, concat_axis=0, tiled...  6.05 us
    ppermute x4, waiting for transfers between devices, swapped(): lax.ppermute(block, axis, [(i, p % count) for i, p in enumerate(partner)])  2.94 us
  transfers between devices with their start and end apart: 5, of which 3 were waited for; matrix products, arithmetic and copies ran while one was open for 0% of the time, Pallas kernels for 5%

profile of v6, /device:TPU:1, one launch (start us, length us, event | category | flops | bytes accessed | tf_op | source)
XLA Modules:
  0.0 94.0 jit_solution(9911813682812348843)
XLA Ops:
  0.6 0.0 copy-start
  0.6 1.3 %copy-done = f32[5,16,16,192]{3,2,1,0:T(8,128)S(1)} copy-done((f32[5,16,16,192]{3,2,1,0:T(8,128)S(1)}, f32[5,16,16,192]{3,2,1,0:T(8,128)}, u32[]{:S(2)}) %copy-start) | copy-done | bytes 983064
  2.0 0.1 edges_kernel.1
  2.1 4.2 %collective-permute-start = (f32[5,16,192]{2,1,0:T(8,128)S(1)}, f32[5,16,192]{2,1,0:T(8,128)S(1)}, u32[]{:S(2)}, u32[]{:S(2)}) collective-permute-start(f32[5,16,192]{2,1,0:T(8,128)S(1)} %get-tuple-element.15), channel_id=1, source_target_pairs={{0,240},{16,32},{32,16},{48,64},{64,48},{80,96},{96,80},{112,128},... | collective-permute-start | bytes 184328 | tf_op jit(solution)/shard_map/ppermute | solution.py:386
  6.3 2.3 %collective-permute-start.1 = (f32[5,16,192]{2,1,0:T(8,128)S(1)}, f32[5,16,192]{2,1,0:T(8,128)S(1)}, u32[]{:S(2)}, u32[]{:S(2)}) collective-permute-start(f32[5,16,192]{2,1,0:T(8,128)S(1)} %get-tuple-element.16), channel_id=1, source_target_pairs={{0,16},{16,0},{32,48},{48,32},{64,80},{80,64},{96,112},{112,96},{1... | collective-permute-start | bytes 184328 | tf_op jit(solution)/shard_map/ppermute | solution.py:386
  8.6 5.6 %collective-permute-start.2 = (f32[5,16,192]{2,1,0:T(8,128)S(1)}, f32[5,16,192]{2,1,0:T(8,128)S(1)}, u32[]{:S(2)}, u32[]{:S(2)}) collective-permute-start(f32[5,16,192]{2,1,0:T(8,128)S(1)} %get-tuple-element.17), channel_id=1, source_target_pairs={{0,15},{1,2},{2,1},{3,4},{4,3},{5,6},{6,5},{7,8},{8,7},{9,10},{10,... | collective-permute-start | bytes 184328 | tf_op jit(solution)/shard_map/ppermute | solution.py:386
  14.2 1.4 %interior_kernel.1 = (f32[3,16,16,192]{3,2,1,0:T(8,128)S(1)}, f32[16,16,192]{2,1,0:T(8,128)S(1)}) custom-call(f32[5,16,16,192]{3,2,1,0:T(8,128)S(1)} %copy-done, f32[5,16,16,192]{3,2,1,0:T(8,128)S(1)} %copy-done.2, s32[1,192]{1,0:T(1,128)S(1)} %bitcast.5, s32[16,16]{1,0:T(8,128)S(1)} %copy-done.8), custom_call_target="tpu_custom_call" | custom-call | flops 10000000 | bytes 1967872 | tf_op jit(solution)/shard_map/interior_kernel/pallas_call | solution.py:373
  15.6 1.4 %collective-permute-done.2.y_outer = f32[5,16,192]{2,1,0:T(8,128)S(1)} collective-permute-done((f32[5,16,192]{2,1,0:T(8,128)S(1)}, f32[5,16,192]{2,1,0:T(8,128)S(1)}, u32[]{:S(2)}, u32[]{:S(2)}) %collective-permute-start.2) | collective-permute-done | bytes 61472 | tf_op jit(solution)/shard_map/ppermute | solution.py:386
  17.0 1.5 %collective-permute-done.3.y_inner = f32[5,16,192]{2,1,0:T(8,128)S(1)} collective-permute-done((f32[5,16,192]{2,1,0:T(8,128)S(1)}, f32[5,16,192]{2,1,0:T(8,128)S(1)}, u32[]{:S(2)}, u32[]{:S(2)}) %collective-permute-start.3) | collective-permute-done | bytes 61472 | tf_op jit(solution)/shard_map/ppermute | solution.py:386
  18.5 0.9 momentum_kernel.1
  19.4 0.0 copy-start.1
  19.4 13.9 %all_to_all.20 = f32[16,16,256]{2,1,0:T(8,128)S(1)} all-to-all(f32[16,16,256]{2,1,0:T(8,128)S(1)} %momentum_kernel.1), channel_id=1, replica_groups=mesh['px'=16,'py'=16] {'px'}, dimensions={0} | all-to-all | bytes 524288 | tf_op jit(solution)/shard_map/all_to_all | solution.py:443
  33.3 1.5 %forward_kernel.1 = f32[256,1,256]{2,1,0:T(1,128)} custom-call(f32[256,256]{1,0:T(8,128)S(1)} %bitcast.4, f32[256,256]{1,0:T(8,128)S(1)} %copy-done.3), custom_call_target="tpu_custom_call" | custom-call | bytes 524288 | tf_op jit(solution)/shard_map/forward_kernel/pallas_call | solution.py:373
  34.8 6.1 %all-to-all-start.1 = ((f32[256,1,256]{2,1,0:T(1,128)}), f32[256,1,256]{2,1,0:T(1,128)S(1)}, u32[]{:S(2)}, u32[]{:S(2)}) async-start(f32[256,1,256]{2,1,0:T(1,128)} %forward_kernel.1), calls=%async_computation.1 | async-start | bytes 524288 | tf_op jit(solution)/shard_map/all_to_all | solution.py:447
  41.0 0.1 subtract_add_fusion.shift
  41.0 3.7 %side_kernel.1 = (f32[3,16,16,192]{3,2,1,0:T(8,128)S(1)}, f32[5,16,16,192]{3,2,1,0:T(8,128)}, f32[16,16,192]{2,1,0:T(8,128)S(1)}) custom-call(f32[5,16,16,192]{3,2,1,0:T(8,128)S(1)} %copy-done.1, f32[5,16,16,192]{3,2,1,0:T(8,128)S(1)} %copy-done.2, f32[5,16,192]{2,1,0:T(8,128)S(1)} %collective-permute-done.x_outer, ...), custom_call_target="tpu_custom_call" | custom-call | flops 20000000 | bytes 2213632 | tf_op jit(solution)/shard_map/side_kernel/pallas_call | solution.py:373
  44.7 0.9 copy-done.4
  45.6 0.7 copy-done.6
  46.3 10.5 %all-to-all-done.1.lines = f32[256,1,256]{2,1,0:T(1,128)S(1)} async-done(((f32[256,1,256]{2,1,0:T(1,128)}), f32[256,1,256]{2,1,0:T(1,128)S(1)}, u32[]{:S(2)}, u32[]{:S(2)}) %all-to-all-start.1) | async-done | bytes 262176 | tf_op jit(solution)/shard_map/all_to_all | solution.py:447
  56.9 2.5 %solve_kernel.1 = f32[256,1,256]{2,1,0:T(1,128)S(1)} custom-call(f32[256,1,256]{2,1,0:T(1,128)S(1)} %all-to-all-done.1.lines, f32[256,256]{1,0:T(8,128)S(1)} %copy-done.3, s32[1,192]{1,0:T(1,128)S(1)} %bitcast.8, f32[1,256]{1,0:T(1,128)S(1)} %subtract_add_fusion.shift), custom_call_target="tpu_custom_call" | custom-call | bytes 526080 | tf_op jit(solution)/shard_map/solve_kernel/pallas_call | solution.py:373
  59.3 20.4 %all_to_all.21.lines = f32[256,1,256]{2,1,0:T(1,128)S(1)} all-to-all(f32[256,1,256]{2,1,0:T(1,128)S(1)} %solve_kernel.1), channel_id=1, replica_groups=mesh['px'=16,'py'=16] {'py','px'}, dimensions={0} | all-to-all | bytes 524288 | tf_op jit(solution)/shard_map/all_to_all | solution.py:453
  79.7 0.8 backward_kernel.1
  80.5 11.8 %all_to_all.22.message = f32[16,16,256]{2,1,0:T(8,128)S(1)} all-to-all(f32[16,16,256]{2,1,0:T(8,128)S(1)} %bitcast.3), channel_id=1, replica_groups=mesh['px'=16,'py'=16] {'px'}, dimensions={0} | all-to-all | bytes 524288 | tf_op jit(solution)/shard_map/all_to_all | solution.py:457
  92.3 1.6 %correct_kernel.1 = (f32[5,16,16,192]{3,2,1,0:T(8,128)}, f32[16,16,192]{2,1,0:T(8,128)}) custom-call(f32[16,16,256]{2,1,0:T(8,128)S(1)} %all_to_all.22.message, f32[3,16,16,192]{3,2,1,0:T(8,128)S(1)} %copy-done.5, s32[1,192]{1,0:T(1,128)S(1)} %bitcast.9, f32[16,16,192]{2,1,0:T(8,128)S(1)} %copy-done.7, ...), custom_call_target="tpu_custom_call", output_to_operand_aliasing={{0}: (4, {})} | custom-call | bytes 2032384 | tf_op jit(solution)/shard_map/correct_kernel/pallas_call | solution.py:373
  (18 shorter events, 0.0 us)
Async XLA Ops:
  0.6 1.3 %copy-start = (f32[5,16,16,192]{3,2,1,0:T(8,128)S(1)}, f32[5,16,16,192]{3,2,1,0:T(8,128)}, u32[]{:S(2)}) copy-start(f32[5,16,16,192]{3,2,1,0:T(8,128)} %state.7) | copy-start | bytes 2949124
  1.9 12.3 %copy-start.2 = (f32[5,16,16,192]{3,2,1,0:T(8,128)S(1)}, f32[5,16,16,192]{3,2,1,0:T(8,128)}, u32[]{:S(2)}) copy-start(f32[5,16,16,192]{3,2,1,0:T(8,128)} %memory.3) | copy-start | bytes 2949124
  2.0 12.3 %copy-start.8 = (s32[16,16]{1,0:T(8,128)S(1)}, s32[16,16]{1,0:T(8,128)}, u32[]{:S(2)}) copy-start(s32[16,16]{1,0:T(8,128)} %height.3) | copy-start | bytes 3076
  2.0 12.3 %copy-start.9 = (s32[192]{0:T(256)S(1)}, s32[192]{0:T(256)}, u32[]{:S(2)}) copy-start(s32[192]{0:T(256)} %param.7) | copy-start | bytes 2308
  2.1 13.5 %collective-permute-start = (f32[5,16,192]{2,1,0:T(8,128)S(1)}, f32[5,16,192]{2,1,0:T(8,128)S(1)}, u32[]{:S(2)}, u32[]{:S(2)}) collective-permute-start(f32[5,16,192]{2,1,0:T(8,128)S(1)} %get-tuple-element.15), channel_id=1, source_target_pairs={{0,240},{16,32},{32,16},{48,64},{64,48},{80,96},{96,80},{112,128},... | collective-permute-start | bytes 184328 | tf_op jit(solution)/shard_map/ppermute | solution.py:386
  6.3 9.3 %collective-permute-start.1 = (f32[5,16,192]{2,1,0:T(8,128)S(1)}, f32[5,16,192]{2,1,0:T(8,128)S(1)}, u32[]{:S(2)}, u32[]{:S(2)}) collective-permute-start(f32[5,16,192]{2,1,0:T(8,128)S(1)} %get-tuple-element.16), channel_id=1, source_target_pairs={{0,16},{16,0},{32,48},{48,32},{64,80},{80,64},{96,112},{112,96},{1... | collective-permute-start | bytes 184328 | tf_op jit(solution)/shard_map/ppermute | solution.py:386
  8.6 8.4 %collective-permute-start.2 = (f32[5,16,192]{2,1,0:T(8,128)S(1)}, f32[5,16,192]{2,1,0:T(8,128)S(1)}, u32[]{:S(2)}, u32[]{:S(2)}) collective-permute-start(f32[5,16,192]{2,1,0:T(8,128)S(1)} %get-tuple-element.17), channel_id=1, source_target_pairs={{0,15},{1,2},{2,1},{3,4},{4,3},{5,6},{6,5},{7,8},{8,7},{9,10},{10,... | collective-permute-start | bytes 184328 | tf_op jit(solution)/shard_map/ppermute | solution.py:386
  14.2 4.3 %collective-permute-start.3 = (f32[5,16,192]{2,1,0:T(8,128)S(1)}, f32[5,16,192]{2,1,0:T(8,128)S(1)}, u32[]{:S(2)}, u32[]{:S(2)}) collective-permute-start(f32[5,16,192]{2,1,0:T(8,128)S(1)} %get-tuple-element.18), channel_id=1, source_target_pairs={{0,1},{1,0},{2,3},{3,2},{4,5},{5,4},{6,7},{7,6},{8,9},{9,8},{10,11... | collective-permute-start | bytes 184328 | tf_op jit(solution)/shard_map/ppermute | solution.py:386
  18.5 14.7 %copy-start.3 = (f32[256,256]{1,0:T(8,128)S(1)}, f32[256,256]{1,0:T(8,128)}, u32[]{:S(2)}) copy-start(f32[256,256]{1,0:T(8,128)} %constant.17.clone.basis) | copy-start | bytes 786436
  19.4 21.6 %copy-start.1 = (f32[5,16,16,192]{3,2,1,0:T(8,128)S(1)}, f32[5,16,16,192]{3,2,1,0:T(8,128)}, u32[]{:S(2)}) copy-start(f32[5,16,16,192]{3,2,1,0:T(8,128)} %state.7) | copy-start | bytes 2949124
  34.8 22.0 %all-to-all-start.1 = ((f32[256,1,256]{2,1,0:T(1,128)}), f32[256,1,256]{2,1,0:T(1,128)S(1)}, u32[]{:S(2)}, u32[]{:S(2)}) async-start(f32[256,1,256]{2,1,0:T(1,128)} %forward_kernel.1), calls=%async_computation.1 | async-start | bytes 524288 | tf_op jit(solution)/shard_map/all_to_all | solution.py:447
  44.7 0.9 copy-start.4
  45.6 0.7 copy-start.6
  56.9 35.5 %copy-start.5 = (f32[3,16,16,192]{3,2,1,0:T(8,128)S(1)}, f32[3,16,16,192]{3,2,1,0:T(8,128)}, u32[]{:S(2)}) copy-start(f32[3,16,16,192]{3,2,1,0:T(8,128)} %copy-done.4) | copy-start | bytes 1769476
  56.9 35.5 %copy-start.7 = (f32[16,16,192]{2,1,0:T(8,128)S(1)}, f32[16,16,192]{2,1,0:T(8,128)}, u32[]{:S(2)}) copy-start(f32[16,16,192]{2,1,0:T(8,128)} %copy-done.6) | copy-start | bytes 589828

commit v7 on v6

--- a/solution.py
+++ b/solution.py
@@ -18,10 +18,10 @@
 LEVELS = 192
 WIDE = 256
 CHUNK = LEVELS // TILE
+FIELDS = 5
 FIRST = 192
 SECOND = 208
 UNROLL = 3
-MOST_VMEM = 48 * 1024 * 1024
 STRIDES = (1, 2, 4, 8, 16, 32, 64, 128)
 
 
@@ -111,13 +111,11 @@
     return e * (DIFFUSION - 0.5 * u) - s * (DIFFUSION + 0.5 * u)
 
 
-def advance_fields(fields, state, memory, halos, level_steps, fluid, store):
+def advance_fields(state, memory, level_steps, fluid, store):
     thickness, spacing = level_rows(level_steps)
     inv_thick = 1.0 / thickness
     inv_space = 1.0 / spacing
     nothing = jnp.zeros((TILE, LEVELS), jnp.float32)
-    if halos:
-        west, east, south, north = halos
 
     def plane(x, before, east_of):
         u = state[0, x]
@@ -128,18 +126,14 @@
         w_to, w_from = DIFFUSION * inv_space - 0.5 * w, DIFFUSION * inv_space + 0.5 * w
         factor = (RK_STEP * TIME_STEP) * fluid[x]
         after = []
-        for i, f in enumerate(fields):
+        for f in range(FIELDS):
             s = state[f, x]
             x_face = east_of(f) * u_to - s * u_from if east_of else nothing
-            last_y, first_y = nothing[:1], nothing[:1]
-            if halos:
-                last_y = faces(s[TILE - 1 :], north[f, pl.ds(x, 1)], v[TILE - 1 :])
-                first_y = faces(south[f, pl.ds(x, 1)], s[:1], south[1, pl.ds(x, 1)])
             y_face = jnp.concatenate([s[1:], s[:1]], axis=0) * v_to - s * v_from
-            y_above = jnp.concatenate([y_face[:-1], last_y], axis=0)
-            y_below = jnp.concatenate([first_y, y_face[:-1]], axis=0)
+            y_above = jnp.concatenate([y_face[:-1], nothing[:1]], axis=0)
+            y_below = jnp.concatenate([nothing[:1], y_face[:-1]], axis=0)
             z_face = lanes_up(s) * w_to - s * w_from
-            change = (x_face - before[i]) + (y_above - y_below)
+            change = (x_face - before[f]) + (y_above - y_below)
             change = change + (z_face - lanes_down(z_face)) * inv_thick
             if f == 2:
                 change = change + BUOYANCY * state[3, x]
@@ -147,13 +141,11 @@
             store(f, x, s + (RK_STEP * RK_KEEP) * memory[f, x] + factor * change)
         return tuple(after)
 
-    before = tuple(
-        faces(west[f], state[f, 0], west[0]) if halos else nothing for f in fields
-    )
+    before = (nothing,) * FIELDS
     before = lax.fori_loop(
         0, TILE - 1, lambda x, b: plane(x, b, lambda f: state[f, x + 1]), before, unroll=UNROLL
     )
-    plane(TILE - 1, before, (lambda f: east[f]) if halos else None)
+    plane(TILE - 1, before, None)
 
 
 PART = 4
@@ -179,28 +171,36 @@
     def store(f, x, value):
         provisional[f, x] = value
 
-    advance_fields((0, 1, 2), state, memory, None, level_steps, fluid, store)
-
-
-def momentum_kernel(
-    state, inner, fluid, x_outer, x_inner, y_outer, y_inner, level_steps, message, provisional
-):
-    provisional[...] = inner[...]
+    advance_fields(state, memory, level_steps, fluid, store)
+
+
+def sides(field, x_outer, x_inner, y_outer, y_inner):
     odd_x, odd_y = odd("px"), odd("py")
-    west = [jnp.where(odd_x, x_inner[f], x_outer[f]) for f in range(3)]
-    east = [jnp.where(odd_x, x_outer[f], x_inner[f]) for f in range(3)]
-    south = [jnp.where(odd_y, y_inner[f], y_outer[f]) for f in range(3)]
-    north = [jnp.where(odd_y, y_outer[f], y_inner[f]) for f in range(3)]
+    return (
+        jnp.where(odd_x, x_inner[field], x_outer[field]),
+        jnp.where(odd_x, x_outer[field], x_inner[field]),
+        jnp.where(odd_y, y_inner[field], y_outer[field]),
+        jnp.where(odd_y, y_outer[field], y_inner[field]),
+    )
+
+
+def add_outer_faces(total, target, edges, halos, fluid):
     last, factor = TILE - 1, RK_STEP * TIME_STEP
-    for f in range(3):
-        provisional[f, 0] -= factor * fluid[0] * faces(west[f], state[f, 0], west[0])
-        provisional[f, last] += factor * fluid[last] * faces(
-            state[f, last], east[f], state[0, last]
-        )
-        provisional[f, :, 0] -= factor * fluid[:, 0] * faces(south[f], state[f, :, 0], south[1])
-        provisional[f, :, last] += factor * fluid[:, last] * faces(
-            state[f, :, last], north[f], state[1, :, last]
-        )
+    west_u, south_v = sides(0, *halos)[0], sides(1, *halos)[2]
+    east_u, north_v = sides(0, *edges)[1], sides(1, *edges)[3]
+    for f in range(total):
+        x_low, x_high, y_low, y_high = sides(f, *edges)
+        west, east, south, north = sides(f, *halos)
+        target[f, 0] -= factor * fluid[0] * faces(west, x_low, west_u)
+        target[f, last] += factor * fluid[last] * faces(x_high, east, east_u)
+        target[f, :, 0] -= factor * fluid[:, 0] * faces(south, y_low, south_v)
+        target[f, :, last] += factor * fluid[:, last] * faces(y_high, north, north_v)
+
+
+def momentum_kernel(inner, fluid, *rest):
+    edges, halos, (level_steps, message, provisional) = rest[:4], rest[4:8], rest[8:]
+    provisional[...] = inner[0:3]
+    add_outer_faces(3, provisional, edges, halos, fluid)
     inv_thick = 1.0 / level_rows(level_steps)[0]
     zeros = jnp.zeros((TILE, WIDE - LEVELS), jnp.float32)
     mask = block_mask()
@@ -280,33 +280,6 @@
         if shared > stride:
             coupling = low(-from_above * coupling[stride:])
     return right / diagonal
-
-
-def side_kernel(
-    state, memory, x_outer, x_inner, y_outer, y_inner, level_steps, height,
-    provisional, updated, fluid_kept, state_here, memory_here, halo_here, fluid, fields, sems,
-):
-    pairs = [(state, state_here), (memory, memory_here)]
-    first_x, first_y = odd("px").astype(jnp.int32), odd("py").astype(jnp.int32)
-    pairs += [(x_outer, halo_here.at[first_x]), (x_inner, halo_here.at[1 - first_x])]
-    pairs += [(y_outer, halo_here.at[2 + first_y]), (y_inner, halo_here.at[3 - first_y])]
-    arriving = loaded(pairs, sems)
-    fill_fluid(height, fluid)
-    leaving = loaded([(fluid, fluid_kept)], sems.at[pl.ds(6, 1)])
-    for copy in arriving:
-        copy.wait()
-
-    def store(f, x, value):
-        fields[f, x] = value
-
-    advance_fields(
-        (0, 1, 2, 3, 4), state_here, memory_here, [halo_here.at[i] for i in range(4)],
-        level_steps, fluid, store,
-    )
-    pairs = [(fields.at[0:3], provisional), (fields.at[3:5], updated.at[3:5])]
-    leaving += loaded(pairs, sems.at[pl.ds(7, 2)])
-    for copy in leaving:
-        copy.wait()
 
 
 def solve_kernel(lines, basis, level_steps, shift, result, tiled):
@@ -335,10 +308,12 @@
     message[:, 128:] = back[:, 128:] + repacked(back, SECOND)
 
 
-def correct_kernel(
-    message, provisional, level_steps, fluid, kept, updated, pressure, fields, cells, sems
-):
-    copies = []
+def correct_kernel(message, inner, fluid, *rest):
+    edges, halos, level_steps = rest[:4], rest[4:8], rest[8]
+    updated, pressure, fields, cells, sems = rest[9:]
+    fields[...] = inner[...]
+    add_outer_faces(FIELDS, fields, edges, halos, fluid)
+    copies = loaded([(fields.at[3:5], updated.at[3:5])], sems.at[pl.ds(2 * TILE // PART, 1)])
     inv_space = 1.0 / level_rows(level_steps)[1]
     lines = message[...].reshape(LINE, WIDE)
     north = unpacked(lines, FIRST, "high")[:, :LEVELS]
@@ -349,13 +324,13 @@
         p_north = jnp.concatenate([p[1:], north[x : x + 1]], axis=0)
         p_upper = jnp.concatenate([p[:, 1:], jnp.zeros_like(p[:, :1])], axis=1)
         open_cell = fluid[x]
-        fields[0, x] = open_cell * (provisional[0, x] - (p_east - p))
-        fields[1, x] = open_cell * (provisional[1, x] - (p_north - p))
-        fields[2, x] = open_cell * (provisional[2, x] - (p_upper - p) * inv_space)
+        fields[0, x] = open_cell * (fields[0, x] - (p_east - p))
+        fields[1, x] = open_cell * (fields[1, x] - (p_north - p))
+        fields[2, x] = open_cell * (fields[2, x] - (p_upper - p) * inv_space)
         cells[x] = p
         part = parts_of(x)
         if part is not None:
-            pairs = [(fields.at[:, part], updated.at[0:3, part]), (cells.at[part], pressure.at[part])]
+            pairs = [(fields.at[0:3, part], updated.at[0:3, part]), (cells.at[part], pressure.at[part])]
             copies += loaded(pairs, sems.at[pl.ds(x // PART * 2, 2)])
     for copy in copies:
         copy.wait()
@@ -365,7 +340,7 @@
     return jax.ShapeDtypeStruct(shape, jnp.float32)
 
 
-def call(kernel, out_shape, *operands, flops=0, vmem=12 * 1024 * 1024, **options):
+def call(kernel, out_shape, *operands, flops=0, **options):
     here = pl.BlockSpec(memory_space=pltpu.VMEM)
     options.setdefault("in_specs", [here] * len(operands))
     options.setdefault("out_specs", jax.tree.map(lambda _: here, out_shape))
@@ -374,7 +349,7 @@
         kernel,
         out_shape=out_shape,
         name=kernel.__name__,
-        compiler_params=pltpu.CompilerParams(vmem_limit_bytes=vmem),
+        compiler_params=pltpu.CompilerParams(vmem_limit_bytes=12 * 1024 * 1024),
         cost_estimate=pl.CostEstimate(flops=flops, bytes_accessed=count, transcendentals=0),
         **options,
     )(*operands)
@@ -402,52 +377,31 @@
     own_x = lax.axis_index("py") * lax.axis_size("px") + lax.axis_index("px")
     shift = eigenvalues(jnp.arange(LINE, dtype=jnp.int32)) + eigenvalues(own_x)
     basis = jnp.asarray(BASIS)
-    vmem, hbm = pl.BlockSpec(memory_space=pltpu.VMEM), pl.BlockSpec(memory_space=pltpu.HBM)
+    hbm = pl.BlockSpec(memory_space=pltpu.HBM)
     scratch = lambda *shape: pltpu.VMEM(shape, jnp.float32)
     sems = pltpu.SemaphoreType.DMA
 
     inner, fluid = call(
         interior_kernel,
-        [shaped(3, TILE, TILE, LEVELS), shaped(TILE, TILE, LEVELS)],
+        [shaped(FIELDS, TILE, TILE, LEVELS), shaped(TILE, TILE, LEVELS)],
         state, memory, steps, building_height,
         flops=10**7,
     )
+    inner, shift = lax.optimization_barrier((inner, shift.reshape(1, LINE)))
     message = call(
         momentum_kernel,
         shaped(TILE, TILE, WIDE),
-        state, inner, fluid, *halos, steps,
+        inner, fluid, *edges, *halos, steps,
         flops=10**7,
         scratch_shapes=[scratch(3, TILE, TILE, LEVELS)],
-    )
-    provisional, updated, fluid = call(
-        side_kernel,
-        [
-            shaped(3, TILE, TILE, LEVELS),
-            shaped(5, TILE, TILE, LEVELS),
-            shaped(TILE, TILE, LEVELS),
-        ],
-        state, memory, *halos, steps, building_height,
-        flops=2 * 10**7,
-        vmem=MOST_VMEM,
-        in_specs=[hbm] * 6 + [vmem] * 2,
-        out_specs=[hbm] * 3,
-        scratch_shapes=[
-            scratch(5, TILE, TILE, LEVELS),
-            scratch(5, TILE, TILE, LEVELS),
-            scratch(4, 5, TILE, LEVELS),
-            scratch(TILE, TILE, LEVELS),
-            scratch(5, TILE, TILE, LEVELS),
-            sems((9,)),
-        ],
     )
     lines = lax.all_to_all(message, "px", split_axis=0, concat_axis=0, tiled=True)
     spectrum = call(
         forward_kernel, shaped(LINE, 1, WIDE), lines.reshape(LINE, WIDE), basis
     )
     lines = lax.all_to_all(spectrum, ("py", "px"), split_axis=0, concat_axis=0, tiled=True)
-    lines, provisional = lax.optimization_barrier((lines, provisional))
     solved = call(
-        solve_kernel, shaped(LINE, 1, WIDE), lines, basis, steps, shift.reshape(1, LINE),
+        solve_kernel, shaped(LINE, 1, WIDE), lines, basis, steps, shift,
         scratch_shapes=[scratch(LINE, WIDE)],
     )
     lines = lax.all_to_all(solved, ("py", "px"), split_axis=0, concat_axis=0, tiled=True)
@@ -460,12 +414,12 @@
     return call(
         correct_kernel,
         [shaped(5, TILE, TILE, LEVELS), shaped(TILE, TILE, LEVELS)],
-        message, provisional, steps, fluid, updated,
-        in_specs=[vmem] * 4 + [hbm],
+        message, inner, fluid, *edges, *halos, steps,
         out_specs=[hbm] * 2,
-        input_output_aliases={4: 0},
         scratch_shapes=[
-            scratch(3, TILE, TILE, LEVELS), scratch(TILE, TILE, LEVELS), sems((2 * TILE // PART,))
+            scratch(FIELDS, TILE, TILE, LEVELS),
+            scratch(TILE, TILE, LEVELS),
+            sems((2 * TILE // PART + 1,)),
         ],
     )
 

time: 94.2 us -> 93.5 us (level)
  blocking collectives: 46 us -> 67.7 us
  waiting for transfers between devices: 13.5 us -> 1.01 us
  starting transfers between devices: 18.2 us -> 12.1 us
  Pallas kernels: 12.5 us -> 8.89 us
    all_to_all x0 -> x1, blocking collectives: none -> 21.7 us  [per_device(): lax.all_to_all(spectrum, ('py', 'px'), split_axis=0, concat_axis=0, tiled...]
    all_to_all x1 -> x0, waiting for transfers between devices: 10.5 us -> none  [per_device(): lax.all_to_all(spectrum, ('py', 'px'), split_axis=0, concat_axis=0, tiled...]
    all_to_all x1 -> x0, starting transfers between devices: 6.05 us -> none  [per_device(): lax.all_to_all(spectrum, ('py', 'px'), split_axis=0, concat_axis=0, tiled...]
    pallas_call x8 -> x7, Pallas kernels: 12.5 us -> 8.89 us  [call(): pl.pallas_call(kernel, out_shape=out_shape, name=kernel.__name__, compile...]
    ppermute x4, waiting for transfers between devices: 2.94 us -> 1.01 us  [swapped(): lax.ppermute(block, axis, [(i, p % count) for i, p in enumerate(partner)])]
    unnamed x20 -> x12, local copies, waits for them, and re-layouts: 2.93 us -> 2.64 us
  transfers between devices with their start and end apart: 5 -> 4, of which waited for: 3 -> 1; matrix products, arithmetic and copies ran while one was open for 0% -> 0% of each run, Pallas kernels for 5% -> 2%
where the time goes in v7:
time: 93.5 us; the launch traced here: 93.2 us
  blocking collectives  67.7 us (72%)
  starting transfers between devices  12.1 us (13%)
  Pallas kernels  8.89 us (10%)
  local copies, waits for them, and re-layouts  2.64 us (3%)
  waiting for transfers between devices  1.01 us (1%)
    all_to_all x1, blocking collectives, per_device(): lax.all_to_all(spectrum, ('py', 'px'), split_axis=0, concat_axis=0, tiled...  21.7 us
    all_to_all x1, blocking collectives, per_device(): lax.all_to_all(solved, ('py', 'px'), split_axis=0, concat_axis=0, tiled=T...  20.4 us
    all_to_all x1, blocking collectives, per_device(): lax.all_to_all(message, 'px', split_axis=0, concat_axis=0, tiled=True)  13.7 us
    ppermute x4, starting transfers between devices, swapped(): lax.ppermute(block, axis, [(i, p % count) for i, p in enumerate(partner)])  12.1 us
    all_to_all x1, blocking collectives, per_device(): lax.all_to_all(message.reshape(TILE, TILE, WIDE), 'px', split_axis=0, con...  11.8 us
    pallas_call x7, Pallas kernels, call(): pl.pallas_call(kernel, out_shape=out_shape, name=kernel.__name__, compile...  8.89 us
    unnamed x12, local copies, waits for them, and re-layouts  2.64 us
  transfers between devices with their start and end apart: 4, of which 1 were waited for; matrix products, arithmetic and copies ran while one was open for 0% of the time, Pallas kernels for 2%

profile of v7, /device:TPU:1, one launch (start us, length us, event | category | flops | bytes accessed | tf_op | source)
XLA Modules:
  0.0 93.2 jit_solution(6646533574473077755)
XLA Ops:
  0.6 0.0 copy-start
  0.6 1.3 %copy-done = f32[5,16,16,192]{3,2,1,0:T(8,128)S(1)} copy-done((f32[5,16,16,192]{3,2,1,0:T(8,128)S(1)}, f32[5,16,16,192]{3,2,1,0:T(8,128)}, u32[]{:S(2)}) %copy-start) | copy-done | bytes 983064
  2.0 0.1 edges_kernel.1
  2.1 4.2 %collective-permute-start = (f32[5,16,192]{2,1,0:T(8,128)S(1)}, f32[5,16,192]{2,1,0:T(8,128)S(1)}, u32[]{:S(2)}, u32[]{:S(2)}) collective-permute-start(f32[5,16,192]{2,1,0:T(8,128)S(1)} %get-tuple-element.13.rest_0_), channel_id=1, source_target_pairs={{0,240},{16,32},{32,16},{48,64},{64,48},{80,96},{96,80},{112,128},... | collective-permute-start | bytes 184328 | tf_op jit(solution)/shard_map/ppermute | solution.py:361
  6.3 2.3 %collective-permute-start.1 = (f32[5,16,192]{2,1,0:T(8,128)S(1)}, f32[5,16,192]{2,1,0:T(8,128)S(1)}, u32[]{:S(2)}, u32[]{:S(2)}) collective-permute-start(f32[5,16,192]{2,1,0:T(8,128)S(1)} %get-tuple-element.14.rest_1_), channel_id=1, source_target_pairs={{0,16},{16,0},{32,48},{48,32},{64,80},{80,64},{96,112},{112,96},{1... | collective-permute-start | bytes 184328 | tf_op jit(solution)/shard_map/ppermute | solution.py:361
  8.6 5.6 %collective-permute-start.2 = (f32[5,16,192]{2,1,0:T(8,128)S(1)}, f32[5,16,192]{2,1,0:T(8,128)S(1)}, u32[]{:S(2)}, u32[]{:S(2)}) collective-permute-start(f32[5,16,192]{2,1,0:T(8,128)S(1)} %get-tuple-element.15.rest_2_), channel_id=1, source_target_pairs={{0,15},{1,2},{2,1},{3,4},{4,3},{5,6},{6,5},{7,8},{8,7},{9,10},{10,... | collective-permute-start | bytes 184328 | tf_op jit(solution)/shard_map/ppermute | solution.py:361
  14.2 0.0 collective-permute-start.3
  14.3 0.0 copy-start.3
  14.3 1.3 %copy-done.3 = f32[5,16,16,192]{3,2,1,0:T(8,128)S(1)} copy-done((f32[5,16,16,192]{3,2,1,0:T(8,128)S(1)}, f32[5,16,16,192]{3,2,1,0:T(8,128)}, u32[]{:S(2)}) %copy-start.3) | copy-done | bytes 983064
  15.6 1.8 %interior_kernel.1 = (f32[5,16,16,192]{3,2,1,0:T(8,128)S(1)}, f32[16,16,192]{2,1,0:T(8,128)S(1)}) custom-call(f32[5,16,16,192]{3,2,1,0:T(8,128)S(1)} %copy-done.1, f32[5,16,16,192]{3,2,1,0:T(8,128)S(1)} %copy-done.3, s32[1,192]{1,0:T(1,128)S(1)} %bitcast.5, s32[16,16]{1,0:T(8,128)S(1)} %copy-done.5), custom_call_target="tpu_custom_call" | custom-call | flops 10000000 | bytes 1967872 | tf_op jit(solution)/shard_map/interior_kernel/pallas_call | solution.py:348
  17.5 0.1 subtract_add_fusion.shift
  17.5 0.0 collective-permute-done.rest_4_
  17.5 0.0 collective-permute-done.1.rest_5_
  17.5 0.0 collective-permute-done.2.rest_6_
  17.5 1.0 %collective-permute-done.3.rest_7_ = f32[5,16,192]{2,1,0:T(8,128)S(1)} collective-permute-done((f32[5,16,192]{2,1,0:T(8,128)S(1)}, f32[5,16,192]{2,1,0:T(8,128)S(1)}, u32[]{:S(2)}, u32[]{:S(2)}) %collective-permute-start.3) | collective-permute-done | bytes 61472 | tf_op jit(solution)/shard_map/ppermute | solution.py:361
  18.5 0.8 momentum_kernel.1
  19.4 13.7 %all_to_all.20 = f32[16,16,256]{2,1,0:T(8,128)S(1)} all-to-all(f32[16,16,256]{2,1,0:T(8,128)S(1)} %momentum_kernel.1), channel_id=1, replica_groups=mesh['px'=16,'py'=16] {'px'}, dimensions={0} | all-to-all | bytes 524288 | tf_op jit(solution)/shard_map/all_to_all | solution.py:398
  33.1 0.8 forward_kernel.1
  33.9 21.7 %all_to_all.21.lines = f32[256,1,256]{2,1,0:T(1,128)S(1)} all-to-all(f32[256,1,256]{2,1,0:T(1,128)S(1)} %forward_kernel.1), channel_id=1, replica_groups=mesh['px'=16,'py'=16] {'py','px'}, dimensions={0} | all-to-all | bytes 524288 | tf_op jit(solution)/shard_map/all_to_all | solution.py:402
  55.7 2.5 %solve_kernel.1 = f32[256,1,256]{2,1,0:T(1,128)S(1)} custom-call(f32[256,1,256]{2,1,0:T(1,128)S(1)} %all_to_all.21.lines, f32[256,256]{1,0:T(8,128)S(1)} %copy-done.2, s32[1,192]{1,0:T(1,128)S(1)} %bitcast.7, f32[1,256]{1,0:T(1,128)S(1)} %subtract_add_fusion.shift), custom_call_target="tpu_custom_call" | custom-call | bytes 526080 | tf_op jit(solution)/shard_map/solve_kernel/pallas_call | solution.py:348
  58.1 20.4 %all_to_all.22.lines = f32[256,1,256]{2,1,0:T(1,128)S(1)} all-to-all(f32[256,1,256]{2,1,0:T(1,128)S(1)} %solve_kernel.1), channel_id=1, replica_groups=mesh['px'=16,'py'=16] {'py','px'}, dimensions={0} | all-to-all | bytes 524288 | tf_op jit(solution)/shard_map/all_to_all | solution.py:407
  78.6 0.8 backward_kernel.1
  79.4 11.8 %all_to_all.23.message = f32[16,16,256]{2,1,0:T(8,128)S(1)} all-to-all(f32[16,16,256]{2,1,0:T(8,128)S(1)} %bitcast.3), channel_id=1, replica_groups=mesh['px'=16,'py'=16] {'px'}, dimensions={0} | all-to-all | bytes 524288 | tf_op jit(solution)/shard_map/all_to_all | solution.py:411
  91.2 2.0 %correct_kernel.1 = (f32[5,16,16,192]{3,2,1,0:T(8,128)}, f32[16,16,192]{2,1,0:T(8,128)}) custom-call(f32[16,16,256]{2,1,0:T(8,128)S(1)} %all_to_all.23.message, f32[5,16,16,192]{3,2,1,0:T(8,128)S(1)} %get-tuple-element.11.inner, f32[16,16,192]{2,1,0:T(8,128)S(1)} %get-tuple-element.12.fluid, f32[5,16,192]{2,1,0:T(8,128)S(1)} %get-tuple-element.13.rest_0_, ...), custom_call_target="tpu_custom_call" | custom-call | bytes 1934080 | tf_op jit(solution)/shard_map/correct_kernel/pallas_call | solution.py:348
  (8 shorter events, 0.0 us)
Async XLA Ops:
  0.6 1.3 %copy-start = (f32[5,16,16,192]{3,2,1,0:T(8,128)S(1)}, f32[5,16,16,192]{3,2,1,0:T(8,128)}, u32[]{:S(2)}) copy-start(f32[5,16,16,192]{3,2,1,0:T(8,128)} %state.3) | copy-start | bytes 2949124
  1.9 12.3 %copy-start.1 = (f32[5,16,16,192]{3,2,1,0:T(8,128)S(1)}, f32[5,16,16,192]{3,2,1,0:T(8,128)}, u32[]{:S(2)}) copy-start(f32[5,16,16,192]{3,2,1,0:T(8,128)} %state.3) | copy-start | bytes 2949124
  1.9 12.4 %copy-start.4 = (s32[192]{0:T(256)S(1)}, s32[192]{0:T(256)}, u32[]{:S(2)}) copy-start(s32[192]{0:T(256)} %param.7) | copy-start | bytes 2308
  2.0 12.4 %copy-start.5 = (s32[16,16]{1,0:T(8,128)S(1)}, s32[16,16]{1,0:T(8,128)}, u32[]{:S(2)}) copy-start(s32[16,16]{1,0:T(8,128)} %height.1) | copy-start | bytes 3076
  2.1 15.4 %collective-permute-start = (f32[5,16,192]{2,1,0:T(8,128)S(1)}, f32[5,16,192]{2,1,0:T(8,128)S(1)}, u32[]{:S(2)}, u32[]{:S(2)}) collective-permute-start(f32[5,16,192]{2,1,0:T(8,128)S(1)} %get-tuple-element.13.rest_0_), channel_id=1, source_target_pairs={{0,240},{16,32},{32,16},{48,64},{64,48},{80,96},{96,80},{112,128},... | collective-permute-start | bytes 184328 | tf_op jit(solution)/shard_map/ppermute | solution.py:361
  6.3 11.2 %collective-permute-start.1 = (f32[5,16,192]{2,1,0:T(8,128)S(1)}, f32[5,16,192]{2,1,0:T(8,128)S(1)}, u32[]{:S(2)}, u32[]{:S(2)}) collective-permute-start(f32[5,16,192]{2,1,0:T(8,128)S(1)} %get-tuple-element.14.rest_1_), channel_id=1, source_target_pairs={{0,16},{16,0},{32,48},{48,32},{64,80},{80,64},{96,112},{112,96},{1... | collective-permute-start | bytes 184328 | tf_op jit(solution)/shard_map/ppermute | solution.py:361
  8.6 8.9 %collective-permute-start.2 = (f32[5,16,192]{2,1,0:T(8,128)S(1)}, f32[5,16,192]{2,1,0:T(8,128)S(1)}, u32[]{:S(2)}, u32[]{:S(2)}) collective-permute-start(f32[5,16,192]{2,1,0:T(8,128)S(1)} %get-tuple-element.15.rest_2_), channel_id=1, source_target_pairs={{0,15},{1,2},{2,1},{3,4},{4,3},{5,6},{6,5},{7,8},{8,7},{9,10},{10,... | collective-permute-start | bytes 184328 | tf_op jit(solution)/shard_map/ppermute | solution.py:361
  14.2 4.3 %collective-permute-start.3 = (f32[5,16,192]{2,1,0:T(8,128)S(1)}, f32[5,16,192]{2,1,0:T(8,128)S(1)}, u32[]{:S(2)}, u32[]{:S(2)}) collective-permute-start(f32[5,16,192]{2,1,0:T(8,128)S(1)} %get-tuple-element.16.rest_3_), channel_id=1, source_target_pairs={{0,1},{1,0},{2,3},{3,2},{4,5},{5,4},{6,7},{7,6},{8,9},{9,8},{10,11... | collective-permute-start | bytes 184328 | tf_op jit(solution)/shard_map/ppermute | solution.py:361
  14.3 1.3 %copy-start.3 = (f32[5,16,16,192]{3,2,1,0:T(8,128)S(1)}, f32[5,16,16,192]{3,2,1,0:T(8,128)}, u32[]{:S(2)}) copy-start(f32[5,16,16,192]{3,2,1,0:T(8,128)} %memory.1) | copy-start | bytes 2949124
  18.5 14.6 %copy-start.2 = (f32[256,256]{1,0:T(8,128)S(1)}, f32[256,256]{1,0:T(8,128)}, u32[]{:S(2)}) copy-start(f32[256,256]{1,0:T(8,128)} %constant.17.clone.basis) | copy-start | bytes 786436

commit v8 on v7

--- a/solution.py
+++ b/solution.py
@@ -22,7 +22,6 @@
 FIRST = 192
 SECOND = 208
 UNROLL = 3
-STRIDES = (1, 2, 4, 8, 16, 32, 64, 128)
 
 
 def table():
@@ -259,15 +258,53 @@
     spectrum[:, 0, :] = product(basis[...], lessened(lines[...], FIRST))
 
 
-def column_of(row):
-    shape = (LEVELS, LEVELS)
-    own = lax.broadcasted_iota(jnp.int32, shape, 0) == lax.broadcasted_iota(jnp.int32, shape, 1)
+def column_of(row, first):
+    shape = (LEVELS // 2, LEVELS)
+    level = 2 * lax.broadcasted_iota(jnp.int32, shape, 0) + first
+    own = level == lax.broadcasted_iota(jnp.int32, shape, 1)
     return jnp.sum(jnp.where(own, row, 0.0), axis=1, keepdims=True)
 
 
+def joined(ref, rows=slice(None)):
+    return jnp.concatenate([ref[0, rows, :], ref[1, rows, :]], axis=1)
+
+
+def keep(ref, rows, value):
+    ref[0, rows, :] = value[:, :128]
+    ref[1, rows, :] = value[:, 128:]
+
+
+def even_odd(ref, levels):
+    return [joined(ref, pl.ds(first, levels // 2, stride=2)) for first in (0, 1)]
+
+
+def without_odd(diagonals, couplings, rights):
+    (diagonal, odd_diagonal), (coupling, odd_coupling) = diagonals, couplings
+    right, odd_right = rights
+    inverse = 1.0 / odd_diagonal
+    below, above = coupling * inverse, odd_coupling * inverse
+    shifted = lambda a: jnp.concatenate([jnp.zeros_like(a[:1]), a[:-1]], axis=0)
+    left = (
+        diagonal - coupling * below - shifted(odd_coupling * above),
+        -below * odd_coupling,
+        right - below * odd_right - shifted(above * odd_right),
+    )
+    return left, (inverse * odd_right, below, above)
+
+
+def put_back(even, rest, ref):
+    own, below, above = rest
+    next_even = jnp.concatenate([even[1:], jnp.zeros_like(even[:1])], axis=0)
+    count = even.shape[0]
+    keep(ref, pl.ds(0, count, stride=2), even)
+    keep(ref, pl.ds(1, count, stride=2), own - below * even - above * next_even)
+
+
 def reduced(diagonal, coupling, right):
-    for stride in STRIDES:
-        shared = LEVELS - stride
+    levels = right.shape[0]
+    stride = 1
+    while stride < levels:
+        shared = levels - stride
         reciprocal = 1.0 / diagonal
         near = coupling[:shared]
         from_above = near * reciprocal[stride:]
@@ -279,24 +316,31 @@
         diagonal = diagonal - low(near * from_above) - high(near * from_below)
         if shared > stride:
             coupling = low(-from_above * coupling[stride:])
+        stride *= 2
     return right / diagonal
 
 
-def solve_kernel(lines, basis, level_steps, shift, result, tiled):
+def solve_kernel(lines, basis, level_steps, shift, result, tiled, solved, *half):
     tiled[...] = lines[:, 0, :]
     thickness, spacing = level_rows(level_steps)
     level = lax.broadcasted_iota(jnp.int32, (1, LEVELS), 1)
     inv_space = 1.0 / spacing
-    thick = column_of(thickness)
-    diagonal = column_of(inv_space + lanes_down(inv_space)) + thick * shift[...]
-    between = column_of(jnp.where(level < LEVELS - 1, -inv_space, 0.0))
-    coupling = jnp.broadcast_to(between, (LEVELS, LINE))
+    middle = inv_space + lanes_down(inv_space)
+    between = jnp.where(level < LEVELS - 1, -inv_space, 0.0)
+    thick = [column_of(thickness, first) for first in (0, 1)]
+    diagonals = [column_of(middle, first) + thick[first] * shift[...] for first in (0, 1)]
+    couplings = [column_of(between, first) for first in (0, 1)]
     values = lessened(tiled[...], SECOND)
-    main = product(values, basis[...], ((0,), (0,)))
-    right = thick * (-main[:LEVELS])
-    solved = reduced(diagonal, coupling, right)
-    solved = jnp.concatenate([solved, jnp.zeros((WIDE - LEVELS, LINE), jnp.float32)], axis=0)
-    back = product(basis[...], solved, ((1,), (1,)))
+    keep(solved, slice(None), product(values, basis[...], ((0,), (0,))))
+    rights = [-t * part for t, part in zip(thick, even_odd(solved, LEVELS))]
+    left, rest = without_odd(diagonals, couplings, rights)
+    for ref, value in zip(half, left):
+        keep(ref, slice(None), value)
+    left, rest_of_half = without_odd(*[even_odd(ref, LEVELS // 2) for ref in half])
+    put_back(reduced(*left), rest_of_half, half[0])
+    put_back(joined(half[0]), rest, solved)
+    keep(solved, slice(LEVELS, WIDE), jnp.zeros((WIDE - LEVELS, LINE), jnp.float32))
+    back = product(basis[...], joined(solved), ((1,), (1,)))
     result[:, 0, :128] = back[:, :128]
     result[:, 0, 128:] = back[:, 128:] + repacked(back, FIRST)
 
@@ -402,7 +446,8 @@
     lines = lax.all_to_all(spectrum, ("py", "px"), split_axis=0, concat_axis=0, tiled=True)
     solved = call(
         solve_kernel, shaped(LINE, 1, WIDE), lines, basis, steps, shift,
-        scratch_shapes=[scratch(LINE, WIDE)],
+        scratch_shapes=[scratch(LINE, WIDE), scratch(2, WIDE, 128)]
+        + [scratch(2, LEVELS // 2, 128)] * 3,
     )
     lines = lax.all_to_all(solved, ("py", "px"), split_axis=0, concat_axis=0, tiled=True)
     message = call(

time: 93.5 us -> 93 us (level)
  no operation moved by 1% of the time
where the time goes in v8:
time: 93 us; the launch traced here: 92.8 us
  blocking collectives  67.7 us (73%)
  starting transfers between devices  12.1 us (13%)
  Pallas kernels  8.44 us (9%)
  local copies, waits for them, and re-layouts  2.64 us (3%)
  waiting for transfers between devices  1.01 us (1%)
    all_to_all x1, blocking collectives, per_device(): lax.all_to_all(spectrum, ('py', 'px'), split_axis=0, concat_axis=0, tiled...  21.7 us
    all_to_all x1, blocking collectives, per_device(): lax.all_to_all(solved, ('py', 'px'), split_axis=0, concat_axis=0, tiled=T...  20.4 us
    all_to_all x1, blocking collectives, per_device(): lax.all_to_all(message, 'px', split_axis=0, concat_axis=0, tiled=True)  13.7 us
    ppermute x4, starting transfers between devices, swapped(): lax.ppermute(block, axis, [(i, p % count) for i, p in enumerate(partner)])  12.1 us
    all_to_all x1, blocking collectives, per_device(): lax.all_to_all(message.reshape(TILE, TILE, WIDE), 'px', split_axis=0, con...  11.8 us
    pallas_call x7, Pallas kernels, call(): pl.pallas_call(kernel, out_shape=out_shape, name=kernel.__name__, compile...  8.44 us
    unnamed x12, local copies, waits for them, and re-layouts  2.64 us
  transfers between devices with their start and end apart: 4, of which 1 were waited for; matrix products, arithmetic and copies ran while one was open for 0% of the time, Pallas kernels for 2%

profile of v8, /device:TPU:1, one launch (start us, length us, event | category | flops | bytes accessed | tf_op | source)
XLA Modules:
  0.0 92.8 jit_solution(6325906227730953330)
XLA Ops:
  0.6 1.3 %copy-done = f32[5,16,16,192]{3,2,1,0:T(8,128)S(1)} copy-done((f32[5,16,16,192]{3,2,1,0:T(8,128)S(1)}, f32[5,16,16,192]{3,2,1,0:T(8,128)}, u32[]{:S(2)}) %copy-start) | copy-done | bytes 983064
  2.0 0.1 edges_kernel.1
  2.1 4.2 %collective-permute-start = (f32[5,16,192]{2,1,0:T(8,128)S(1)}, f32[5,16,192]{2,1,0:T(8,128)S(1)}, u32[]{:S(2)}, u32[]{:S(2)}) collective-permute-start(f32[5,16,192]{2,1,0:T(8,128)S(1)} %get-tuple-element.13.rest_0_), channel_id=1, source_target_pairs={{0,240},{16,32},{32,16},{48,64},{64,48},{80,96},{96,80},{112,128},... | collective-permute-start | bytes 184328 | tf_op jit(solution)/shard_map/ppermute | solution.py:405
  6.3 2.3 %collective-permute-start.1 = (f32[5,16,192]{2,1,0:T(8,128)S(1)}, f32[5,16,192]{2,1,0:T(8,128)S(1)}, u32[]{:S(2)}, u32[]{:S(2)}) collective-permute-start(f32[5,16,192]{2,1,0:T(8,128)S(1)} %get-tuple-element.14.rest_1_), channel_id=1, source_target_pairs={{0,16},{16,0},{32,48},{48,32},{64,80},{80,64},{96,112},{112,96},{1... | collective-permute-start | bytes 184328 | tf_op jit(solution)/shard_map/ppermute | solution.py:405
  8.6 5.6 %collective-permute-start.2 = (f32[5,16,192]{2,1,0:T(8,128)S(1)}, f32[5,16,192]{2,1,0:T(8,128)S(1)}, u32[]{:S(2)}, u32[]{:S(2)}) collective-permute-start(f32[5,16,192]{2,1,0:T(8,128)S(1)} %get-tuple-element.15.rest_2_), channel_id=1, source_target_pairs={{0,15},{1,2},{2,1},{3,4},{4,3},{5,6},{6,5},{7,8},{8,7},{9,10},{10,... | collective-permute-start | bytes 184328 | tf_op jit(solution)/shard_map/ppermute | solution.py:405
  14.2 0.0 collective-permute-start.3
  14.3 0.0 copy-done.1
  14.3 0.0 copy-start.3
  14.3 1.3 %copy-done.3 = f32[5,16,16,192]{3,2,1,0:T(8,128)S(1)} copy-done((f32[5,16,16,192]{3,2,1,0:T(8,128)S(1)}, f32[5,16,16,192]{3,2,1,0:T(8,128)}, u32[]{:S(2)}) %copy-start.3) | copy-done | bytes 983064
  15.6 1.8 %interior_kernel.1 = (f32[5,16,16,192]{3,2,1,0:T(8,128)S(1)}, f32[16,16,192]{2,1,0:T(8,128)S(1)}) custom-call(f32[5,16,16,192]{3,2,1,0:T(8,128)S(1)} %copy-done.1, f32[5,16,16,192]{3,2,1,0:T(8,128)S(1)} %copy-done.3, s32[1,192]{1,0:T(1,128)S(1)} %bitcast.5, s32[16,16]{1,0:T(8,128)S(1)} %copy-done.5), custom_call_target="tpu_custom_call" | custom-call | flops 10000000 | bytes 1967872 | tf_op jit(solution)/shard_map/interior_kernel/pallas_call | solution.py:392
  17.5 0.1 subtract_add_fusion.shift
  17.5 0.0 collective-permute-done.rest_4_
  17.5 0.0 collective-permute-done.1.rest_5_
  17.5 0.0 collective-permute-done.2.rest_6_
  17.5 1.0 %collective-permute-done.3.rest_7_ = f32[5,16,192]{2,1,0:T(8,128)S(1)} collective-permute-done((f32[5,16,192]{2,1,0:T(8,128)S(1)}, f32[5,16,192]{2,1,0:T(8,128)S(1)}, u32[]{:S(2)}, u32[]{:S(2)}) %collective-permute-start.3) | collective-permute-done | bytes 61472 | tf_op jit(solution)/shard_map/ppermute | solution.py:405
  18.5 0.8 momentum_kernel.1
  19.4 13.7 %all_to_all.20 = f32[16,16,256]{2,1,0:T(8,128)S(1)} all-to-all(f32[16,16,256]{2,1,0:T(8,128)S(1)} %momentum_kernel.1), channel_id=1, replica_groups=mesh['px'=16,'py'=16] {'px'}, dimensions={0} | all-to-all | bytes 524288 | tf_op jit(solution)/shard_map/all_to_all | solution.py:442
  33.1 0.8 forward_kernel.1
  33.9 21.7 %all_to_all.21.lines = f32[256,1,256]{2,1,0:T(1,128)S(1)} all-to-all(f32[256,1,256]{2,1,0:T(1,128)S(1)} %forward_kernel.1), channel_id=1, replica_groups=mesh['px'=16,'py'=16] {'py','px'}, dimensions={0} | all-to-all | bytes 524288 | tf_op jit(solution)/shard_map/all_to_all | solution.py:446
  55.7 2.0 %solve_kernel.1 = f32[256,1,256]{2,1,0:T(1,128)S(1)} custom-call(f32[256,1,256]{2,1,0:T(1,128)S(1)} %all_to_all.21.lines, f32[256,256]{1,0:T(8,128)S(1)} %copy-done.2, s32[1,192]{1,0:T(1,128)S(1)} %bitcast.7, f32[1,256]{1,0:T(1,128)S(1)} %subtract_add_fusion.shift), custom_call_target="tpu_custom_call" | custom-call | bytes 526080 | tf_op jit(solution)/shard_map/solve_kernel/pallas_call | solution.py:392
  57.7 20.4 %all_to_all.22.lines = f32[256,1,256]{2,1,0:T(1,128)S(1)} all-to-all(f32[256,1,256]{2,1,0:T(1,128)S(1)} %solve_kernel.1), channel_id=1, replica_groups=mesh['px'=16,'py'=16] {'py','px'}, dimensions={0} | all-to-all | bytes 524288 | tf_op jit(solution)/shard_map/all_to_all | solution.py:452
  78.1 0.8 backward_kernel.1
  78.9 11.8 %all_to_all.23.message = f32[16,16,256]{2,1,0:T(8,128)S(1)} all-to-all(f32[16,16,256]{2,1,0:T(8,128)S(1)} %bitcast.3), channel_id=1, replica_groups=mesh['px'=16,'py'=16] {'px'}, dimensions={0} | all-to-all | bytes 524288 | tf_op jit(solution)/shard_map/all_to_all | solution.py:456
  90.7 2.0 %correct_kernel.1 = (f32[5,16,16,192]{3,2,1,0:T(8,128)}, f32[16,16,192]{2,1,0:T(8,128)}) custom-call(f32[16,16,256]{2,1,0:T(8,128)S(1)} %all_to_all.23.message, f32[5,16,16,192]{3,2,1,0:T(8,128)S(1)} %get-tuple-element.11.inner, f32[16,16,192]{2,1,0:T(8,128)S(1)} %get-tuple-element.12.fluid, f32[5,16,192]{2,1,0:T(8,128)S(1)} %get-tuple-element.13.rest_0_, ...), custom_call_target="tpu_custom_call" | custom-call | bytes 1934080 | tf_op jit(solution)/shard_map/correct_kernel/pallas_call | solution.py:392
  (8 shorter events, 0.0 us)
Async XLA Ops:
  0.6 1.3 %copy-start = (f32[5,16,16,192]{3,2,1,0:T(8,128)S(1)}, f32[5,16,16,192]{3,2,1,0:T(8,128)}, u32[]{:S(2)}) copy-start(f32[5,16,16,192]{3,2,1,0:T(8,128)} %state.3) | copy-start | bytes 2949124
  1.9 12.3 %copy-start.1 = (f32[5,16,16,192]{3,2,1,0:T(8,128)S(1)}, f32[5,16,16,192]{3,2,1,0:T(8,128)}, u32[]{:S(2)}) copy-start(f32[5,16,16,192]{3,2,1,0:T(8,128)} %state.3) | copy-start | bytes 2949124
  1.9 12.4 %copy-start.4 = (s32[192]{0:T(256)S(1)}, s32[192]{0:T(256)}, u32[]{:S(2)}) copy-start(s32[192]{0:T(256)} %param.7) | copy-start | bytes 2308
  2.0 12.4 %copy-start.5 = (s32[16,16]{1,0:T(8,128)S(1)}, s32[16,16]{1,0:T(8,128)}, u32[]{:S(2)}) copy-start(s32[16,16]{1,0:T(8,128)} %height.1) | copy-start | bytes 3076
  2.1 15.4 %collective-permute-start = (f32[5,16,192]{2,1,0:T(8,128)S(1)}, f32[5,16,192]{2,1,0:T(8,128)S(1)}, u32[]{:S(2)}, u32[]{:S(2)}) collective-permute-start(f32[5,16,192]{2,1,0:T(8,128)S(1)} %get-tuple-element.13.rest_0_), channel_id=1, source_target_pairs={{0,240},{16,32},{32,16},{48,64},{64,48},{80,96},{96,80},{112,128},... | collective-permute-start | bytes 184328 | tf_op jit(solution)/shard_map/ppermute | solution.py:405
  6.3 11.2 %collective-permute-start.1 = (f32[5,16,192]{2,1,0:T(8,128)S(1)}, f32[5,16,192]{2,1,0:T(8,128)S(1)}, u32[]{:S(2)}, u32[]{:S(2)}) collective-permute-start(f32[5,16,192]{2,1,0:T(8,128)S(1)} %get-tuple-element.14.rest_1_), channel_id=1, source_target_pairs={{0,16},{16,0},{32,48},{48,32},{64,80},{80,64},{96,112},{112,96},{1... | collective-permute-start | bytes 184328 | tf_op jit(solution)/shard_map/ppermute | solution.py:405
  8.6 8.9 %collective-permute-start.2 = (f32[5,16,192]{2,1,0:T(8,128)S(1)}, f32[5,16,192]{2,1,0:T(8,128)S(1)}, u32[]{:S(2)}, u32[]{:S(2)}) collective-permute-start(f32[5,16,192]{2,1,0:T(8,128)S(1)} %get-tuple-element.15.rest_2_), channel_id=1, source_target_pairs={{0,15},{1,2},{2,1},{3,4},{4,3},{5,6},{6,5},{7,8},{8,7},{9,10},{10,... | collective-permute-start | bytes 184328 | tf_op jit(solution)/shard_map/ppermute | solution.py:405
  14.2 4.3 %collective-permute-start.3 = (f32[5,16,192]{2,1,0:T(8,128)S(1)}, f32[5,16,192]{2,1,0:T(8,128)S(1)}, u32[]{:S(2)}, u32[]{:S(2)}) collective-permute-start(f32[5,16,192]{2,1,0:T(8,128)S(1)} %get-tuple-element.16.rest_3_), channel_id=1, source_target_pairs={{0,1},{1,0},{2,3},{3,2},{4,5},{5,4},{6,7},{7,6},{8,9},{9,8},{10,11... | collective-permute-start | bytes 184328 | tf_op jit(solution)/shard_map/ppermute | solution.py:405
  14.3 1.3 %copy-start.3 = (f32[5,16,16,192]{3,2,1,0:T(8,128)S(1)}, f32[5,16,16,192]{3,2,1,0:T(8,128)}, u32[]{:S(2)}) copy-start(f32[5,16,16,192]{3,2,1,0:T(8,128)} %memory.1) | copy-start | bytes 2949124
  18.5 14.6 %copy-start.2 = (f32[256,256]{1,0:T(8,128)S(1)}, f32[256,256]{1,0:T(8,128)}, u32[]{:S(2)}) copy-start(f32[256,256]{1,0:T(8,128)} %constant.17.clone.basis) | copy-start | bytes 786436

commit v9 on v8

--- a/solution.py
+++ b/solution.py
@@ -164,13 +164,26 @@
         fluid[x] = jnp.where(level >= bottom[x * TILE : (x + 1) * TILE], 1.0, 0.0)
 
 
-def interior_kernel(state, memory, level_steps, height, provisional, fluid):
+def divergence(du, dv, dw, inv_thick):
+    dv_before = jnp.concatenate([jnp.zeros_like(dv[:1]), dv[:-1]], axis=0)
+    return du + (dv - dv_before) + (dw - lanes_down(dw)) * inv_thick
+
+
+def interior_kernel(state, memory, level_steps, height, provisional, fluid, message):
     fill_fluid(height, fluid)
 
     def store(f, x, value):
         provisional[f, x] = value
 
     advance_fields(state, memory, level_steps, fluid, store)
+    inv_thick = 1.0 / level_rows(level_steps)[0]
+    for x in range(TILE):
+        u, v, w = (provisional[f, x] for f in range(3))
+        du = u - provisional[0, x - 1] if x else u
+        total = divergence(du, v, w, inv_thick)
+        rest = jnp.zeros((TILE, WIDE - LEVELS), jnp.float32)
+        message[:, x, :128] = total[:, :128]
+        message[:, x, 128:] = jnp.concatenate([total[:, 128:], rest], axis=1)
 
 
 def sides(field, x_outer, x_inner, y_outer, y_inner):
@@ -183,44 +196,65 @@
     )
 
 
-def add_outer_faces(total, target, edges, halos, fluid):
+def outer_faces(total, edges, halos, fluid):
     last, factor = TILE - 1, RK_STEP * TIME_STEP
     west_u, south_v = sides(0, *halos)[0], sides(1, *halos)[2]
     east_u, north_v = sides(0, *edges)[1], sides(1, *edges)[3]
+    added = []
     for f in range(total):
         x_low, x_high, y_low, y_high = sides(f, *edges)
         west, east, south, north = sides(f, *halos)
-        target[f, 0] -= factor * fluid[0] * faces(west, x_low, west_u)
-        target[f, last] += factor * fluid[last] * faces(x_high, east, east_u)
-        target[f, :, 0] -= factor * fluid[:, 0] * faces(south, y_low, south_v)
-        target[f, :, last] += factor * fluid[:, last] * faces(y_high, north, north_v)
-
-
-def momentum_kernel(inner, fluid, *rest):
-    edges, halos, (level_steps, message, provisional) = rest[:4], rest[4:8], rest[8:]
-    provisional[...] = inner[0:3]
-    add_outer_faces(3, provisional, edges, halos, fluid)
+        added.append(
+            (
+                -factor * fluid[0] * faces(west, x_low, west_u),
+                factor * fluid[last] * faces(x_high, east, east_u),
+                -factor * fluid[:, 0] * faces(south, y_low, south_v),
+                factor * fluid[:, last] * faces(y_high, north, north_v),
+            )
+        )
+    return added
+
+
+def add_outer_faces(total, target, edges, halos, fluid):
+    last = TILE - 1
+    for f, (west, east, south, north) in enumerate(outer_faces(total, edges, halos, fluid)):
+        target[f, 0] += west
+        target[f, last] += east
+        target[f, :, 0] += south
+        target[f, :, last] += north
+
+
+def momentum_kernel(inner, fluid, inner_message, *rest):
+    edges, halos, (level_steps, message) = rest[:4], rest[4:8], rest[8:]
+    added = outer_faces(3, edges, halos, fluid)
+    (west_u, east_u, south_u, north_u), (west_v, east_v, south_v, north_v), w_added = added
+    last = TILE - 1
     inv_thick = 1.0 / level_rows(level_steps)[0]
+    row = lax.broadcasted_iota(jnp.int32, (TILE, LEVELS), 0)
+
+    def with_ends(plane, first_row, last_row):
+        return plane + jnp.where(row == 0, first_row, 0.0) + jnp.where(row == last, last_row, 0.0)
+
     zeros = jnp.zeros((TILE, WIDE - LEVELS), jnp.float32)
+    last_u = with_ends(inner[0, last] + east_u, south_u[last:], north_u[last:])
+    last_v = with_ends(inner[1, :, last] + north_v, west_v[last:], east_v[last:])
+    last_u = jnp.concatenate([last_u, zeros], axis=1)
+    last_v = jnp.concatenate([last_v, zeros], axis=1)
     mask = block_mask()
-    last_u = jnp.concatenate([provisional[0, TILE - 1], zeros], axis=1)
     u_packed = jnp.concatenate(
         [jnp.where(mask, last_u[y : y + 1], 0.0) for y in range(TILE)], axis=0
     )
-    last_v = jnp.concatenate([provisional[1, :, TILE - 1], zeros], axis=1)
     ones = jnp.where(mask, 1.0, 0.0)
     v_packed = jnp.concatenate([last_v * ones[y : y + 1] for y in range(TILE)], axis=0)
     upper = picked(u_packed, pack_places(FIRST)) + picked(v_packed, pack_places(SECOND))
-    upper = upper.reshape(TILE, TILE, 128)
-    for x in range(TILE):
-        u = provisional[0, x]
-        v = provisional[1, x]
-        w = provisional[2, x]
-        v_before = jnp.concatenate([jnp.zeros_like(v[:1]), v[:-1]], axis=0)
-        diverge = (v - v_before) + (w - lanes_down(w)) * inv_thick
-        diverge = diverge + (u - provisional[0, x - 1] if x else u)
-        message[:, x, :128] = diverge[:, :128]
-        message[:, x, 128:] = jnp.concatenate([diverge[:, 128:], zeros], axis=1) + upper[:, x]
+    message[:, :, :128] = inner_message[:, :, :128]
+    message[:, :, 128:] = inner_message[:, :, 128:] + upper.reshape(TILE, TILE, 128)
+    message[:, 0, :LEVELS] += divergence(west_u, west_v, w_added[0], inv_thick)
+    message[:, 1, :LEVELS] -= west_u
+    message[:, last, :LEVELS] += divergence(east_u, east_v, w_added[1], inv_thick)
+    message[0, :, :LEVELS] += divergence(south_v, south_u, w_added[2], inv_thick)
+    message[1, :, :LEVELS] -= south_v
+    message[last, :, :LEVELS] += divergence(north_v, north_u, w_added[3], inv_thick)
 
 
 def loaded(pairs, sems):
@@ -412,32 +446,35 @@
 def per_device(state, memory, level_steps, building_height):
     plane = shaped(5, TILE, LEVELS)
     edges = call(edges_kernel, [plane] * 4, state)
+    own_x = lax.axis_index("py") * lax.axis_size("px") + lax.axis_index("px")
+    shift = eigenvalues(jnp.arange(LINE, dtype=jnp.int32)) + eigenvalues(own_x)
+    *edges, shift = lax.optimization_barrier((*edges, shift.reshape(1, LINE)))
     halos = [
         swapped(edges[i], axis, outer)
         for i, (axis, outer) in enumerate([("px", 1), ("px", 0), ("py", 1), ("py", 0)])
     ]
 
     steps = level_steps.reshape(1, LEVELS)
-    own_x = lax.axis_index("py") * lax.axis_size("px") + lax.axis_index("px")
-    shift = eigenvalues(jnp.arange(LINE, dtype=jnp.int32)) + eigenvalues(own_x)
     basis = jnp.asarray(BASIS)
     hbm = pl.BlockSpec(memory_space=pltpu.HBM)
     scratch = lambda *shape: pltpu.VMEM(shape, jnp.float32)
     sems = pltpu.SemaphoreType.DMA
 
-    inner, fluid = call(
+    inner, fluid, message = call(
         interior_kernel,
-        [shaped(FIELDS, TILE, TILE, LEVELS), shaped(TILE, TILE, LEVELS)],
+        [
+            shaped(FIELDS, TILE, TILE, LEVELS),
+            shaped(TILE, TILE, LEVELS),
+            shaped(TILE, TILE, WIDE),
+        ],
         state, memory, steps, building_height,
         flops=10**7,
     )
-    inner, shift = lax.optimization_barrier((inner, shift.reshape(1, LINE)))
     message = call(
         momentum_kernel,
         shaped(TILE, TILE, WIDE),
-        inner, fluid, *edges, *halos, steps,
+        inner, fluid, message, *edges, *halos, steps,
         flops=10**7,
-        scratch_shapes=[scratch(3, TILE, TILE, LEVELS)],
     )
     lines = lax.all_to_all(message, "px", split_axis=0, concat_axis=0, tiled=True)
     spectrum = call(

time: 93 us -> 92.8 us (level)
  local copies, waits for them, and re-layouts: 2.64 us -> 1.33 us
  waiting for transfers between devices: 1.01 us -> 2.27 us
    unnamed x12 -> x10, local copies, waits for them, and re-layouts: 2.64 us -> 1.33 us
    ppermute x4, waiting for transfers between devices: 1.01 us -> 2.27 us  [swapped(): lax.ppermute(block, axis, [(i, p % count) for i, p in enumerate(partner)])]
  transfers between devices with their start and end apart: 4 -> 4, of which waited for: 1 -> 2; matrix products, arithmetic and copies ran while one was open for 0% -> 0% of each run, Pallas kernels for 2% -> 2%
where the time goes in v9:
time: 92.8 us; the launch traced here: 92.6 us
  blocking collectives  67.7 us (73%)
  starting transfers between devices  12.1 us (13%)
  Pallas kernels  8.32 us (9%)
  waiting for transfers between devices  2.27 us (2%)
  local copies, waits for them, and re-layouts  1.33 us (1%)
    all_to_all x1, blocking collectives, per_device(): lax.all_to_all(spectrum, ('py', 'px'), split_axis=0, concat_axis=0, tiled...  21.7 us
    all_to_all x1, blocking collectives, per_device(): lax.all_to_all(solved, ('py', 'px'), split_axis=0, concat_axis=0, tiled=T...  20.4 us
    all_to_all x1, blocking collectives, per_device(): lax.all_to_all(message, 'px', split_axis=0, concat_axis=0, tiled=True)  13.7 us
    ppermute x4, starting transfers between devices, swapped(): lax.ppermute(block, axis, [(i, p % count) for i, p in enumerate(partner)])  12.1 us
    all_to_all x1, blocking collectives, per_device(): lax.all_to_all(message.reshape(TILE, TILE, WIDE), 'px', split_axis=0, con...  11.8 us
    pallas_call x7, Pallas kernels, call(): pl.pallas_call(kernel, out_shape=out_shape, name=kernel.__name__, compile...  8.32 us
    ppermute x4, waiting for transfers between devices, swapped(): lax.ppermute(block, axis, [(i, p % count) for i, p in enumerate(partner)])  2.27 us
  transfers between devices with their start and end apart: 4, of which 2 were waited for; matrix products, arithmetic and copies ran while one was open for 0% of the time, Pallas kernels for 2%

profile of v9, /device:TPU:1, one launch (start us, length us, event | category | flops | bytes accessed | tf_op | source)
XLA Modules:
  0.0 92.6 jit_solution(6846707256299969034)
XLA Ops:
  0.6 0.0 copy-start.4
  0.6 0.0 copy-start.3
  0.7 0.1 subtract_add_fusion.shift
  0.8 0.0 copy-start
  0.8 1.3 %copy-done = f32[5,16,16,192]{3,2,1,0:T(8,128)S(1)} copy-done((f32[5,16,16,192]{3,2,1,0:T(8,128)S(1)}, f32[5,16,16,192]{3,2,1,0:T(8,128)}, u32[]{:S(2)}) %copy-start) | copy-done | bytes 983064
  2.1 0.1 edges_kernel.1
  2.3 4.2 %collective-permute-start = (f32[5,16,192]{2,1,0:T(8,128)S(1)}, f32[5,16,192]{2,1,0:T(8,128)S(1)}, u32[]{:S(2)}, u32[]{:S(2)}) collective-permute-start(f32[5,16,192]{2,1,0:T(8,128)S(1)} %get-tuple-element.21.rest_0_), channel_id=1, source_target_pairs={{0,240},{16,32},{32,16},{48,64},{64,48},{80,96},{96,80},{112,128},... | collective-permute-start | bytes 184328 | tf_op jit(solution)/shard_map/ppermute | solution.py:439
  6.5 2.3 %collective-permute-start.1 = (f32[5,16,192]{2,1,0:T(8,128)S(1)}, f32[5,16,192]{2,1,0:T(8,128)S(1)}, u32[]{:S(2)}, u32[]{:S(2)}) collective-permute-start(f32[5,16,192]{2,1,0:T(8,128)S(1)} %get-tuple-element.22.rest_1_), channel_id=1, source_target_pairs={{0,16},{16,0},{32,48},{48,32},{64,80},{80,64},{96,112},{112,96},{1... | collective-permute-start | bytes 184328 | tf_op jit(solution)/shard_map/ppermute | solution.py:439
  8.8 5.6 %collective-permute-start.2 = (f32[5,16,192]{2,1,0:T(8,128)S(1)}, f32[5,16,192]{2,1,0:T(8,128)S(1)}, u32[]{:S(2)}, u32[]{:S(2)}) collective-permute-start(f32[5,16,192]{2,1,0:T(8,128)S(1)} %get-tuple-element.23.rest_2_), channel_id=1, source_target_pairs={{0,15},{1,2},{2,1},{3,4},{4,3},{5,6},{6,5},{7,8},{8,7},{9,10},{10,... | collective-permute-start | bytes 184328 | tf_op jit(solution)/shard_map/ppermute | solution.py:439
  14.4 0.0 collective-permute-start.3
  14.4 2.0 %interior_kernel.1 = (f32[5,16,16,192]{3,2,1,0:T(8,128)S(1)}, f32[16,16,192]{2,1,0:T(8,128)S(1)}, f32[16,16,256]{2,1,0:T(8,128)S(1)}) custom-call(f32[5,16,16,192]{3,2,1,0:T(8,128)S(1)} %copy-done, f32[5,16,16,192]{3,2,1,0:T(8,128)S(1)} %copy-done.2, s32[1,192]{1,0:T(1,128)S(1)} %bitcast.5, s32[16,16]{1,0:T(8,128)S(1)} %copy-done.4), custom_call_target="tpu_custom_call" | custom-call | flops 10000000 | bytes 1967872 | tf_op jit(solution)/shard_map/interior_kernel/pallas_call | solution.py:426
  16.4 0.0 collective-permute-done.rest_4_
  16.4 0.0 collective-permute-done.1.rest_5_
  16.4 0.7 collective-permute-done.2.rest_6_
  17.2 1.5 %collective-permute-done.3.rest_7_ = f32[5,16,192]{2,1,0:T(8,128)S(1)} collective-permute-done((f32[5,16,192]{2,1,0:T(8,128)S(1)}, f32[5,16,192]{2,1,0:T(8,128)S(1)}, u32[]{:S(2)}, u32[]{:S(2)}) %collective-permute-start.3) | collective-permute-done | bytes 61472 | tf_op jit(solution)/shard_map/ppermute | solution.py:439
  18.7 0.5 momentum_kernel.1
  19.2 13.7 %all_to_all.20 = f32[16,16,256]{2,1,0:T(8,128)S(1)} all-to-all(f32[16,16,256]{2,1,0:T(8,128)S(1)} %momentum_kernel.1), channel_id=1, replica_groups=mesh['px'=16,'py'=16] {'px'}, dimensions={0} | all-to-all | bytes 524288 | tf_op jit(solution)/shard_map/all_to_all | solution.py:479
  32.9 0.8 forward_kernel.1
  33.8 21.7 %all_to_all.21.lines = f32[256,1,256]{2,1,0:T(1,128)S(1)} all-to-all(f32[256,1,256]{2,1,0:T(1,128)S(1)} %forward_kernel.1), channel_id=1, replica_groups=mesh['px'=16,'py'=16] {'py','px'}, dimensions={0} | all-to-all | bytes 524288 | tf_op jit(solution)/shard_map/all_to_all | solution.py:483
  55.5 2.0 %solve_kernel.1 = f32[256,1,256]{2,1,0:T(1,128)S(1)} custom-call(f32[256,1,256]{2,1,0:T(1,128)S(1)} %all_to_all.21.lines, f32[256,256]{1,0:T(8,128)S(1)} %copy-done.1, s32[1,192]{1,0:T(1,128)S(1)} %bitcast.7, f32[1,256]{1,0:T(1,128)S(1)} %subtract_add_fusion.shift), custom_call_target="tpu_custom_call" | custom-call | bytes 526080 | tf_op jit(solution)/shard_map/solve_kernel/pallas_call | solution.py:426
  57.5 20.4 %all_to_all.22.lines = f32[256,1,256]{2,1,0:T(1,128)S(1)} all-to-all(f32[256,1,256]{2,1,0:T(1,128)S(1)} %solve_kernel.1), channel_id=1, replica_groups=mesh['px'=16,'py'=16] {'py','px'}, dimensions={0} | all-to-all | bytes 524288 | tf_op jit(solution)/shard_map/all_to_all | solution.py:489
  77.9 0.8 backward_kernel.1
  78.8 11.8 %all_to_all.23.message = f32[16,16,256]{2,1,0:T(8,128)S(1)} all-to-all(f32[16,16,256]{2,1,0:T(8,128)S(1)} %bitcast.3), channel_id=1, replica_groups=mesh['px'=16,'py'=16] {'px'}, dimensions={0} | all-to-all | bytes 524288 | tf_op jit(solution)/shard_map/all_to_all | solution.py:493
  90.6 2.0 %correct_kernel.1 = (f32[5,16,16,192]{3,2,1,0:T(8,128)}, f32[16,16,192]{2,1,0:T(8,128)}) custom-call(f32[16,16,256]{2,1,0:T(8,128)S(1)} %all_to_all.23.message, f32[5,16,16,192]{3,2,1,0:T(8,128)S(1)} %get-tuple-element.14.inner, f32[16,16,192]{2,1,0:T(8,128)S(1)} %get-tuple-element.15.fluid, f32[5,16,192]{2,1,0:T(8,128)S(1)} %get-tuple-element.21.rest_0_, ...), custom_call_target="tpu_custom_call" | custom-call | bytes 1934080 | tf_op jit(solution)/shard_map/correct_kernel/pallas_call | solution.py:426
  (6 shorter events, 0.0 us)
Async XLA Ops:
  0.6 13.7 %copy-start.4 = (s32[16,16]{1,0:T(8,128)S(1)}, s32[16,16]{1,0:T(8,128)}, u32[]{:S(2)}) copy-start(s32[16,16]{1,0:T(8,128)} %height.1) | copy-start | bytes 3076
  0.6 13.7 %copy-start.3 = (s32[192]{0:T(256)S(1)}, s32[192]{0:T(256)}, u32[]{:S(2)}) copy-start(s32[192]{0:T(256)} %param.7) | copy-start | bytes 2308
  0.8 1.3 %copy-start = (f32[5,16,16,192]{3,2,1,0:T(8,128)S(1)}, f32[5,16,16,192]{3,2,1,0:T(8,128)}, u32[]{:S(2)}) copy-start(f32[5,16,16,192]{3,2,1,0:T(8,128)} %state.3) | copy-start | bytes 2949124
  2.1 12.3 %copy-start.2 = (f32[5,16,16,192]{3,2,1,0:T(8,128)S(1)}, f32[5,16,16,192]{3,2,1,0:T(8,128)}, u32[]{:S(2)}) copy-start(f32[5,16,16,192]{3,2,1,0:T(8,128)} %memory.1) | copy-start | bytes 2949124
  2.3 14.2 %collective-permute-start = (f32[5,16,192]{2,1,0:T(8,128)S(1)}, f32[5,16,192]{2,1,0:T(8,128)S(1)}, u32[]{:S(2)}, u32[]{:S(2)}) collective-permute-start(f32[5,16,192]{2,1,0:T(8,128)S(1)} %get-tuple-element.21.rest_0_), channel_id=1, source_target_pairs={{0,240},{16,32},{32,16},{48,64},{64,48},{80,96},{96,80},{112,128},... | collective-permute-start | bytes 184328 | tf_op jit(solution)/shard_map/ppermute | solution.py:439
  6.5 10.0 %collective-permute-start.1 = (f32[5,16,192]{2,1,0:T(8,128)S(1)}, f32[5,16,192]{2,1,0:T(8,128)S(1)}, u32[]{:S(2)}, u32[]{:S(2)}) collective-permute-start(f32[5,16,192]{2,1,0:T(8,128)S(1)} %get-tuple-element.22.rest_1_), channel_id=1, source_target_pairs={{0,16},{16,0},{32,48},{48,32},{64,80},{80,64},{96,112},{112,96},{1... | collective-permute-start | bytes 184328 | tf_op jit(solution)/shard_map/ppermute | solution.py:439
  8.8 8.4 %collective-permute-start.2 = (f32[5,16,192]{2,1,0:T(8,128)S(1)}, f32[5,16,192]{2,1,0:T(8,128)S(1)}, u32[]{:S(2)}, u32[]{:S(2)}) collective-permute-start(f32[5,16,192]{2,1,0:T(8,128)S(1)} %get-tuple-element.23.rest_2_), channel_id=1, source_target_pairs={{0,15},{1,2},{2,1},{3,4},{4,3},{5,6},{6,5},{7,8},{8,7},{9,10},{10,... | collective-permute-start | bytes 184328 | tf_op jit(solution)/shard_map/ppermute | solution.py:439
  14.4 4.3 %collective-permute-start.3 = (f32[5,16,192]{2,1,0:T(8,128)S(1)}, f32[5,16,192]{2,1,0:T(8,128)S(1)}, u32[]{:S(2)}, u32[]{:S(2)}) collective-permute-start(f32[5,16,192]{2,1,0:T(8,128)S(1)} %get-tuple-element.24.rest_3_), channel_id=1, source_target_pairs={{0,1},{1,0},{2,3},{3,2},{4,5},{5,4},{6,7},{7,6},{8,9},{9,8},{10,11... | collective-permute-start | bytes 184328 | tf_op jit(solution)/shard_map/ppermute | solution.py:439
  18.7 14.2 %copy-start.1 = (f32[256,256]{1,0:T(8,128)S(1)}, f32[256,256]{1,0:T(8,128)}, u32[]{:S(2)}) copy-start(f32[256,256]{1,0:T(8,128)} %constant.17.clone.basis) | copy-start | bytes 786436

commit v10 on v9

--- a/solution.py
+++ b/solution.py
@@ -169,7 +169,10 @@
     return du + (dv - dv_before) + (dw - lanes_down(dw)) * inv_thick
 
 
-def interior_kernel(state, memory, level_steps, height, provisional, fluid, message):
+def interior_kernel(
+    state, memory, level_steps, height, shift, provisional, fluid, message, shift_kept
+):
+    shift_kept[...] = shift[...]
     fill_fluid(height, fluid)
 
     def store(f, x, value):
@@ -448,7 +451,6 @@
     edges = call(edges_kernel, [plane] * 4, state)
     own_x = lax.axis_index("py") * lax.axis_size("px") + lax.axis_index("px")
     shift = eigenvalues(jnp.arange(LINE, dtype=jnp.int32)) + eigenvalues(own_x)
-    *edges, shift = lax.optimization_barrier((*edges, shift.reshape(1, LINE)))
     halos = [
         swapped(edges[i], axis, outer)
         for i, (axis, outer) in enumerate([("px", 1), ("px", 0), ("py", 1), ("py", 0)])
@@ -460,14 +462,15 @@
     scratch = lambda *shape: pltpu.VMEM(shape, jnp.float32)
     sems = pltpu.SemaphoreType.DMA
 
-    inner, fluid, message = call(
+    inner, fluid, message, shift = call(
         interior_kernel,
         [
             shaped(FIELDS, TILE, TILE, LEVELS),
             shaped(TILE, TILE, LEVELS),
             shaped(TILE, TILE, WIDE),
+            shaped(1, LINE),
         ],
-        state, memory, steps, building_height,
+        state, memory, steps, building_height, shift.reshape(1, LINE),
         flops=10**7,
     )
     message = call(

time: 92.8 us -> 92.7 us (level)
  waiting for transfers between devices: 2.27 us -> 0.84 us
  local copies, waits for them, and re-layouts: 1.33 us -> 2.64 us
    ppermute x4, waiting for transfers between devices: 2.27 us -> 0.84 us  [swapped(): lax.ppermute(block, axis, [(i, p % count) for i, p in enumerate(partner)])]
    unnamed x10 -> x12, local copies, waits for them, and re-layouts: 1.33 us -> 2.64 us
  transfers between devices with their start and end apart: 4 -> 4, of which waited for: 2 -> 1; matrix products, arithmetic and copies ran while one was open for 0% -> 0% of each run, Pallas kernels for 2% -> 2%
where the time goes in v10:
time: 92.7 us; the launch traced here: 92.4 us
  blocking collectives  67.7 us (73%)
  starting transfers between devices  12.1 us (13%)
  Pallas kernels  8.26 us (9%)
  local copies, waits for them, and re-layouts  2.64 us (3%)
    all_to_all x1, blocking collectives, per_device(): lax.all_to_all(spectrum, ('py', 'px'), split_axis=0, concat_axis=0, tiled...  21.7 us
    all_to_all x1, blocking collectives, per_device(): lax.all_to_all(solved, ('py', 'px'), split_axis=0, concat_axis=0, tiled=T...  20.4 us
    all_to_all x1, blocking collectives, per_device(): lax.all_to_all(message, 'px', split_axis=0, concat_axis=0, tiled=True)  13.7 us
    ppermute x4, starting transfers between devices, swapped(): lax.ppermute(block, axis, [(i, p % count) for i, p in enumerate(partner)])  12.1 us
    all_to_all x1, blocking collectives, per_device(): lax.all_to_all(message.reshape(TILE, TILE, WIDE), 'px', split_axis=0, con...  11.8 us
    pallas_call x7, Pallas kernels, call(): pl.pallas_call(kernel, out_shape=out_shape, name=kernel.__name__, compile...  8.26 us
    unnamed x12, local copies, waits for them, and re-layouts  2.64 us
  transfers between devices with their start and end apart: 4, of which 1 were waited for; matrix products, arithmetic and copies ran while one was open for 0% of the time, Pallas kernels for 2%

profile of v10, /device:TPU:1, one launch (start us, length us, event | category | flops | bytes accessed | tf_op | source)
XLA Modules:
  0.0 92.4 jit_solution(8652120259976827373)
XLA Ops:
  0.6 0.0 copy-start
  0.6 1.3 %copy-done = f32[5,16,16,192]{3,2,1,0:T(8,128)S(1)} copy-done((f32[5,16,16,192]{3,2,1,0:T(8,128)S(1)}, f32[5,16,16,192]{3,2,1,0:T(8,128)}, u32[]{:S(2)}) %copy-start) | copy-done | bytes 983064
  2.0 0.1 edges_kernel.1
  2.1 4.2 %collective-permute-start = (f32[5,16,192]{2,1,0:T(8,128)S(1)}, f32[5,16,192]{2,1,0:T(8,128)S(1)}, u32[]{:S(2)}, u32[]{:S(2)}) collective-permute-start(f32[5,16,192]{2,1,0:T(8,128)S(1)} %get-tuple-element.13.rest_0_), channel_id=1, source_target_pairs={{0,240},{16,32},{32,16},{48,64},{64,48},{80,96},{96,80},{112,128},... | collective-permute-start | bytes 184328 | tf_op jit(solution)/shard_map/ppermute | solution.py:442
  6.3 2.3 %collective-permute-start.1 = (f32[5,16,192]{2,1,0:T(8,128)S(1)}, f32[5,16,192]{2,1,0:T(8,128)S(1)}, u32[]{:S(2)}, u32[]{:S(2)}) collective-permute-start(f32[5,16,192]{2,1,0:T(8,128)S(1)} %get-tuple-element.14.rest_1_), channel_id=1, source_target_pairs={{0,16},{16,0},{32,48},{48,32},{64,80},{80,64},{96,112},{112,96},{1... | collective-permute-start | bytes 184328 | tf_op jit(solution)/shard_map/ppermute | solution.py:442
  8.6 5.6 %collective-permute-start.2 = (f32[5,16,192]{2,1,0:T(8,128)S(1)}, f32[5,16,192]{2,1,0:T(8,128)S(1)}, u32[]{:S(2)}, u32[]{:S(2)}) collective-permute-start(f32[5,16,192]{2,1,0:T(8,128)S(1)} %get-tuple-element.15.rest_2_), channel_id=1, source_target_pairs={{0,15},{1,2},{2,1},{3,4},{4,3},{5,6},{6,5},{7,8},{8,7},{9,10},{10,... | collective-permute-start | bytes 184328 | tf_op jit(solution)/shard_map/ppermute | solution.py:442
  14.2 0.0 collective-permute-start.3
  14.3 0.1 subtract_add_fusion.shift
  14.4 0.0 copy-start.3
  14.4 1.3 %copy-done.3 = f32[5,16,16,192]{3,2,1,0:T(8,128)S(1)} copy-done((f32[5,16,16,192]{3,2,1,0:T(8,128)S(1)}, f32[5,16,16,192]{3,2,1,0:T(8,128)}, u32[]{:S(2)}) %copy-start.3) | copy-done | bytes 983064
  15.7 2.0 %interior_kernel.1 = (f32[5,16,16,192]{3,2,1,0:T(8,128)S(1)}, f32[16,16,192]{2,1,0:T(8,128)S(1)}, f32[16,16,256]{2,1,0:T(8,128)S(1)}, f32[1,256]{1,0:T(1,128)S(1)}) custom-call(f32[5,16,16,192]{3,2,1,0:T(8,128)S(1)} %copy-done.1, f32[5,16,16,192]{3,2,1,0:T(8,128)S(1)} %copy-done.3, s32[1,192]{1,0:T(1,128)S(1)} %bitcast.5, s32[16,16]{1,0:T(8,128)S(1)} %copy-done.5, ...), custom_call_target="tpu_custom_call" | custom-call | flops 10000000 | bytes 1968896 | tf_op jit(solution)/shard_map/interior_kernel/pallas_call | solution.py:429
  17.7 0.0 collective-permute-done.rest_4_
  17.7 0.0 collective-permute-done.1.rest_5_
  17.7 0.0 collective-permute-done.2.rest_6_
  17.7 0.8 collective-permute-done.3.rest_7_
  18.5 0.5 momentum_kernel.1
  19.0 13.7 %all_to_all.20 = f32[16,16,256]{2,1,0:T(8,128)S(1)} all-to-all(f32[16,16,256]{2,1,0:T(8,128)S(1)} %momentum_kernel.1), channel_id=1, replica_groups=mesh['px'=16,'py'=16] {'px'}, dimensions={0} | all-to-all | bytes 524288 | tf_op jit(solution)/shard_map/all_to_all | solution.py:482
  32.8 0.8 forward_kernel.1
  33.6 21.7 %all_to_all.21.lines = f32[256,1,256]{2,1,0:T(1,128)S(1)} all-to-all(f32[256,1,256]{2,1,0:T(1,128)S(1)} %forward_kernel.1), channel_id=1, replica_groups=mesh['px'=16,'py'=16] {'py','px'}, dimensions={0} | all-to-all | bytes 524288 | tf_op jit(solution)/shard_map/all_to_all | solution.py:486
  55.3 2.0 %solve_kernel.1 = f32[256,1,256]{2,1,0:T(1,128)S(1)} custom-call(f32[256,1,256]{2,1,0:T(1,128)S(1)} %all_to_all.21.lines, f32[256,256]{1,0:T(8,128)S(1)} %copy-done.2, s32[1,192]{1,0:T(1,128)S(1)} %bitcast.7, f32[1,256]{1,0:T(1,128)S(1)} %get-tuple-element.17.shift), custom_call_target="tpu_custom_call" | custom-call | bytes 526080 | tf_op jit(solution)/shard_map/solve_kernel/pallas_call | solution.py:429
  57.3 20.4 %all_to_all.22.lines = f32[256,1,256]{2,1,0:T(1,128)S(1)} all-to-all(f32[256,1,256]{2,1,0:T(1,128)S(1)} %solve_kernel.1), channel_id=1, replica_groups=mesh['px'=16,'py'=16] {'py','px'}, dimensions={0} | all-to-all | bytes 524288 | tf_op jit(solution)/shard_map/all_to_all | solution.py:492
  77.8 0.8 backward_kernel.1
  78.6 11.8 %all_to_all.23.message = f32[16,16,256]{2,1,0:T(8,128)S(1)} all-to-all(f32[16,16,256]{2,1,0:T(8,128)S(1)} %bitcast.3), channel_id=1, replica_groups=mesh['px'=16,'py'=16] {'px'}, dimensions={0} | all-to-all | bytes 524288 | tf_op jit(solution)/shard_map/all_to_all | solution.py:496
  90.4 2.0 %correct_kernel.1 = (f32[5,16,16,192]{3,2,1,0:T(8,128)}, f32[16,16,192]{2,1,0:T(8,128)}) custom-call(f32[16,16,256]{2,1,0:T(8,128)S(1)} %all_to_all.23.message, f32[5,16,16,192]{3,2,1,0:T(8,128)S(1)} %get-tuple-element.10.inner, f32[16,16,192]{2,1,0:T(8,128)S(1)} %get-tuple-element.11.fluid, f32[5,16,192]{2,1,0:T(8,128)S(1)} %get-tuple-element.13.rest_0_, ...), custom_call_target="tpu_custom_call" | custom-call | bytes 1934080 | tf_op jit(solution)/shard_map/correct_kernel/pallas_call | solution.py:429
  (8 shorter events, 0.0 us)
Async XLA Ops:
  0.6 1.3 %copy-start = (f32[5,16,16,192]{3,2,1,0:T(8,128)S(1)}, f32[5,16,16,192]{3,2,1,0:T(8,128)}, u32[]{:S(2)}) copy-start(f32[5,16,16,192]{3,2,1,0:T(8,128)} %state.3) | copy-start | bytes 2949124
  1.9 12.4 %copy-start.1 = (f32[5,16,16,192]{3,2,1,0:T(8,128)S(1)}, f32[5,16,16,192]{3,2,1,0:T(8,128)}, u32[]{:S(2)}) copy-start(f32[5,16,16,192]{3,2,1,0:T(8,128)} %state.3) | copy-start | bytes 2949124
  1.9 12.4 %copy-start.4 = (s32[192]{0:T(256)S(1)}, s32[192]{0:T(256)}, u32[]{:S(2)}) copy-start(s32[192]{0:T(256)} %param.7) | copy-start | bytes 2308
  2.0 12.4 %copy-start.5 = (s32[16,16]{1,0:T(8,128)S(1)}, s32[16,16]{1,0:T(8,128)}, u32[]{:S(2)}) copy-start(s32[16,16]{1,0:T(8,128)} %height.1) | copy-start | bytes 3076
  2.1 15.6 %collective-permute-start = (f32[5,16,192]{2,1,0:T(8,128)S(1)}, f32[5,16,192]{2,1,0:T(8,128)S(1)}, u32[]{:S(2)}, u32[]{:S(2)}) collective-permute-start(f32[5,16,192]{2,1,0:T(8,128)S(1)} %get-tuple-element.13.rest_0_), channel_id=1, source_target_pairs={{0,240},{16,32},{32,16},{48,64},{64,48},{80,96},{96,80},{112,128},... | collective-permute-start | bytes 184328 | tf_op jit(solution)/shard_map/ppermute | solution.py:442
  6.3 11.4 %collective-permute-start.1 = (f32[5,16,192]{2,1,0:T(8,128)S(1)}, f32[5,16,192]{2,1,0:T(8,128)S(1)}, u32[]{:S(2)}, u32[]{:S(2)}) collective-permute-start(f32[5,16,192]{2,1,0:T(8,128)S(1)} %get-tuple-element.14.rest_1_), channel_id=1, source_target_pairs={{0,16},{16,0},{32,48},{48,32},{64,80},{80,64},{96,112},{112,96},{1... | collective-permute-start | bytes 184328 | tf_op jit(solution)/shard_map/ppermute | solution.py:442
  8.6 9.1 %collective-permute-start.2 = (f32[5,16,192]{2,1,0:T(8,128)S(1)}, f32[5,16,192]{2,1,0:T(8,128)S(1)}, u32[]{:S(2)}, u32[]{:S(2)}) collective-permute-start(f32[5,16,192]{2,1,0:T(8,128)S(1)} %get-tuple-element.15.rest_2_), channel_id=1, source_target_pairs={{0,15},{1,2},{2,1},{3,4},{4,3},{5,6},{6,5},{7,8},{8,7},{9,10},{10,... | collective-permute-start | bytes 184328 | tf_op jit(solution)/shard_map/ppermute | solution.py:442
  14.2 4.3 %collective-permute-start.3 = (f32[5,16,192]{2,1,0:T(8,128)S(1)}, f32[5,16,192]{2,1,0:T(8,128)S(1)}, u32[]{:S(2)}, u32[]{:S(2)}) collective-permute-start(f32[5,16,192]{2,1,0:T(8,128)S(1)} %get-tuple-element.16.rest_3_), channel_id=1, source_target_pairs={{0,1},{1,0},{2,3},{3,2},{4,5},{5,4},{6,7},{7,6},{8,9},{9,8},{10,11... | collective-permute-start | bytes 184328 | tf_op jit(solution)/shard_map/ppermute | solution.py:442
  14.4 1.3 %copy-start.3 = (f32[5,16,16,192]{3,2,1,0:T(8,128)S(1)}, f32[5,16,16,192]{3,2,1,0:T(8,128)}, u32[]{:S(2)}) copy-start(f32[5,16,16,192]{3,2,1,0:T(8,128)} %memory.1) | copy-start | bytes 2949124
  18.5 14.2 %copy-start.2 = (f32[256,256]{1,0:T(8,128)S(1)}, f32[256,256]{1,0:T(8,128)}, u32[]{:S(2)}) copy-start(f32[256,256]{1,0:T(8,128)} %constant.17.clone.basis) | copy-start | bytes 786436

commit v11 on v10

--- a/solution.py
+++ b/solution.py
@@ -147,7 +147,7 @@
     plane(TILE - 1, before, None)
 
 
-PART = 4
+PART = 8
 
 
 def parts_of(x):

time: 92.7 us -> 92.7 us (level)
  no operation moved by 1% of the time
where the time goes in v11:
time: 92.7 us; the launch traced here: 92.4 us
  blocking collectives  67.7 us (73%)
  starting transfers between devices  12.1 us (13%)
  Pallas kernels  8.23 us (9%)
  local copies, waits for them, and re-layouts  2.64 us (3%)
    all_to_all x1, blocking collectives, per_device(): lax.all_to_all(spectrum, ('py', 'px'), split_axis=0, concat_axis=0, tiled...  21.7 us
    all_to_all x1, blocking collectives, per_device(): lax.all_to_all(solved, ('py', 'px'), split_axis=0, concat_axis=0, tiled=T...  20.4 us
    all_to_all x1, blocking collectives, per_device(): lax.all_to_all(message, 'px', split_axis=0, concat_axis=0, tiled=True)  13.7 us
    ppermute x4, starting transfers between devices, swapped(): lax.ppermute(block, axis, [(i, p % count) for i, p in enumerate(partner)])  12.1 us
    all_to_all x1, blocking collectives, per_device(): lax.all_to_all(message.reshape(TILE, TILE, WIDE), 'px', split_axis=0, con...  11.8 us
    pallas_call x7, Pallas kernels, call(): pl.pallas_call(kernel, out_shape=out_shape, name=kernel.__name__, compile...  8.23 us
    unnamed x12, local copies, waits for them, and re-layouts  2.64 us
  transfers between devices with their start and end apart: 4, of which 1 were waited for; matrix products, arithmetic and copies ran while one was open for 0% of the time, Pallas kernels for 2%

profile of v11, /device:TPU:1, one launch (start us, length us, event | category | flops | bytes accessed | tf_op | source)
XLA Modules:
  0.0 92.4 jit_solution(13132711570339207520)
XLA Ops:
  0.6 0.0 copy-start
  0.6 1.3 %copy-done = f32[5,16,16,192]{3,2,1,0:T(8,128)S(1)} copy-done((f32[5,16,16,192]{3,2,1,0:T(8,128)S(1)}, f32[5,16,16,192]{3,2,1,0:T(8,128)}, u32[]{:S(2)}) %copy-start) | copy-done | bytes 983064
  2.0 0.1 edges_kernel.1
  2.1 4.2 %collective-permute-start = (f32[5,16,192]{2,1,0:T(8,128)S(1)}, f32[5,16,192]{2,1,0:T(8,128)S(1)}, u32[]{:S(2)}, u32[]{:S(2)}) collective-permute-start(f32[5,16,192]{2,1,0:T(8,128)S(1)} %get-tuple-element.13.rest_0_), channel_id=1, source_target_pairs={{0,240},{16,32},{32,16},{48,64},{64,48},{80,96},{96,80},{112,128},... | collective-permute-start | bytes 184328 | tf_op jit(solution)/shard_map/ppermute | solution.py:442
  6.3 2.3 %collective-permute-start.1 = (f32[5,16,192]{2,1,0:T(8,128)S(1)}, f32[5,16,192]{2,1,0:T(8,128)S(1)}, u32[]{:S(2)}, u32[]{:S(2)}) collective-permute-start(f32[5,16,192]{2,1,0:T(8,128)S(1)} %get-tuple-element.14.rest_1_), channel_id=1, source_target_pairs={{0,16},{16,0},{32,48},{48,32},{64,80},{80,64},{96,112},{112,96},{1... | collective-permute-start | bytes 184328 | tf_op jit(solution)/shard_map/ppermute | solution.py:442
  8.6 5.6 %collective-permute-start.2 = (f32[5,16,192]{2,1,0:T(8,128)S(1)}, f32[5,16,192]{2,1,0:T(8,128)S(1)}, u32[]{:S(2)}, u32[]{:S(2)}) collective-permute-start(f32[5,16,192]{2,1,0:T(8,128)S(1)} %get-tuple-element.15.rest_2_), channel_id=1, source_target_pairs={{0,15},{1,2},{2,1},{3,4},{4,3},{5,6},{6,5},{7,8},{8,7},{9,10},{10,... | collective-permute-start | bytes 184328 | tf_op jit(solution)/shard_map/ppermute | solution.py:442
  14.2 0.0 collective-permute-start.3
  14.3 0.1 subtract_add_fusion.shift
  14.4 0.0 copy-start.3
  14.4 1.3 %copy-done.3 = f32[5,16,16,192]{3,2,1,0:T(8,128)S(1)} copy-done((f32[5,16,16,192]{3,2,1,0:T(8,128)S(1)}, f32[5,16,16,192]{3,2,1,0:T(8,128)}, u32[]{:S(2)}) %copy-start.3) | copy-done | bytes 983064
  15.7 2.0 %interior_kernel.1 = (f32[5,16,16,192]{3,2,1,0:T(8,128)S(1)}, f32[16,16,192]{2,1,0:T(8,128)S(1)}, f32[16,16,256]{2,1,0:T(8,128)S(1)}, f32[1,256]{1,0:T(1,128)S(1)}) custom-call(f32[5,16,16,192]{3,2,1,0:T(8,128)S(1)} %copy-done.1, f32[5,16,16,192]{3,2,1,0:T(8,128)S(1)} %copy-done.3, s32[1,192]{1,0:T(1,128)S(1)} %bitcast.5, s32[16,16]{1,0:T(8,128)S(1)} %copy-done.5, ...), custom_call_target="tpu_custom_call" | custom-call | flops 10000000 | bytes 1968896 | tf_op jit(solution)/shard_map/interior_kernel/pallas_call | solution.py:429
  17.7 0.0 collective-permute-done.rest_4_
  17.7 0.0 collective-permute-done.1.rest_5_
  17.7 0.0 collective-permute-done.2.rest_6_
  17.7 0.8 collective-permute-done.3.rest_7_
  18.5 0.5 momentum_kernel.1
  19.0 13.7 %all_to_all.20 = f32[16,16,256]{2,1,0:T(8,128)S(1)} all-to-all(f32[16,16,256]{2,1,0:T(8,128)S(1)} %momentum_kernel.1), channel_id=1, replica_groups=mesh['px'=16,'py'=16] {'px'}, dimensions={0} | all-to-all | bytes 524288 | tf_op jit(solution)/shard_map/all_to_all | solution.py:482
  32.8 0.8 forward_kernel.1
  33.6 21.7 %all_to_all.21.lines = f32[256,1,256]{2,1,0:T(1,128)S(1)} all-to-all(f32[256,1,256]{2,1,0:T(1,128)S(1)} %forward_kernel.1), channel_id=1, replica_groups=mesh['px'=16,'py'=16] {'py','px'}, dimensions={0} | all-to-all | bytes 524288 | tf_op jit(solution)/shard_map/all_to_all | solution.py:486
  55.3 2.0 %solve_kernel.1 = f32[256,1,256]{2,1,0:T(1,128)S(1)} custom-call(f32[256,1,256]{2,1,0:T(1,128)S(1)} %all_to_all.21.lines, f32[256,256]{1,0:T(8,128)S(1)} %copy-done.2, s32[1,192]{1,0:T(1,128)S(1)} %bitcast.7, f32[1,256]{1,0:T(1,128)S(1)} %get-tuple-element.17.shift), custom_call_target="tpu_custom_call" | custom-call | bytes 526080 | tf_op jit(solution)/shard_map/solve_kernel/pallas_call | solution.py:429
  57.3 20.4 %all_to_all.22.lines = f32[256,1,256]{2,1,0:T(1,128)S(1)} all-to-all(f32[256,1,256]{2,1,0:T(1,128)S(1)} %solve_kernel.1), channel_id=1, replica_groups=mesh['px'=16,'py'=16] {'py','px'}, dimensions={0} | all-to-all | bytes 524288 | tf_op jit(solution)/shard_map/all_to_all | solution.py:492
  77.8 0.8 backward_kernel.1
  78.6 11.8 %all_to_all.23.message = f32[16,16,256]{2,1,0:T(8,128)S(1)} all-to-all(f32[16,16,256]{2,1,0:T(8,128)S(1)} %bitcast.3), channel_id=1, replica_groups=mesh['px'=16,'py'=16] {'px'}, dimensions={0} | all-to-all | bytes 524288 | tf_op jit(solution)/shard_map/all_to_all | solution.py:496
  90.4 2.0 %correct_kernel.1 = (f32[5,16,16,192]{3,2,1,0:T(8,128)}, f32[16,16,192]{2,1,0:T(8,128)}) custom-call(f32[16,16,256]{2,1,0:T(8,128)S(1)} %all_to_all.23.message, f32[5,16,16,192]{3,2,1,0:T(8,128)S(1)} %get-tuple-element.10.inner, f32[16,16,192]{2,1,0:T(8,128)S(1)} %get-tuple-element.11.fluid, f32[5,16,192]{2,1,0:T(8,128)S(1)} %get-tuple-element.13.rest_0_, ...), custom_call_target="tpu_custom_call" | custom-call | bytes 1934080 | tf_op jit(solution)/shard_map/correct_kernel/pallas_call | solution.py:429
  (8 shorter events, 0.0 us)
Async XLA Ops:
  0.6 1.3 %copy-start = (f32[5,16,16,192]{3,2,1,0:T(8,128)S(1)}, f32[5,16,16,192]{3,2,1,0:T(8,128)}, u32[]{:S(2)}) copy-start(f32[5,16,16,192]{3,2,1,0:T(8,128)} %state.3) | copy-start | bytes 2949124
  1.9 12.4 %copy-start.1 = (f32[5,16,16,192]{3,2,1,0:T(8,128)S(1)}, f32[5,16,16,192]{3,2,1,0:T(8,128)}, u32[]{:S(2)}) copy-start(f32[5,16,16,192]{3,2,1,0:T(8,128)} %state.3) | copy-start | bytes 2949124
  1.9 12.4 %copy-start.4 = (s32[192]{0:T(256)S(1)}, s32[192]{0:T(256)}, u32[]{:S(2)}) copy-start(s32[192]{0:T(256)} %param.7) | copy-start | bytes 2308
  2.0 12.4 %copy-start.5 = (s32[16,16]{1,0:T(8,128)S(1)}, s32[16,16]{1,0:T(8,128)}, u32[]{:S(2)}) copy-start(s32[16,16]{1,0:T(8,128)} %height.1) | copy-start | bytes 3076
  2.1 15.6 %collective-permute-start = (f32[5,16,192]{2,1,0:T(8,128)S(1)}, f32[5,16,192]{2,1,0:T(8,128)S(1)}, u32[]{:S(2)}, u32[]{:S(2)}) collective-permute-start(f32[5,16,192]{2,1,0:T(8,128)S(1)} %get-tuple-element.13.rest_0_), channel_id=1, source_target_pairs={{0,240},{16,32},{32,16},{48,64},{64,48},{80,96},{96,80},{112,128},... | collective-permute-start | bytes 184328 | tf_op jit(solution)/shard_map/ppermute | solution.py:442
  6.3 11.4 %collective-permute-start.1 = (f32[5,16,192]{2,1,0:T(8,128)S(1)}, f32[5,16,192]{2,1,0:T(8,128)S(1)}, u32[]{:S(2)}, u32[]{:S(2)}) collective-permute-start(f32[5,16,192]{2,1,0:T(8,128)S(1)} %get-tuple-element.14.rest_1_), channel_id=1, source_target_pairs={{0,16},{16,0},{32,48},{48,32},{64,80},{80,64},{96,112},{112,96},{1... | collective-permute-start | bytes 184328 | tf_op jit(solution)/shard_map/ppermute | solution.py:442
  8.6 9.1 %collective-permute-start.2 = (f32[5,16,192]{2,1,0:T(8,128)S(1)}, f32[5,16,192]{2,1,0:T(8,128)S(1)}, u32[]{:S(2)}, u32[]{:S(2)}) collective-permute-start(f32[5,16,192]{2,1,0:T(8,128)S(1)} %get-tuple-element.15.rest_2_), channel_id=1, source_target_pairs={{0,15},{1,2},{2,1},{3,4},{4,3},{5,6},{6,5},{7,8},{8,7},{9,10},{10,... | collective-permute-start | bytes 184328 | tf_op jit(solution)/shard_map/ppermute | solution.py:442
  14.2 4.3 %collective-permute-start.3 = (f32[5,16,192]{2,1,0:T(8,128)S(1)}, f32[5,16,192]{2,1,0:T(8,128)S(1)}, u32[]{:S(2)}, u32[]{:S(2)}) collective-permute-start(f32[5,16,192]{2,1,0:T(8,128)S(1)} %get-tuple-element.16.rest_3_), channel_id=1, source_target_pairs={{0,1},{1,0},{2,3},{3,2},{4,5},{5,4},{6,7},{7,6},{8,9},{9,8},{10,11... | collective-permute-start | bytes 184328 | tf_op jit(solution)/shard_map/ppermute | solution.py:442
  14.4 1.3 %copy-start.3 = (f32[5,16,16,192]{3,2,1,0:T(8,128)S(1)}, f32[5,16,16,192]{3,2,1,0:T(8,128)}, u32[]{:S(2)}) copy-start(f32[5,16,16,192]{3,2,1,0:T(8,128)} %memory.1) | copy-start | bytes 2949124
  18.5 14.2 %copy-start.2 = (f32[256,256]{1,0:T(8,128)S(1)}, f32[256,256]{1,0:T(8,128)}, u32[]{:S(2)}) copy-start(f32[256,256]{1,0:T(8,128)} %constant.17.clone.basis) | copy-start | bytes 786436
